TPU v7x, 32 devices: a whole 2x2x4 slice. The times are simulated.
32 devices in a mesh: seq: 8 (over z, y), row: 2 (over x), col: 2 (over core).
Axes of the slice: x: 2, y: 2, z: 4, core: 2. Of those that a mesh axis runs over, the one named last changes fastest.
Arguments:
- hidden_in: bfloat16 [4096, 1600], P('seq', ('col', 'row')), may hold values from -6 to 6
- grad_out: bfloat16 [4096, 1600], P('seq', ('col', 'row')), may hold values from -6 to 6
- segment_ids: int32 [4096], replicated, may hold values from 0 to 6, as said below
- pre_gain: float32 [1600], P(('col', 'row')), may hold values from 0.5 to 1.5
- qkv_weight: bfloat16 [1600, 2240], P('col', 'row'), may hold values from -0.15625 to 0.15625
- mixer_in_weight: bfloat16 [1600, 6400], P('col', 'row'), may hold values from -0.15625 to 0.15625
- meta_cache: bfloat16 [2, 128, 320], replicated, may hold values from -6 to 6
- conv_weight: float32 [4, 3200], replicated, may hold values from -3 to 3
- conv_bias: float32 [3200], replicated, may hold values from -3 to 3
- select_weight: float32 [3200, 132], replicated, may hold values from -0.109375 to 0.109375
- step_weight: float32 [100, 3200], replicated, may hold values from -0.625 to 0.625
- step_bias: float32 [3200], replicated, may hold values from -7 to -2
- log_rates: float32 [3200, 16], replicated, may hold values from -4 to 1
- skip_gain: float32 [3200], replicated, may hold values from 0.5 to 1.5
- attn_gain: float32 [1600], replicated, may hold values from 0.5 to 1.5
- mixer_gain: float32 [3200], replicated, may hold values from 0.5 to 1.5
- attn_out_weight: bfloat16 [1600, 1600], P('row', 'col'), may hold values from -0.15625 to 0.15625
- mixer_out_weight: bfloat16 [3200, 1600], P('row', 'col'), may hold values from -0.109375 to 0.109375
- post_gain: float32 [1600], P(('col', 'row')), may hold values from 0.5 to 1.5
- gate_weight: bfloat16 [1600, 5504], P('col', 'row'), may hold values from -0.15625 to 0.15625
- up_weight: bfloat16 [1600, 5504], P('col', 'row'), may hold values from -0.15625 to 0.15625
- down_weight: bfloat16 [5504, 1600], P('row', 'col'), may hold values from -0.078125 to 0.078125
Outputs:
- hidden_out: bfloat16 [4096, 1600], P('seq', ('col', 'row'))
- grad_in: float32 [4096, 1600], P('seq', ('col', 'row'))
- grad_pre_gain: float32 [1600], replicated
- grad_qkv: float32 [1600, 2240], P('col', ('row', 'seq'))
- grad_mixer_in: float32 [1600, 6400], P('col', ('row', 'seq'))
- grad_meta: float32 [2, 128, 320], replicated
- grad_conv_weight: float32 [4, 3200], replicated
- grad_conv_bias: float32 [3200], replicated
- grad_select: float32 [3200, 132], replicated
- grad_step_weight: float32 [100, 3200], replicated
- grad_step_bias: float32 [3200], replicated
- grad_log_rates: float32 [3200, 16], replicated
- grad_skip: float32 [3200], replicated
- grad_attn_gain: float32 [1600], replicated
- grad_mixer_gain: float32 [3200], replicated
- grad_attn_out: float32 [1600, 1600], P('row', ('col', 'seq'))
- grad_mixer_out: float32 [3200, 1600], P('row', ('col', 'seq'))
- grad_post_gain: float32 [1600], replicated
- grad_gate: float32 [1600, 5504], P('col', ('row', 'seq'))
- grad_up: float32 [1600, 5504], P('col', ('row', 'seq'))
- grad_down: float32 [5504, 1600], P('row', ('col', 'seq'))
Inputs may be any that keep to these rules, and one draw needn't show every extreme that they name: `segment_ids`: segment numbers start at 0 and never fall along the tokens; the tokens with one number form one document, and documents run across the shards of devices. Some numbers in the range may be unused.
All inputs are finite; a program needn't handle non-finite values.
Results may differ from a plain program's by a relative error of at most 0.014.
Values may be sent and summed in bfloat16 or wider, within the bound.
No kernel may reach another device: no remote copies, remote signals or barrier semaphores. Data moves between devices by JAX's collectives and lax.ppermute only.
A program may use at most 320 MiB of HBM per device.

v0:
```python
import math

import jax
import jax.numpy as jnp
from jax import lax
from jax.sharding import PartitionSpec as P

D = 1600
H = 25
KVH = 5
HD = 64
DI = 3200
STATE = 16
DT_RANK = 100
CONV = 4
META = 128
WIN = 1024


EPS = 1e-05
NEG = -1e30
THETA = 10000.0
HIGH = lax.Precision.HIGHEST


def as_sent(x):

    def short(part):
        return part.astype(jnp.bfloat16) if part.dtype == jnp.float32 else part

    return jax.tree.map(short, x)


def shifted_2(block, axis, distance):
    devices = range(lax.axis_size(axis))
    route = [(i - distance, i) for i in devices if i - distance in devices]
    return lax.ppermute(block, axis, route)


def entering(x, axis, combine, identity, reverse):
    count, position = (lax.axis_size(axis), lax.axis_index(axis))
    everything = jax.tree.map(lambda part: lax.all_gather(part, axis), x)
    start = jax.tree.map(
        lambda part, zero: jnp.broadcast_to(jnp.asarray(zero, part.dtype), part.shape), x, identity
    )

    def turn(k, before):
        at = count - 1 - k if reverse else k
        reached = at > position if reverse else at < position
        new = combine(before, jax.tree.map(lambda part: part[at], everything))
        return jax.tree.map(lambda a, b: jnp.where(reached, a, b), new, before)

    return lax.fori_loop(0, count, turn, start)


def dot_plain(left_op, right_op):
    return jnp.dot(left_op, right_op, preferred_element_type=jnp.float32)


def dot_left(left_op, right_op):
    return lax.dot_general(
        left_op, right_op, (((0,), (0,)), ((), ())), preferred_element_type=jnp.float32
    )


def dot_right(left_op, right_op):
    return lax.dot_general(
        left_op, right_op, (((1,), (1,)), ((), ())), preferred_element_type=jnp.float32
    )


def exact_dot(left_op, right_op):
    return jnp.dot(left_op, right_op, precision=HIGH, preferred_element_type=jnp.float32)


def exact_left(left_op, right_op):
    return lax.dot_general(
        left_op,
        right_op,
        (((0,), (0,)), ((), ())),
        precision=HIGH,
        preferred_element_type=jnp.float32,
    )


def exact_right(left_op, right_op):
    return lax.dot_general(
        left_op,
        right_op,
        (((1,), (1,)), ((), ())),
        precision=HIGH,
        preferred_element_type=jnp.float32,
    )


def gather_rows(values):
    return lax.all_gather(values, "row", axis=1, tiled=True)


def gather_cols(values):
    return jax.tree.map(
        lambda part, own: part.astype(own.dtype),
        lax.all_gather(as_sent(values), "col", axis=1, tiled=True),
        values,
    )


def scatter_rows(values):
    return lax.psum_scatter(values, "row", scatter_dimension=1, tiled=True)


def scatter_cols(values):
    return lax.psum_scatter(values, "col", scatter_dimension=1, tiled=True)


def feature_total(values):
    return lax.psum(values, ("row", "col"))


def to_core(values):
    return (
        lax.all_to_all(values[0], ("row", "col"), split_axis=0, concat_axis=1, tiled=True),
        lax.all_to_all(values[1], ("row", "col"), split_axis=0, concat_axis=1, tiled=True),
    )


def to_grid(values):
    return (
        lax.all_to_all(values[0], ("row", "col"), split_axis=1, concat_axis=0, tiled=True),
        lax.all_to_all(values[1], ("row", "col"), split_axis=1, concat_axis=0, tiled=True),
    )


def pass_forward(values, offset):
    return jax.tree.map(
        lambda part, own: part.astype(own.dtype),
        shifted_2(as_sent(values), ("seq", "row", "col"), offset),
        values,
    )


def pass_backward(values, offset):
    return shifted_2(values, ("seq", "row", "col"), -offset)


def reduce_grads(values):
    return (
        lax.psum_scatter(values[0], "seq", scatter_dimension=1, tiled=True),
        lax.psum_scatter(values[1], "seq", scatter_dimension=1, tiled=True),
        lax.psum_scatter(values[2], "seq", scatter_dimension=1, tiled=True),
        lax.psum_scatter(values[3], "seq", scatter_dimension=1, tiled=True),
        lax.psum_scatter(values[4], "seq", scatter_dimension=1, tiled=True),
        lax.psum_scatter(values[5], "seq", scatter_dimension=1, tiled=True),
        lax.psum_scatter(values[6], "seq", scatter_dimension=1, tiled=True),
    )


def grid_norm(values, gain_part):
    totals = feature_total(jnp.sum(values * values, axis=1))
    factor = lax.rsqrt(totals / D + EPS)
    return (factor, values * factor[:, None] * gain_part[None, :])


def grid_norm_back(values, factor, gain_part, incoming):
    weighted = incoming * gain_part[None, :]
    inner_sum = feature_total(jnp.sum(weighted * values, axis=1)) / D
    result = factor[:, None] * weighted - values * (factor**3 * inner_sum)[:, None]
    return (result, jnp.sum(incoming * values * factor[:, None], axis=0))


def local_norm(values, gain_vec):
    factor = lax.rsqrt(jnp.mean(values * values, axis=1) + EPS)
    return (factor, values * factor[:, None] * gain_vec[None, :])


def local_norm_back(values, factor, gain_vec, incoming):
    weighted = incoming * gain_vec[None, :]
    inner_sum = jnp.mean(weighted * values, axis=1)
    result = factor[:, None] * weighted - values * (factor**3 * inner_sum)[:, None]
    return (result, jnp.sum(incoming * values * factor[:, None], axis=0))


def doc_positions(seg_all):
    total = seg_all.shape[0]
    index_all = jnp.arange(total, dtype=jnp.int32)
    starts = jnp.concatenate([jnp.ones((1,), jnp.bool_), seg_all[1:] != seg_all[:-1]])
    start_at = lax.cummax(jnp.where(starts, index_all, jnp.zeros_like(index_all)), axis=0)
    return index_all - start_at


def rope_tables(positions):
    half_width = HD // 2
    frequency = THETA ** (-2.0 * jnp.arange(half_width, dtype=jnp.float32) / HD)
    angles = positions.astype(jnp.float32)[:, None] * frequency[None, :]
    cosine = jnp.concatenate([jnp.cos(angles), jnp.cos(angles)], axis=1)
    sine_tab = jnp.concatenate([jnp.sin(angles), jnp.sin(angles)], axis=1)
    return (cosine, sine_tab)


def rotate_half(values):
    half_width = values.shape[-1] // 2
    return jnp.concatenate([-values[..., half_width:], values[..., :half_width]], axis=-1)


def apply_rope(values, cosine, sine_tab):
    return values * cosine[:, None, :] + rotate_half(values) * sine_tab[:, None, :]


def rope_back(incoming, cosine, sine_tab):
    return incoming * cosine[:, None, :] - rotate_half(incoming * sine_tab[:, None, :])


def pair_combine(earlier, latter):
    return (earlier[0] * latter[0], earlier[1] * latter[0] + latter[1])


def linear_run(decay_blk, inject, initial):
    run_prod, run_total = lax.associative_scan(pair_combine, (decay_blk, inject), axis=0)
    return run_total + run_prod * initial[None]


def adjoint_run(incoming, decay_blk, pulls):
    shifted = jnp.concatenate([decay_blk[1:], jnp.ones_like(decay_blk[:1])], axis=0)
    return linear_run(shifted[::-1], pulls[::-1], incoming)[::-1]


def block_terms(slab_in, decay_rates):
    step_blk, input_blk, inject_gate, keep_blk = slab_in
    decay_blk = jnp.exp(-step_blk[:, :, None] * decay_rates[None]) * keep_blk[:, None, None]
    inject = (step_blk * input_blk)[:, :, None] * inject_gate[:, None, :]
    return (decay_blk, inject)


def shards(
    hidden_in,
    grad_out,
    segment_ids,
    pre_gain,
    qkv_weight,
    mixer_in_weight,
    meta_cache,
    conv_weight,
    conv_bias,
    select_weight,
    step_weight,
    step_bias,
    log_rates,
    skip_gain,
    attn_gain,
    mixer_gain,
    attn_out_weight,
    mixer_out_weight,
    post_gain,
    gate_weight,
    up_weight,
    down_weight,
):
    resid_in = hidden_in.astype(jnp.float32)
    pre_factor, pre_normed = grid_norm(resid_in, pre_gain)
    first_rows = gather_rows(pre_normed.astype(jnp.bfloat16))
    qkv_grid, inner_grid = scatter_cols(
        (dot_plain(first_rows, qkv_weight), dot_plain(first_rows, mixer_in_weight))
    )
    qkv_core, inner_core = to_core((qkv_grid.astype(jnp.bfloat16), inner_grid.astype(jnp.bfloat16)))
    tok_core = qkv_core.shape[0]
    devices_back = (WIN + tok_core - 2) // tok_core
    halo_rows = devices_back * tok_core
    tail_rows = CONV - 1
    repeats = H // KVH
    kv_width = KVH * HD
    score_scale = HD ** (-0.5)
    start_row = lax.axis_index(("seq", "row", "col")) * tok_core
    seg_padded = jnp.concatenate([jnp.full((halo_rows,), -1, jnp.int32), segment_ids])
    key_segs = lax.dynamic_slice(seg_padded, (start_row,), (halo_rows + tok_core,))
    query_segs = key_segs[halo_rows:]
    query_glob = start_row + jnp.arange(tok_core, dtype=jnp.int32)
    key_glob = start_row - halo_rows + jnp.arange(halo_rows + tok_core, dtype=jnp.int32)
    own_positions = lax.dynamic_slice(doc_positions(segment_ids), (start_row,), (tok_core,))
    cosine, sine_tab = rope_tables(own_positions)
    query_rot = apply_rope(
        qkv_core[:, :D].astype(jnp.float32).reshape(tok_core, H, HD), cosine, sine_tab
    ).astype(jnp.bfloat16)
    key_rot = (
        apply_rope(
            qkv_core[:, D : D + kv_width].astype(jnp.float32).reshape(tok_core, KVH, HD),
            cosine,
            sine_tab,
        )
        .astype(jnp.bfloat16)
        .reshape(tok_core, kv_width)
    )
    value_own = qkv_core[:, D + kv_width :]
    inner_own = inner_core[:, :DI]
    gate_z = inner_core[:, DI:].astype(jnp.float32)
    halo_keys = []
    halo_values = []
    conv_tail = None
    for offset in range(1, devices_back + 1):
        if offset == 1:
            got_key, got_value, conv_tail = pass_forward(
                (key_rot, value_own, inner_own[tok_core - tail_rows :]), offset
            )
        else:
            got_key, got_value = pass_forward((key_rot, value_own), offset)
        halo_keys.insert(0, got_key)
        halo_values.insert(0, got_value)
    keys_all = jnp.concatenate([meta_cache[0]] + halo_keys + [key_rot], axis=0)
    values_all = jnp.concatenate([meta_cache[1]] + halo_values + [value_own], axis=0)
    key_count = keys_all.shape[0]
    distance = query_glob[:, None] - key_glob[None, :]
    visible = (key_segs[None, :] == query_segs[:, None]) & (distance >= 0) & (distance < WIN)
    visible = jnp.concatenate([jnp.ones((tok_core, META), jnp.bool_), visible], axis=1)
    query_groups = query_rot.reshape(tok_core, KVH, repeats, HD).transpose(1, 2, 0, 3)
    key_groups = keys_all.reshape(key_count, KVH, HD).transpose(1, 0, 2)
    value_groups = values_all.reshape(key_count, KVH, HD).transpose(1, 0, 2)

    def group_scores(query_grp, key_grp):
        raw_scores = (
            jnp.einsum("rqd,kd->rqk", query_grp, key_grp, preferred_element_type=jnp.float32)
            * score_scale
        )
        return jnp.where(visible[None], raw_scores, NEG)

    def group_forward(operands):
        query_grp, key_grp, value_grp = operands
        scores = group_scores(query_grp, key_grp)
        highest = jnp.max(scores, axis=-1, keepdims=True)
        exponent = jnp.exp(scores - highest)
        totals = jnp.sum(exponent, axis=-1, keepdims=True)
        softmax_out = exponent / totals
        output = jnp.einsum(
            "rqk,kd->rqd",
            softmax_out.astype(jnp.bfloat16),
            value_grp,
            preferred_element_type=jnp.float32,
        )
        return (output, (highest + jnp.log(totals))[..., 0])

    attn_groups, log_totals = lax.map(group_forward, (query_groups, key_groups, value_groups))
    attn_flat = attn_groups.transpose(2, 0, 1, 3).reshape(tok_core, D)
    attn_factor, attn_normed = local_norm(attn_flat, attn_gain)
    attn_low = attn_normed.astype(jnp.bfloat16)
    conv_input = jnp.concatenate([conv_tail, inner_own], axis=0).astype(jnp.float32)
    conv_segs = key_segs[halo_rows - tail_rows :]
    tap_masks = [
        (conv_segs[tap_index : tap_index + tok_core] == query_segs).astype(jnp.float32)[:, None]
        for tap_index in range(CONV)
    ]
    conv_sum = conv_bias[None, :]
    for tap_index in range(CONV):
        conv_sum = (
            conv_sum
            + conv_weight[tap_index][None, :]
            * conv_input[tap_index : tap_index + tok_core]
            * tap_masks[tap_index]
        )
    mixed_in = jax.nn.silu(conv_sum)
    selected = exact_dot(mixed_in, select_weight)
    step_low = selected[:, :DT_RANK]
    in_gate = selected[:, DT_RANK : DT_RANK + STATE]
    out_gate = selected[:, DT_RANK + STATE :]
    step_pre = exact_dot(step_low, step_weight) + step_bias[None, :]
    step_sizes = jax.nn.softplus(step_pre)
    keep_flag = (key_segs[halo_rows - 1 : halo_rows - 1 + tok_core] == query_segs).astype(
        jnp.float32
    )
    decay_rates = jnp.exp(log_rates)
    block_len = math.gcd(tok_core, 16)
    block_count = tok_core // block_len

    def blocked(array):
        return array.reshape((block_count, block_len) + array.shape[1:])

    slabs = (blocked(step_sizes), blocked(mixed_in), blocked(in_gate), blocked(keep_flag))
    zero_state = jnp.zeros((DI, STATE), jnp.float32)
    one_state = jnp.ones((DI, STATE), jnp.float32)

    def local_pass(carried, slab_in):
        decay_blk, inject = block_terms(slab_in, decay_rates)
        run_prod, run_total = lax.associative_scan(pair_combine, (decay_blk, inject), axis=0)
        return (pair_combine(carried, (run_prod[-1], run_total[-1])), None)

    (decay_total, state_local), _ = lax.scan(local_pass, (one_state, zero_state), slabs)
    _, state_in = entering(
        (decay_total, state_local),
        ("seq", "row", "col"),
        pair_combine,
        (one_state, zero_state),
        False,
    )

    def output_pass(state_now, slab_in):
        decay_blk, inject = block_terms(slab_in[:4], decay_rates)
        states = linear_run(decay_blk, inject, state_now)
        return (states[-1], (jnp.sum(states * slab_in[4][:, None, :], axis=2), state_now))

    _, (scan_out, block_starts) = lax.scan(output_pass, state_in, slabs + (blocked(out_gate),))
    mixed_out = scan_out.reshape(tok_core, DI) + skip_gain[None, :] * mixed_in
    z_silu = jax.nn.silu(gate_z)
    mixer_value = mixed_out * z_silu
    mixer_factor, mixer_normed = local_norm(mixer_value, mixer_gain)
    mixer_low = mixer_normed.astype(jnp.bfloat16)
    attn_grid, mixer_grid = to_grid((attn_low, mixer_low))
    attn_rows, mixer_rows = gather_cols((attn_grid, mixer_grid))
    mix_total = scatter_rows(
        0.5 * (dot_plain(attn_rows, attn_out_weight) + dot_plain(mixer_rows, mixer_out_weight))
    )
    resid_mid = resid_in + mix_total
    post_factor, post_normed = grid_norm(resid_mid, post_gain)
    second_rows = gather_rows(post_normed.astype(jnp.bfloat16))
    gate_grid, up_grid = scatter_cols(
        (dot_plain(second_rows, gate_weight), dot_plain(second_rows, up_weight))
    )
    act_low = (jax.nn.silu(gate_grid) * up_grid).astype(jnp.bfloat16)
    act_rows = gather_cols(act_low)
    ffn_out = scatter_rows(dot_plain(act_rows, down_weight))
    hidden_out = (resid_mid + ffn_out).astype(jnp.bfloat16)
    grad_top = grad_out.astype(jnp.float32)
    grad_rows = gather_rows(grad_out)
    dact = scatter_cols(dot_right(grad_rows, down_weight))
    grad_down = dot_left(act_rows, grad_rows)
    sig_gate = jax.nn.sigmoid(gate_grid)
    dgate_low = (dact * up_grid * sig_gate * (1.0 + gate_grid * (1.0 - sig_gate))).astype(
        jnp.bfloat16
    )
    dup_low = (dact * gate_grid * sig_gate).astype(jnp.bfloat16)
    dgate_rows, dup_rows = gather_cols((dgate_low, dup_low))
    grad_gate = dot_left(second_rows, dgate_rows)
    grad_up = dot_left(second_rows, dup_rows)
    dsecond = scatter_rows(dot_right(dgate_rows, gate_weight) + dot_right(dup_rows, up_weight))
    dmid_norm, post_gain_part = grid_norm_back(resid_mid, post_factor, post_gain, dsecond)
    dmid = grad_top + dmid_norm
    dmid_rows = gather_rows(dmid.astype(jnp.bfloat16))
    grad_attn_out = 0.5 * dot_left(attn_rows, dmid_rows)
    grad_mixer_out = 0.5 * dot_left(mixer_rows, dmid_rows)
    dattn_grid, dmixer_grid = scatter_cols(
        (0.5 * dot_right(dmid_rows, attn_out_weight), 0.5 * dot_right(dmid_rows, mixer_out_weight))
    )
    dattn_core, dmixer_core = to_core(
        (dattn_grid.astype(jnp.bfloat16), dmixer_grid.astype(jnp.bfloat16))
    )
    dattn_flat, attn_gain_part = local_norm_back(
        attn_flat, attn_factor, attn_gain, dattn_core.astype(jnp.float32)
    )
    dattn_groups = (
        dattn_flat.astype(jnp.bfloat16).reshape(tok_core, KVH, repeats, HD).transpose(1, 2, 0, 3)
    )

    def group_backward(operands):
        query_grp, key_grp, value_grp, dout_grp, lse_grp = operands
        scores = group_scores(query_grp, key_grp)
        softmax_out = jnp.exp(scores - lse_grp[..., None])
        dprobs = jnp.einsum("rqd,kd->rqk", dout_grp, value_grp, preferred_element_type=jnp.float32)
        delta_row = jnp.sum(softmax_out * dprobs, axis=-1, keepdims=True)
        dscores = (softmax_out * (dprobs - delta_row)).astype(jnp.bfloat16)
        dquery = (
            jnp.einsum("rqk,kd->rqd", dscores, key_grp, preferred_element_type=jnp.float32)
            * score_scale
        )
        dkey = (
            jnp.einsum("rqk,rqd->kd", dscores, query_grp, preferred_element_type=jnp.float32)
            * score_scale
        )
        dvalue = jnp.einsum(
            "rqk,rqd->kd",
            softmax_out.astype(jnp.bfloat16),
            dout_grp,
            preferred_element_type=jnp.float32,
        )
        return (dquery, dkey, dvalue)

    dquery_groups, dkey_groups, dvalue_groups = lax.map(
        group_backward, (query_groups, key_groups, value_groups, dattn_groups, log_totals)
    )
    dquery_flat = dquery_groups.transpose(2, 0, 1, 3).reshape(tok_core, H, HD)
    dkey_all = dkey_groups.transpose(1, 0, 2).reshape(key_count, kv_width)
    dvalue_all = dvalue_groups.transpose(1, 0, 2).reshape(key_count, kv_width)
    dmixer_value, mixer_gain_part = local_norm_back(
        mixer_value, mixer_factor, mixer_gain, dmixer_core.astype(jnp.float32)
    )
    sig_z = jax.nn.sigmoid(gate_z)
    dmixed_out = dmixer_value * z_silu
    dgate_z = dmixer_value * mixed_out * sig_z * (1.0 + gate_z * (1.0 - sig_z))
    skip_part = jnp.sum(dmixed_out * mixed_in, axis=0)
    dmixed_in = dmixed_out * skip_gain[None, :]
    back_slabs = slabs + (blocked(out_gate), blocked(dmixed_out))

    def first_adjoint(incoming, slab_in):
        decay_blk, _ = block_terms(slab_in[:4], decay_rates)
        pulls = slab_in[5][:, :, None] * slab_in[4][:, None, :]
        adjoint = adjoint_run(incoming, decay_blk, pulls)
        return (decay_blk[0] * adjoint[0], None)

    adjoint_local, _ = lax.scan(first_adjoint, zero_state, back_slabs, reverse=True)
    _, adjoint_in = entering(
        (decay_total, adjoint_local),
        ("seq", "row", "col"),
        pair_combine,
        (one_state, zero_state),
        True,
    )

    def second_adjoint(carried, slab_in):
        incoming, rate_total = carried
        step_blk, input_blk, inject_gate, keep_blk, read_gate, dout_blk, start_blk = slab_in
        decay_blk, inject = block_terms((step_blk, input_blk, inject_gate, keep_blk), decay_rates)
        states = linear_run(decay_blk, inject, start_blk)
        before = jnp.concatenate([start_blk[None], states[:-1]], axis=0)
        pulls = dout_blk[:, :, None] * read_gate[:, None, :]
        adjoint = adjoint_run(incoming, decay_blk, pulls)
        decay_pull = adjoint * before * decay_blk
        dstep_decay = -jnp.sum(decay_pull * decay_rates[None], axis=2)
        rate_total = rate_total - jnp.sum(decay_pull * step_blk[:, :, None], axis=0)
        dproduct = jnp.sum(adjoint * inject_gate[:, None, :], axis=2)
        dinject_gate = jnp.sum(adjoint * (step_blk * input_blk)[:, :, None], axis=1)
        dread_gate = jnp.sum(states * dout_blk[:, :, None], axis=1)
        return (
            (decay_blk[0] * adjoint[0], rate_total),
            (dstep_decay, dproduct, dinject_gate, dread_gate),
        )

    (_, rate_grad), (dstep_decay, dproduct, din_gate, dout_gate) = lax.scan(
        second_adjoint, (adjoint_in, zero_state), back_slabs + (block_starts,), reverse=True
    )
    dproduct = dproduct.reshape(tok_core, DI)
    dsteps = dstep_decay.reshape(tok_core, DI) + dproduct * mixed_in
    dmixed_in = dmixed_in + dproduct * step_sizes
    dstep_pre = dsteps * jax.nn.sigmoid(step_pre)
    step_bias_part = jnp.sum(dstep_pre, axis=0)
    step_weight_part = exact_left(step_low, dstep_pre)
    dselected = jnp.concatenate(
        [
            exact_right(dstep_pre, step_weight),
            din_gate.reshape(tok_core, STATE),
            dout_gate.reshape(tok_core, STATE),
        ],
        axis=1,
    )
    select_part = exact_left(mixed_in, dselected)
    dmixed_in = dmixed_in + exact_right(dselected, select_weight)
    sig_conv = jax.nn.sigmoid(conv_sum)
    dconv_sum = dmixed_in * sig_conv * (1.0 + conv_sum * (1.0 - sig_conv))
    conv_bias_part = jnp.sum(dconv_sum, axis=0)
    conv_weight_rows = []
    dconv_input = jnp.zeros((tok_core + tail_rows, DI), jnp.float32)
    for tap_index in range(CONV):
        masked_grad = dconv_sum * tap_masks[tap_index]
        conv_weight_rows.append(
            jnp.sum(masked_grad * conv_input[tap_index : tap_index + tok_core], axis=0)
        )
        dconv_input = dconv_input + jnp.pad(
            masked_grad * conv_weight[tap_index][None, :],
            ((tap_index, tail_rows - tap_index), (0, 0)),
        )
    conv_weight_part = jnp.stack(conv_weight_rows, axis=0)
    rates_part = rate_grad * decay_rates
    dconv_head = dconv_input[:tail_rows]
    dkey_own = dkey_all[META + halo_rows :]
    dvalue_own = dvalue_all[META + halo_rows :]
    dtail_back = None
    for offset in range(1, devices_back + 1):
        low_row = META + (devices_back - offset) * tok_core
        pieces = (dkey_all[low_row : low_row + tok_core], dvalue_all[low_row : low_row + tok_core])
        if offset == 1:
            got_key, got_value, dtail_back = pass_backward(pieces + (dconv_head,), offset)
        else:
            got_key, got_value = pass_backward(pieces, offset)
        dkey_own = dkey_own + got_key
        dvalue_own = dvalue_own + got_value
    dinner_own = dconv_input[tail_rows:] + jnp.pad(dtail_back, ((tok_core - tail_rows, 0), (0, 0)))
    dquery_rot = rope_back(dquery_flat, cosine, sine_tab).reshape(tok_core, D)
    dkey_rot = rope_back(dkey_own.reshape(tok_core, KVH, HD), cosine, sine_tab).reshape(
        tok_core, kv_width
    )
    dqkv_core = jnp.concatenate([dquery_rot, dkey_rot, dvalue_own], axis=1).astype(jnp.bfloat16)
    dinner_core = jnp.concatenate([dinner_own, dgate_z], axis=1).astype(jnp.bfloat16)
    meta_part = jnp.stack([dkey_all[:META], dvalue_all[:META]], axis=0)
    dqkv_grid, dinner_grid = to_grid((dqkv_core, dinner_core))
    dqkv_rows, dinner_rows = gather_cols((dqkv_grid, dinner_grid))
    grad_qkv = dot_left(first_rows, dqkv_rows)
    grad_mixer_in = dot_left(first_rows, dinner_rows)
    dfirst = scatter_rows(
        dot_right(dqkv_rows, qkv_weight) + dot_right(dinner_rows, mixer_in_weight)
    )
    dinput_norm, pre_gain_part = grid_norm_back(resid_in, pre_factor, pre_gain, dfirst)
    grad_in = dmid + dinput_norm
    all_grads = reduce_grads(
        (grad_down, grad_gate, grad_up, grad_attn_out, grad_mixer_out, grad_qkv, grad_mixer_in)
    )
    ffn_grads = all_grads[0:3]
    proj_grads = all_grads[3:5]
    in_grads = all_grads[5:7]
    gain_block = pre_gain.shape[0]
    block_pos = (lax.axis_index("col") * lax.axis_size("row") + lax.axis_index("row")) * gain_block
    pre_full = lax.dynamic_update_slice(jnp.zeros((D,), jnp.float32), pre_gain_part, (block_pos,))
    post_full = lax.dynamic_update_slice(jnp.zeros((D,), jnp.float32), post_gain_part, (block_pos,))
    summed = lax.psum(
        (
            pre_full,
            post_full,
            meta_part,
            conv_weight_part,
            conv_bias_part,
            select_part,
            step_weight_part,
            step_bias_part,
            rates_part,
            skip_part,
            attn_gain_part,
            mixer_gain_part,
        ),
        ("seq", "row", "col"),
    )
    return (
        hidden_out,
        grad_in,
        summed[0],
        in_grads[0],
        in_grads[1],
        summed[2],
        summed[3],
        summed[4],
        summed[5],
        summed[6],
        summed[7],
        summed[8],
        summed[9],
        summed[10],
        summed[11],
        proj_grads[0],
        proj_grads[1],
        summed[1],
        ffn_grads[1],
        ffn_grads[2],
        ffn_grads[0],
    )


def solution(mesh):
    in_specs = (
        P("seq", ("col", "row")),
        P("seq", ("col", "row")),
        P(),
        P(("col", "row")),
        P("col", "row"),
        P("col", "row"),
        P(),
        P(),
        P(),
        P(),
        P(),
        P(),
        P(),
        P(),
        P(),
        P(),
        P("row", "col"),
        P("row", "col"),
        P(("col", "row")),
        P("col", "row"),
        P("col", "row"),
        P("row", "col"),
    )
    out_specs = (
        P("seq", ("col", "row")),
        P("seq", ("col", "row")),
        P(),
        P("col", ("row", "seq")),
        P("col", ("row", "seq")),
        P(),
        P(),
        P(),
        P(),
        P(),
        P(),
        P(),
        P(),
        P(),
        P(),
        P("row", ("col", "seq")),
        P("row", ("col", "seq")),
        P(),
        P("col", ("row", "seq")),
        P("col", ("row", "seq")),
        P("row", ("col", "seq")),
    )
    return jax.shard_map(shards, mesh=mesh, in_specs=in_specs, out_specs=out_specs, check_vma=False)
```

profile of v0, /device:TPU:0, one launch (start us, length us, event | category | flops | bytes accessed | tf_op | source)
XLA Modules:
  0.0 6292.3 jit_solution(12582097613972941103)
XLA Ops:
  8.5 8.3 psum.112
  19.1 10.5 all_gather.53
  29.6 9.5 fusion.185
  39.2 16.4 reduce-scatter.25.cloned.1.call-done
  71.9 12.2 all-to-all-done.2
  106.1 602.1 %while.126 = (s32[]{:T(128)}, f32[3200,16]{0,1:T(8,128)}, f32[3200,16]{0,1:T(8,128)}, f32[8,16,3200]{2,1,0:T(8,128)}, f32[3200,16]{0,1:T(8,128)}, /*index=5*/f32...) while((s32[]{:T(128)}, f32[3200,16]{0,1:T(8,128)}, ...), condition=%wide.region_12.13_spmd.clone, body=%wide.region_11.12_spmd.clone.sunk | while | flops 8345603 | bytes 112438968 | solution.py:383
  720.0 8.6 all-to-all-done
  784.5 7.9 all-gather.25.cloned.1.call-done
  798.5 66.8 %all-gather.27.cloned.1.call-done = f32[102400,16]{0,1:T(8,128)} async-done(((f32[3200,16]{0,1:T(8,128)}), f32[102400,16]{0,1:T(8,128)}) %all-gather.27.cloned.1.call-update) | async-done | bytes 6553616 | tf_op jit(solution)/shard_map/all_gather | solution.py:42
  872.1 86.5 %while.127 = (s32[]{:T(128)}, f32[3200,16]{0,1:T(8,128)S(1)}, s32[]{:T(128)}, f32[32,3200,16]{1,2,0:T(8,128)}, f32[32,3200,16]{1,0,2:T(8,128)}, /*index=5*/s32[]{:T(128)}, s32[]{:T(128)}) while((s32[]{:T(128)}, f32[3200,16]{0,1:T(8,128)S(1)}, s32[]{:T(128)}, f32[32,3200,16]{1,2,0:T(8,128)}, f32[32,3200,16]{1,0,2:T(8,128)}, ...), condition=%wide.region_14.15_spmd.clone, body=%wide.region_13.14_spmd.clone.sunk | while | flops 204804 | bytes 1228913 | solution.py:53
  960.0 811.5 %while.123 = (s32[]{:T(128)}, f32[3200,16]{0,1:T(8,128)S(1)}, f32[8,16,3200]{2,1,0:T(8,128)}, f32[8,3200,16]{1,2,0:T(8,128)}, f32[8,16,3200]{2,1,0:T(8,128)}, /*...) while((s32[]{:T(128)}, f32[3200,16]{0,1:T(8,128)S(1)}, ...), condition=%wide.region_17.18_spmd, body=%wide.region_15.17_spmd.sunk | while | flops 15411202 | bytes 175520464 | solution.py:397
  1793.9 24.2 while.122
  1818.6 10.0 all_to_all.131
  1837.8 19.5 all_gather.62
  1858.2 8.2 fusion.189
  1876.1 11.8 all_gather.60
  1888.8 8.2 fusion.187
  1897.3 9.0 fusion.188
  1909.3 17.4 reduce-scatter.31.cloned.1.call-done
  1933.5 12.2 all-gather.17.cloned.1.call-done
  1952.6 8.1 all-gather.19.cloned.1.call-done
  1968.2 28.1 reduce-scatter.37.cloned.1.call-done
  2005.6 11.9 all_gather.65
  2021.2 11.2 reduce-scatter.41.cloned.1.call-done
  2041.0 9.3 all-to-all-done.6
  2060.6 644.7 %while.125 = (s32[]{:T(128)}, f32[3200,16]{0,1:T(8,128)}, f32[8,16,3200]{2,1,0:T(8,128)}, f32[3200,16]{0,1:T(8,128)}, f32[8,16]{1,0:T(8,128)S(1)}, /*index=5*/f3...) while((s32[]{:T(128)}, f32[3200,16]{0,1:T(8,128)}, ...), condition=%wide.region_37.38_spmd, body=%wide.region_36.37_spmd.sunk | while | flops 8140803 | bytes 123088408 | solution.py:494
  2711.0 8.9 all-to-all-done.4
  2723.5 53.9 all-gather.29.cloned.1.call-done
  2784.3 106.8 %while.128 = (s32[]{:T(128)}, f32[3200,16]{0,1:T(8,128)}, s32[]{:T(128)}, f32[32,3200,16]{1,2,0:T(8,128)}, f32[32,3200,16]{1,0,2:T(8,128)}, /*index=5*/s32[]{:T(128)}, s32[]{:T(128)}, s32[]{:T(128)}, s32[]{:T(128)}) while((s32[]{:T(128)}, f32[3200,16]{0,1:T(8,128)}, s32[]{:T(128)}, f32[32,3200,16]{1,2,0:T(8,128)}, ...), condition=%wide.region_39.40_spmd.clone, body=%wide.region_38.39_spmd.clone.sunk | while | flops 204808 | bytes 1228975 | solution.py:53
  2895.0 1805.5 %while.129 = (s32[]{:T(128)}, f32[3200,16]{0,1:T(8,128)}, f32[3200,16]{1,0:T(8,128)}, f32[8,16,3200]{2,1,0:T(8,128)}, f32[8,16,3200]{2,1,0:T(8,128)}, /*index=5*...) while((s32[]{:T(128)}, f32[3200,16]{0,1:T(8,128)}, ...), condition=%wide.region_46.47_spmd.clone, body=%wide.region_40.46_spmd.clone.sunk | while | flops 37836288 | bytes 449565280 | solution.py:522
  3097.9 7.6 pad.1253
  3323.5 7.6 pad.1253
  3549.1 7.6 pad.1253
  3774.7 7.6 pad.1253
  4727.1 52.0 while.124
  4814.5 11.8 collective-permute-done.32
  4835.7 17.0 all_to_all.132
  4860.1 8.1 all-gather.21.cloned.1.call-done
  4873.6 8.3 fusion.193
  4915.4 8.6 fusion.192
  4925.1 7.9 fusion.195
  4942.0 541.5 %fusion.160 = (f32[800,144]{0,1:T(8,128)}, f32[800,112]{0,1:T(8,128)}, f32[1600,112]{0,1:T(8,128)}, f32[2752,104]{0,1:T(8,128)}) fusion(f32[800,1120]{0,1:T(8,128)} %fusion.191, f32[800,800]{0,1:T(8,128)S(1)} %convolution_multiply_fusion.5, f32[1600,800]{0,1:T(8,128)} %convolution_multiply_fusion.3, f32[2752,800]{0,1:T(8,128)} %fusion.195), kind=kCustom, calls=%all-reduce-scatter.4 | all-reduce-scatter fusion | flops 5361667 | bytes 22751744
  5485.3 9.0 collective-permute-start.35
  5543.3 220.6 %all-reduce.113.cloned.1.call-done = (f32[800,2752]{1,0:T(8,128)}, f32[800,2752]{1,0:T(8,128)}) async-done(((f32[800,2752]{1,0:T(8,128)}, f32[800,2752]{1,0:T(8,128)}), (f32[800,2752]{1,0:T(8,128)}, f32[800,2752]{1,0:T(8,128)})) %all-reduce.113.cloned.1.call-update) | async-done | bytes 17612816
  5776.9 15.3 reduce-scatter.33.cloned.1.call-done
  5794.8 145.4 %all-reduce.111.cloned.1.call-done = (f32[2,128,320]{1,2,0:T(8,128)}, f32[3200,132]{0,1:T(8,128)}, f32[100,3200]{1,0:T(8,128)}, f32[3200,16]{0,1:T(8,128)}) async-done(((f32[2,128,320]{1,2,0:T(8,128)}, f32[3200,132]{0,1:T(8,128)}, f32[100,3200]{1,0:T(8,128)}, f32[3200,16]{0,1:T(8,128)}), (f32[2,128,320]{1,2,0:T(8,128)}, f32[3200,132]{0,1:T(8,128)}, f32[100,3200]{1,0:T(8,128)}, ...) | async-done | bytes 3502096 | tf_op jit(solution)/shard_map/psum | solution.py:597
  5940.2 131.8 %all-reduce.109.cloned.1.call-done = (f32[1600]{0:T(1024)}, f32[4,3200]{1,0:T(4,128)}, f32[3200]{0:T(1024)}, f32[3200]{0:T(1024)}, f32[3200]{0:T(1024)}, /*index...) async-done(((f32[1600]{0:T(1024)}, f32[4,3200]{1,0:T(4,128)}, f32[3200]{0:T(1024)}, f32[3200]{0:T(1024)}, f32[3200]{0:T(1024)}, /*index=5*/f32[1600]{0:T(1024)}, f32[3200]{0:T(1024)}, ...) | async-done | bytes 121616 | tf_op jit(solution)/shard_map/psum | solution.py:597
  6072.0 199.7 %reduce-scatter.45.cloned.1.call-done = f32[800,400]{0,1:T(8,128)} async-done(((f32[800,3200]{0,1:T(8,128)}), f32[800,400]{0,1:T(8,128)}) %reduce-scatter.45.cloned.1.call-update) | async-done | bytes 1280016 | tf_op jit(solution)/shard_map/reduce_scatter | solution.py:154
  (3498 shorter events, 4542.3 us)
Async XLA Ops:
  7.2 48.4 reduce-scatter.25.cloned.1.call-start
  58.9 25.2 all-to-all-start.2
  63.2 648.4 %reduce-scatter.23.cloned.1.call-start = ((), (), s32[]{:S(2)}) async-start(), calls=%async_computation.20 | async-start | bytes 3440640 | tf_op jit(solution)/shard_map/reduce_scatter | solution.py:113
  67.7 724.7 %all-gather.25.cloned.1.call-start = ((), (), s32[]{:S(2)}) async-start(), calls=%async_computation.38 | async-start | bytes 6758400 | tf_op jit(solution)/shard_map/all_gather | solution.py:42
  708.2 157.1 %all-gather.27.cloned.1.call-start = ((), (), s32[]{:S(2)}) async-start(), calls=%async_computation.39 | async-start | bytes 6758400 | tf_op jit(solution)/shard_map/all_gather | solution.py:42
  729.3 16.9 collective-permute-start
  732.7 16.6 collective-permute-start.1
  735.4 18.4 collective-permute-start.2
  739.9 15.8 collective-permute-start.3
  746.1 15.8 collective-permute-start.5
  755.8 16.4 collective-permute-start.8
  757.9 16.8 collective-permute-start.9
  761.9 17.1 collective-permute-start.10
  764.4 1016.3 %collective-permute-start.11 = (bf16[128,320]{0,1:T(8,128)(2,1)}, bf16[128,320]{0,1:T(8,128)(2,1)}, u32[]{:S(2)}, u32[]{:S(2)}) collective-permute-start(bf16[128,320]{0,1:T(8,128)(2,1)} %get-tuple-element.1539), channel_id=1, source_target_pairs={{0,5},{1,6},{2,7},{3,8},{4,9},{5,10},{6,11},{7,12},{8,13},{9,14},{... | collective-permute-start | bytes 245768 | tf_op jit(solution)/shard_map/ppermute | solution.py:37
  768.2 1014.0 %collective-permute-start.12 = (bf16[128,320]{0,1:T(8,128)(2,1)}, bf16[128,320]{0,1:T(8,128)(2,1)}, u32[]{:S(2)}, u32[]{:S(2)}) collective-permute-start(bf16[128,320]{0,1:T(8,128)(2,1)} %get-tuple-element.1539), channel_id=1, source_target_pairs={{0,4},{1,5},{2,6},{3,7},{4,8},{5,9},{6,10},{7,11},{8,12},{9,13},{1... | collective-permute-start | bytes 245768 | tf_op jit(solution)/shard_map/ppermute | solution.py:37
  772.1 1011.6 %collective-permute-start.13 = (bf16[128,320]{0,1:T(8,128)(2,1)}, bf16[128,320]{0,1:T(8,128)(2,1)}, u32[]{:S(2)}, u32[]{:S(2)}) collective-permute-start(bf16[128,320]{0,1:T(8,128)(2,1)} %get-tuple-element.1539), channel_id=1, source_target_pairs={{0,3},{1,4},{2,5},{3,6},{4,7},{5,8},{6,9},{7,10},{8,11},{9,12},{10... | collective-permute-start | bytes 245768 | tf_op jit(solution)/shard_map/ppermute | solution.py:37
  774.7 1010.5 %collective-permute-start.14 = (bf16[128,320]{0,1:T(8,128)(2,1)}, bf16[128,320]{0,1:T(8,128)(2,1)}, u32[]{:S(2)}, u32[]{:S(2)}) collective-permute-start(bf16[128,320]{0,1:T(8,128)(2,1)} %get-tuple-element.1539), channel_id=1, source_target_pairs={{0,2},{1,3},{2,4},{3,5},{4,6},{5,7},{6,8},{7,9},{8,10},{9,11},{10,... | collective-permute-start | bytes 245768 | tf_op jit(solution)/shard_map/ppermute | solution.py:37
  779.0 1007.7 %collective-permute-start.15 = (bf16[128,320]{0,1:T(8,128)(2,1)}, bf16[128,320]{0,1:T(8,128)(2,1)}, u32[]{:S(2)}, u32[]{:S(2)}) collective-permute-start(bf16[128,320]{0,1:T(8,128)(2,1)} %get-tuple-element.1539), channel_id=1, source_target_pairs={{0,1},{1,2},{2,3},{3,4},{4,5},{5,6},{6,7},{7,8},{8,9},{9,10},{10,1... | collective-permute-start | bytes 245768 | tf_op jit(solution)/shard_map/ppermute | solution.py:37
  1780.6 50.6 all-gather.13.cloned.1.call-start
  1793.5 75.2 %reduce-scatter.27.cloned.1.call-start = ((), (), s32[]{:S(2)}) async-start(), calls=%async_computation.23 | async-start | bytes 2457600 | tf_op jit(solution)/shard_map/reduce_scatter | solution.py:109
  1836.8 69.6 %reduce-scatter.35.cloned.1.call-start = ((), (), s32[]{:S(2)}) async-start(), calls=%async_computation.28 | async-start | bytes 8454144 | tf_op jit(solution)/shard_map/reduce_scatter | solution.py:113
  1866.5 42.9 reduce-scatter.29.cloned.1.call-start
  1897.1 29.6 reduce-scatter.31.cloned.1.call-start
  1906.3 39.4 all-gather.17.cloned.1.call-start
  1932.7 28.0 all-gather.19.cloned.1.call-start
  1933.4 62.8 reduce-scatter.37.cloned.1.call-start
  1968.1 64.3 %reduce-scatter.41.cloned.1.call-start = ((), (), s32[]{:S(2)}) async-start(), calls=%async_computation.34 | async-start | bytes 4915200 | tf_op jit(solution)/shard_map/reduce_scatter | solution.py:113
  2038.3 667.1 %reduce-scatter.39.cloned.1.call-start = ((), (), s32[]{:S(2)}) async-start(), calls=%async_computation.32 | async-start | bytes 2457600 | tf_op jit(solution)/shard_map/reduce_scatter | solution.py:113
  2040.6 736.9 %all-gather.29.cloned.1.call-start = ((), (), s32[]{:S(2)}) async-start(), calls=%async_computation.40 | async-start | bytes 6758400 | tf_op jit(solution)/shard_map/all_gather | solution.py:42
  4721.1 58.0 all-to-all-start.7
  4727.0 127.3 %all-gather.23.cloned.1.call-start = ((), (), s32[]{:S(2)}) async-start(), calls=%async_computation.35 | async-start | bytes 4915200 | tf_op jit(solution)/shard_map/all_gather | solution.py:103
  4786.3 82.0 %all-gather.21.cloned.1.call-start = ((), (), s32[]{:S(2)}) async-start(), calls=%async_computation.33 | async-start | bytes 1720320 | tf_op jit(solution)/shard_map/all_gather | solution.py:103
  4807.0 19.4 collective-permute-start.32
  4808.3 19.4 collective-permute-start.31
  4810.5 18.4 collective-permute-start.30
  4811.8 18.5 collective-permute-start.29
  4813.1 17.2 collective-permute-start.28
  4853.6 34.3 all-gather.15.cloned.1.call-start
  4854.2 58.7 reduce-scatter.43.cloned.1.call-start
  4872.5 891.4 %all-reduce.113.cloned.1.call-start = ((), (), s32[]{:S(2)}) async-start(), calls=%async_computation.43 | async-start | bytes 36044800
  4887.9 904.3 %reduce-scatter.33.cloned.1.call-start = ((), (), s32[]{:S(2)}) async-start(), calls=%async_computation.27 | async-start | bytes 2457600 | tf_op jit(solution)/shard_map/reduce_scatter | solution.py:109
  4894.8 1045.3 %all-reduce.111.cloned.1.call-start = ((), (), s32[]{:S(2)}) async-start(), calls=%async_computation.42 | async-start | bytes 7208960 | tf_op jit(solution)/shard_map/psum | solution.py:597
  4904.8 1167.2 %all-reduce.109.cloned.1.call-start = ((), (), s32[]{:S(2)}) async-start(), calls=%async_computation.41 | async-start | bytes 282624 | tf_op jit(solution)/shard_map/psum | solution.py:597
  4915.3 1356.4 %reduce-scatter.45.cloned.1.call-start = ((), (), s32[]{:S(2)}) async-start(), calls=%async_computation.37 | async-start | bytes 12902400 | tf_op jit(solution)/shard_map/reduce_scatter | solution.py:154
  5485.3 32.8 collective-permute-start.35
  5495.2 18.0 collective-permute-start.34
  5501.6 24.5 collective-permute-start.37
  5507.7 27.9 collective-permute-start.36
  (688 other events, 8607.0 us)
Sparse Core Ops, SparseCore 0:
  39.3 16.2 reduce-scatter.24
  67.8 11.4 reduce-scatter.22
  708.4 84.0 all-gather.24
  795.7 69.5 all-gather.26
  1793.7 8.3 all-gather.12
  1836.9 31.8 reduce-scatter.26
  1871.2 12.0 reduce-scatter.34
  1897.2 12.0 reduce-scatter.28
  1911.8 14.8 reduce-scatter.30
  1932.8 12.8 all-gather.16
  1947.9 12.7 all-gather.18
  1968.2 27.9 reduce-scatter.36
  2021.3 11.0 reduce-scatter.40
  2041.1 10.7 reduce-scatter.38
  2705.5 71.9 all-gather.28
  4786.4 13.4 all-gather.22
  4853.8 14.4 all-gather.20
  4869.7 12.7 all-gather.14
  4884.9 27.9 reduce-scatter.42
  4917.1 846.7 all-reduce.112
  5766.2 25.9 reduce-scatter.32
  5799.4 140.7 all-reduce.110
  5949.5 122.4 all-reduce.108
  6076.4 195.2 reduce-scatter.44
where the time goes:
time: 6350 us; the launch traced here: 6290 us
  local copies, waits for them, and re-layouts  2650 us (42%)
  other arithmetic  1610 us (25%)
  waiting for transfers between devices  1030 us (16%)
  blocking collectives  652 us (10%)
  matrix products  207 us (3%)
  starting transfers between devices  114 us (2%)
    pad x352, local copies, waits for them, and re-layouts, linear_run(): lax.associative_scan(pair_combine, (decay_blk, inject), axis=0)  1570 us
    unnamed x1, blocking collectives  542 us
    add x192, other arithmetic, linear_run(): lax.associative_scan(pair_combine, (decay_blk, inject), axis=0)  424 us
    while x1088, local copies, waits for them, and re-layouts  407 us
    psum x2, waiting for transfers between devices, shards(): lax.psum((pre_full, post_full, meta_part, conv_weight_part, conv_bias_par...  277 us
    add x168, other arithmetic, pair_combine(): return (earlier[0] * latter[0], earlier[1] * latter[0] + latter[1])  250 us
    concatenate x168, other arithmetic, linear_run(): lax.associative_scan(pair_combine, (decay_blk, inject), axis=0)  245 us
    unnamed x29, waiting for transfers between devices  230 us
  transfers between devices with their start and end apart: 68, of which 35 were waited for; matrix products, arithmetic and copies ran while one was open for 47% of the time, Pallas kernels for 0%

commit v1 on v0

v1 whole, which is shorter than its diff:
```python
import functools
import math

import jax
import jax.numpy as jnp
from jax import lax
from jax.experimental import pallas as pl
from jax.experimental.pallas import tpu as pltpu
from jax.sharding import PartitionSpec as P

D = 1600
H = 25
KVH = 5
HD = 64
DI = 3200
STATE = 16
DT_RANK = 100
CONV = 4
META = 128
WIN = 1024


EPS = 1e-05
NEG = -1e30
THETA = 10000.0
HIGH = lax.Precision.HIGHEST
ALL = ("seq", "row", "col")
GROUP = ("row", "col")
LOG2E = 1.4426950408889634
LN2 = 0.6931471805599453
FAR = 1e30
SUB = 8
LANE = 128
VMEM_ASK = 58 * 2**20


def spread_gates(src_ref, dst_ref, length):

    def one(t, carry):
        rows = src_ref[pl.ds(t, SUB, stride=length), :]
        for n in range(STATE):
            dst_ref[t * STATE + n] = jnp.broadcast_to(rows[:, n : n + 1], (SUB, LANE))
        return carry

    lax.fori_loop(0, length, one, 0)


def chunk_decay(rate_ref, total_row):
    return jnp.exp2(rate_ref[...] * total_row)


def scan_totals(length, step_ref, input_ref, keep_ref, gate_ref, rate_ref, end_ref, part_ref, span_ref, wide):
    @pl.when(pl.program_id(0) == 0)
    def _():
        spread_gates(gate_ref, wide, length)

    rates = [jnp.broadcast_to(rate_ref[n : n + 1, :], (SUB, LANE)) for n in range(STATE)]

    def one(t, carry):
        states, span = carry
        rows = pl.ds(t, SUB, stride=length)
        step = step_ref[rows, :]
        lapse = jnp.where(keep_ref[rows, :] > 0.0, step, FAR)
        push = step * input_ref[rows, :]
        states = tuple(
            jnp.exp2(lapse * rates[n]) * states[n] + push * wide[t * STATE + n] for n in range(STATE)
        )
        return (states, span + lapse)

    zero = jnp.zeros((SUB, LANE), jnp.float32)
    states, span = lax.fori_loop(0, length, one, ((zero,) * STATE, zero), unroll=2)
    for n in range(STATE):
        part_ref[0, n] = states[n]
    span_ref[...] = span
    total = jnp.zeros((STATE, LANE), jnp.float32)
    lapsed = jnp.zeros((1, LANE), jnp.float32)
    for k in range(SUB):
        here = span_ref[k : k + 1, :]
        total = chunk_decay(rate_ref, here) * total + part_ref[0, :, k, :]
        lapsed = lapsed + here
    end_ref[0:STATE, :] = total
    end_ref[STATE:, :] = jnp.broadcast_to(lapsed, (SUB, LANE))


def scan_outputs(
    length, step_ref, input_ref, keep_ref, gate_ref, read_ref, rate_ref, part_ref, span_ref, start_ref,
    out_ref, kept_ref, wide, wide_read,
):
    @pl.when(pl.program_id(0) == 0)
    def _():
        spread_gates(gate_ref, wide, length)
        spread_gates(read_ref, wide_read, length)

    state = start_ref[...]
    for k in range(SUB):
        kept_ref[0, 0:STATE, k, :] = state
        state = chunk_decay(rate_ref, span_ref[k : k + 1, :]) * state + part_ref[0, :, k, :]
    rates = [jnp.broadcast_to(rate_ref[n : n + 1, :], (SUB, LANE)) for n in range(STATE)]

    def one(t, states):
        rows = pl.ds(t, SUB, stride=length)
        step = step_ref[rows, :]
        lapse = jnp.where(keep_ref[rows, :] > 0.0, step, FAR)
        push = step * input_ref[rows, :]
        new = []
        seen = [None, None]
        for n in range(STATE):
            value = jnp.exp2(lapse * rates[n]) * states[n] + push * wide[t * STATE + n]
            kept_ref[0, (t + 1) * STATE + n] = value
            part = value * wide_read[t * STATE + n]
            seen[n % 2] = part if seen[n % 2] is None else seen[n % 2] + part
            new.append(value)
        out_ref[rows, :] = seen[0] + seen[1]
        return tuple(new)

    lax.fori_loop(0, length, one, tuple(kept_ref[0, n] for n in range(STATE)), unroll=2)


def adjoint_totals(length, step_ref, dout_ref, keep_ref, read_ref, rate_ref, span_ref, end_ref, part_ref, wide):
    @pl.when(pl.program_id(0) == 0)
    def _():
        spread_gates(read_ref, wide, length)

    rates = [jnp.broadcast_to(rate_ref[n : n + 1, :], (SUB, LANE)) for n in range(STATE)]

    def one(k, carry):
        t = length - 1 - k
        rows = pl.ds(t, SUB, stride=length)
        lapse = jnp.where(keep_ref[rows, :] > 0.0, step_ref[rows, :], FAR)
        dout = dout_ref[rows, :]
        return tuple(
            jnp.exp2(lapse * rates[n]) * (carry[n] + dout * wide[t * STATE + n]) for n in range(STATE)
        )

    zero = jnp.zeros((SUB, LANE), jnp.float32)
    carry = lax.fori_loop(0, length, one, (zero,) * STATE, unroll=2)
    for n in range(STATE):
        part_ref[0, n] = carry[n]
    total = jnp.zeros((STATE, LANE), jnp.float32)
    for k in reversed(range(SUB)):
        total = chunk_decay(rate_ref, span_ref[k : k + 1, :]) * total + part_ref[0, :, k, :]
    end_ref[...] = total


def adjoint_grads(
    length, step_ref, input_ref, keep_ref, dout_ref, gate_ref, read_ref, rate_ref, part_ref, span_ref, start_ref, kept_ref,
    dprod_ref, dstep_ref, drate_ref, dgate_ref, dread_ref, wide, wide_read, entry,
):
    @pl.when(pl.program_id(0) == 0)
    def _():
        spread_gates(gate_ref, wide, length)
        spread_gates(read_ref, wide_read, length)
        dgate_ref[...] = jnp.zeros_like(dgate_ref)
        dread_ref[...] = jnp.zeros_like(dread_ref)

    state = start_ref[...]
    for k in reversed(range(SUB)):
        entry[:, k, :] = state
        state = chunk_decay(rate_ref, span_ref[k : k + 1, :]) * state + part_ref[0, :, k, :]
    half = STATE // 2
    zero = jnp.zeros((SUB, LANE), jnp.float32)
    for low in (0, half):
        rates = [jnp.broadcast_to(rate_ref[n : n + 1, :], (SUB, LANE)) for n in range(low, low + half)]

        def one(j, carry, low=low, rates=rates):
            incoming, rate_sum = carry
            t = length - 1 - j
            rows = pl.ds(t, SUB, stride=length)
            step = step_ref[rows, :]
            lapse = jnp.where(keep_ref[rows, :] > 0.0, step, FAR)
            push = step * input_ref[rows, :]
            dout = dout_ref[rows, :]
            outgoing, sums = [], []
            dprod, dstep = zero, zero
            for i in range(half):
                at = t * STATE + low + i
                adjoint = incoming[i] + dout * wide_read[at]
                dread_ref[at] = dread_ref[at] + kept_ref[0, at + STATE] * dout
                dgate_ref[at] = dgate_ref[at] + adjoint * push
                dprod = dprod + adjoint * wide[at]
                passed = jnp.exp2(lapse * rates[i]) * adjoint
                pull = passed * kept_ref[0, at]
                dstep = dstep + pull * rates[i]
                sums.append(rate_sum[i] + pull * step)
                outgoing.append(passed)
            if low == 0:
                dprod_ref[rows, :] = dprod
                dstep_ref[rows, :] = dstep
            else:
                dprod_ref[rows, :] = dprod_ref[rows, :] + dprod
                dstep_ref[rows, :] = (dstep_ref[rows, :] + dstep) * LN2
            return (tuple(outgoing), tuple(sums))

        start = (tuple(entry[low + i] for i in range(half)), (zero,) * half)
        _, rate_sum = lax.fori_loop(0, length, one, start)
        for i in range(half):
            drate_ref[low + i : low + i + 1, :] = -jnp.sum(rate_sum[i], axis=0, keepdims=True)


def column(rows):
    return pl.BlockSpec((rows, LANE), lambda i: (0, i))


def shared(shape):
    return pl.BlockSpec(shape, lambda i: (0,) * len(shape))


def tile_of(shape):
    return pl.BlockSpec((1,) + shape, lambda i: (i,) + (0,) * len(shape))


def scan_call(body, total, width, in_specs, outs, scratch, args, work):
    length = total // SUB
    params = pltpu.CompilerParams(dimension_semantics=("arbitrary",), vmem_limit_bytes=VMEM_ASK)
    return pl.pallas_call(
        functools.partial(body, length),
        grid=(width // LANE,),
        in_specs=in_specs,
        out_specs=[spec for spec, _ in outs],
        out_shape=[jax.ShapeDtypeStruct(shape, jnp.float32) for _, shape in outs],
        scratch_shapes=[pltpu.VMEM(shape, jnp.float32) for shape in scratch],
        compiler_params=params,
        cost_estimate=pl.CostEstimate(
            flops=work * total * width * STATE,
            transcendentals=total * width * STATE,
            bytes_accessed=16 * total * width,
        ),
    )(*args)


def run_totals(step, mixed, keep, gate, rates):
    total, width = step.shape
    length, tiles = total // SUB, width // LANE
    return scan_call(
        scan_totals,
        total,
        width,
        [column(total), column(total), shared((total, LANE)), shared((total, STATE)), column(STATE)],
        [
            (column(STATE + SUB), (STATE + SUB, width)),
            (tile_of((STATE, SUB, LANE)), (tiles, STATE, SUB, LANE)),
            (column(SUB), (SUB, width)),
        ],
        [(length * STATE, SUB, LANE)],
        (step, mixed, keep, gate, rates),
        6,
    )


def run_outputs(step, mixed, keep, gate, read, rates, part, span, start):
    total, width = step.shape
    length, tiles = total // SUB, width // LANE
    kept = ((length + 1) * STATE, SUB, LANE)
    return scan_call(
        scan_outputs,
        total,
        width,
        [column(total), column(total), shared((total, LANE)), shared((total, STATE)), shared((total, STATE)), column(STATE), tile_of((STATE, SUB, LANE)), column(SUB), column(STATE)],
        [(column(total), (total, width)), (tile_of(kept), (tiles,) + kept)],
        [(length * STATE, SUB, LANE)] * 2,
        (step, mixed, keep, gate, read, rates, part, span, start),
        9,
    )


def run_adjoint_totals(step, dout, keep, read, rates, span):
    total, width = step.shape
    length, tiles = total // SUB, width // LANE
    return scan_call(
        adjoint_totals,
        total,
        width,
        [column(total), column(total), shared((total, LANE)), shared((total, STATE)), column(STATE), column(SUB)],
        [
            (column(STATE), (STATE, width)),
            (tile_of((STATE, SUB, LANE)), (tiles, STATE, SUB, LANE)),
        ],
        [(length * STATE, SUB, LANE)],
        (step, dout, keep, read, rates, span),
        6,
    )


def run_adjoint_grads(step, mixed, keep, dout, gate, read, rates, part, span, start, kept):
    total, width = step.shape
    length = total // SUB
    wide = (length * STATE, SUB, LANE)
    return scan_call(
        adjoint_grads,
        total,
        width,
        [
            column(total), column(total), shared((total, LANE)), column(total),
            shared((total, STATE)), shared((total, STATE)), column(STATE),
            tile_of((STATE, SUB, LANE)), column(SUB), column(STATE), tile_of(kept.shape[1:]),
        ],
        [
            (column(total), (total, width)),
            (column(total), (total, width)),
            (column(STATE), (STATE, width)),
            (shared(wide), wide),
            (shared(wide), wide),
        ],
        [wide, wide, (STATE, SUB, LANE)],
        (step, mixed, keep, dout, gate, read, rates, part, span, start, kept),
        18,
    )


def dot_plain(left_op, right_op):
    return jnp.dot(left_op, right_op, preferred_element_type=jnp.float32)


def dot_left(left_op, right_op):
    return lax.dot_general(
        left_op, right_op, (((0,), (0,)), ((), ())), preferred_element_type=jnp.float32
    )


def dot_right(left_op, right_op):
    return lax.dot_general(
        left_op, right_op, (((1,), (1,)), ((), ())), preferred_element_type=jnp.float32
    )


def exact_dot(left_op, right_op):
    return jnp.dot(left_op, right_op, precision=HIGH, preferred_element_type=jnp.float32)


def exact_left(left_op, right_op):
    return lax.dot_general(
        left_op,
        right_op,
        (((0,), (0,)), ((), ())),
        precision=HIGH,
        preferred_element_type=jnp.float32,
    )


def exact_right(left_op, right_op):
    return lax.dot_general(
        left_op,
        right_op,
        (((1,), (1,)), ((), ())),
        precision=HIGH,
        preferred_element_type=jnp.float32,
    )


def low(values):
    return values.astype(jnp.bfloat16)


def wide(values):
    return values.astype(jnp.float32)


def swapped(values, axis):
    return lax.ppermute(values, axis, [(0, 1), (1, 0)])


def moved(values, axis, distance):
    count = lax.axis_size(axis)
    route = [(i, i + distance) for i in range(count) if 0 <= i + distance < count]
    return lax.ppermute(values, axis, route)


def joined(mine, other, place, axis):
    first = jnp.where(place == 0, mine, other)
    second = jnp.where(place == 0, other, mine)
    return jnp.concatenate([first, second], axis=axis)


def chosen(pieces, place):
    result = pieces[0]
    for index, piece in enumerate(pieces[1:], 1):
        result = jnp.where(place == index, piece, result)
    return result


def pieces_of(values, count, axis):
    size = values.shape[axis] // count
    return [lax.slice_in_dim(values, i * size, (i + 1) * size, axis=axis) for i in range(count)]


def group_total(values):
    over_cols = values + swapped(values, "col")
    return over_cols + swapped(over_cols, "row")


def seq_reduce(values):
    count, place = lax.axis_size("seq"), lax.axis_index("seq")
    parts = values.reshape((count, values.shape[0] // count) + values.shape[1:])
    if count > 8:
        return lax.psum_scatter(wide(parts), "seq", scatter_dimension=0)
    lines = count // 2
    odd, line = place % 2, place // 2
    pairs = parts.reshape((lines, 2) + parts.shape[1:])
    mine = jnp.where(odd == 0, pairs[:, 0], pairs[:, 1])
    other = jnp.where(odd == 0, pairs[:, 1], pairs[:, 0])
    got = lax.ppermute(other, "seq", [(i, i ^ 1) for i in range(count)])
    both = low(wide(mine) + wide(got))
    total = wide(lax.dynamic_index_in_dim(both, line, 0, keepdims=False))
    for step in range(1, lines):
        away = lax.dynamic_index_in_dim(both, (line + step) % lines, 0, keepdims=False)
        route = [(i, ((i // 2 + step) % lines) * 2 + i % 2) for i in range(count)]
        total = total + wide(lax.ppermute(away, "seq", route))
    return total


def rope_tables(positions):
    half_width = HD // 2
    frequency = THETA ** (-2.0 * jnp.arange(half_width, dtype=jnp.float32) / HD)
    angles = positions.astype(jnp.float32)[:, None] * frequency[None, :]
    cosine = jnp.concatenate([jnp.cos(angles), jnp.cos(angles)], axis=1)
    sine_tab = jnp.concatenate([jnp.sin(angles), jnp.sin(angles)], axis=1)
    return (cosine, sine_tab)


def rotate_half(values):
    half_width = values.shape[-1] // 2
    return jnp.concatenate([-values[..., half_width:], values[..., :half_width]], axis=-1)


def apply_rope(values, cosine, sine_tab):
    return values * cosine[:, None, :] + rotate_half(values) * sine_tab[:, None, :]


def rope_back(incoming, cosine, sine_tab):
    return incoming * cosine[:, None, :] - rotate_half(incoming * sine_tab[:, None, :])


def local_norm(values, gain_vec):
    factor = lax.rsqrt(jnp.mean(values * values, axis=1) + EPS)
    return (factor, values * factor[:, None] * gain_vec[None, :])


def local_norm_back(values, factor, gain_vec, incoming):
    weighted = incoming * gain_vec[None, :]
    inner_sum = jnp.mean(weighted * values, axis=1)
    result = factor[:, None] * weighted - values * (factor**3 * inner_sum)[:, None]
    return (result, jnp.sum(incoming * values * factor[:, None], axis=0))


def padded(values, width):
    return jnp.pad(values, ((0, 0), (0, width - values.shape[1])))


def shared_ends(values):
    count = lax.axis_size("seq")
    return lax.all_to_all(
        jnp.broadcast_to(values[None], (count,) + values.shape), "seq", split_axis=0, concat_axis=0
    )


def entering_state(ends, spans, rates, reverse):
    count, place = lax.axis_size("seq"), lax.axis_index("seq")
    state = jnp.zeros_like(ends[0])
    for k in range(count):
        at = count - 1 - k if reverse else k
        reached = at > place if reverse else at < place
        decay = jnp.exp2(rates * spans[at][None, :])
        state = jnp.where(reached, decay * state + ends[at], state)
    return state


def shards(
    hidden_in,
    grad_out,
    segment_ids,
    pre_gain,
    qkv_weight,
    mixer_in_weight,
    meta_cache,
    conv_weight,
    conv_bias,
    select_weight,
    step_weight,
    step_bias,
    log_rates,
    skip_gain,
    attn_gain,
    mixer_gain,
    attn_out_weight,
    mixer_out_weight,
    post_gain,
    gate_weight,
    up_weight,
    down_weight,
):
    row, col, seq = lax.axis_index("row"), lax.axis_index("col"), lax.axis_index("seq")
    tokens = hidden_in.shape[0]
    quarter = DI // 4
    lanes = -(-quarter // LANE) * LANE
    member = 2 * row + col

    def by_row(first, second):
        return jnp.where(row == 0, first, second)

    def row_joined(values):
        return joined(values, swapped(values, "row"), row, 1)

    def col_joined(values):
        return joined(values, swapped(values, "col"), col, 1)

    hidden_m = row_joined(hidden_in)
    gains_m = row_joined(jnp.stack([pre_gain, post_gain]))
    hidden_o = swapped(hidden_m, "col")
    gains_o = swapped(gains_m, "col")

    mixer_parts = pieces_of(mixer_in_weight, 4, 1)
    keep_w = by_row(chosen(mixer_parts[:2], col), chosen(mixer_parts[2:], col))
    give_w = by_row(chosen(mixer_parts[2:], col), chosen(mixer_parts[:2], col))
    keep_send = by_row(chosen(mixer_parts[:2], 1 - col), chosen(mixer_parts[2:], 1 - col))
    give_send = by_row(chosen(mixer_parts[2:], 1 - col), chosen(mixer_parts[:2], 1 - col))
    give_got = swapped(give_send, "col")
    keep_got = swapped(keep_send, "col")
    qkv_parts = pieces_of(qkv_weight, 2, 1)
    qkv_w = chosen(qkv_parts, col)
    qkv_got = swapped(chosen(qkv_parts, 1 - col), "col")

    def split_cols(weight):
        parts = pieces_of(weight, 2, 1)
        return chosen(parts, col), swapped(chosen(parts, 1 - col), "col")

    def split_rows(weight):
        parts = pieces_of(weight, 2, 0)
        return chosen(parts, col), swapped(chosen(parts, 1 - col), "col")

    hm, ho = wide(hidden_m), wide(hidden_o)
    pre_factor = lax.rsqrt((jnp.sum(hm * hm, axis=1) + jnp.sum(ho * ho, axis=1)) / D + EPS)
    first_m = low(hm * pre_factor[:, None] * gains_m[0][None, :])
    first_o = low(ho * pre_factor[:, None] * gains_o[0][None, :])

    given = low(dot_plain(first_m, give_w) + dot_plain(first_o, give_got))
    taken = swapped(given, "row")
    kept_in = low(dot_plain(first_m, keep_w) + dot_plain(first_o, keep_got))
    qkv_part = low(dot_plain(first_m, qkv_w) + dot_plain(first_o, qkv_got))
    qkv_core = lax.all_to_all(qkv_part, GROUP, split_axis=0, concat_axis=1, tiled=True)
    inner_own = by_row(kept_in, taken)
    gate_z = wide(by_row(taken, kept_in))

    grad_m = row_joined(grad_out)
    grad_o = swapped(grad_m, "col")
    gate_w, gate_got = split_cols(gate_weight)
    up_w, up_got = split_cols(up_weight)
    down_w, down_got = split_rows(down_weight)
    mixer_out_w, mixer_out_got = split_rows(mixer_out_weight)
    attn_out_w, attn_out_got = split_rows(attn_out_weight)

    own_tokens = tokens // 4
    devices_back = (WIN + own_tokens - 2) // own_tokens
    halo_rows = devices_back * own_tokens
    tail_rows = CONV - 1
    repeats = H // KVH
    kv_width = KVH * HD
    score_scale = HD ** (-0.5)
    start_row = seq * tokens + member * own_tokens
    seg_padded = jnp.concatenate([jnp.full((halo_rows,), -1, jnp.int32), segment_ids])
    key_segs = lax.dynamic_slice(seg_padded, (start_row,), (halo_rows + own_tokens,))
    query_segs = key_segs[halo_rows:]
    query_glob = start_row + jnp.arange(own_tokens, dtype=jnp.int32)
    key_glob = start_row - halo_rows + jnp.arange(halo_rows + own_tokens, dtype=jnp.int32)
    doc_start = jnp.sum((segment_ids[None, :] < query_segs[:, None]).astype(jnp.int32), axis=1)
    cosine, sine_tab = rope_tables(query_glob - doc_start)
    query_rot = low(
        apply_rope(wide(qkv_core[:, :D]).reshape(own_tokens, H, HD), cosine, sine_tab)
    )
    key_rot = low(
        apply_rope(
            wide(qkv_core[:, D : D + kv_width]).reshape(own_tokens, KVH, HD), cosine, sine_tab
        )
    ).reshape(own_tokens, kv_width)
    pair_own = jnp.concatenate([key_rot, qkv_core[:, D + kv_width :]], axis=1)
    halo = [moved(pair_own, ALL, offset) for offset in range(devices_back, 0, -1)]
    conv_tail = moved(inner_own[tokens - tail_rows :], "seq", 1)

    def channels(values, axis):
        return chosen(pieces_of(values, 4, axis), member)

    conv_w, conv_b = channels(conv_weight, 1), channels(conv_bias, 0)
    select_w, step_w = channels(select_weight, 0), channels(step_weight, 1)
    step_b, skip_g = channels(step_bias, 0), channels(skip_gain, 0)
    mixer_g = channels(mixer_gain, 0)
    decay_rates = jnp.exp(channels(log_rates, 0).T)
    rates = padded(-LOG2E * decay_rates, lanes)

    group_start = seq * tokens
    conv_segs = lax.dynamic_slice(
        seg_padded, (group_start + halo_rows - tail_rows,), (tokens + tail_rows,)
    )
    own_segs = conv_segs[tail_rows:]
    conv_input = wide(jnp.concatenate([conv_tail, inner_own], axis=0))
    tap_masks = [
        wide(conv_segs[tap : tap + tokens] == own_segs)[:, None] for tap in range(CONV)
    ]
    conv_sum = conv_b[None, :]
    for tap in range(CONV):
        conv_sum = conv_sum + conv_w[tap][None, :] * conv_input[tap : tap + tokens] * tap_masks[tap]
    mixed_in = jax.nn.silu(conv_sum)
    selected = group_total(exact_dot(mixed_in, select_w))
    step_low = selected[:, :DT_RANK]
    in_gate = selected[:, DT_RANK : DT_RANK + STATE]
    out_gate = selected[:, DT_RANK + STATE :]
    step_pre = exact_dot(step_low, step_w) + step_b[None, :]
    step_sizes = jax.nn.softplus(step_pre)
    keep_wide = jnp.broadcast_to(tap_masks[CONV - 2], (tokens, LANE))
    step_pad, mixed_pad = padded(step_sizes, lanes), padded(mixed_in, lanes)
    end, scan_part, scan_span = run_totals(step_pad, mixed_pad, keep_wide, in_gate, rates)
    ends = shared_ends(end)
    spans = ends[:, STATE, :]
    state_in = entering_state(ends[:, :STATE], spans, rates, False)

    keys_all = jnp.concatenate([meta_cache[0]] + [h[:, :kv_width] for h in halo] + [key_rot], axis=0)
    values_all = jnp.concatenate(
        [meta_cache[1]] + [h[:, kv_width:] for h in halo] + [pair_own[:, kv_width:]], axis=0
    )
    key_count = keys_all.shape[0]
    distance = query_glob[:, None] - key_glob[None, :]
    visible = (key_segs[None, :] == query_segs[:, None]) & (distance >= 0) & (distance < WIN)
    visible = jnp.concatenate([jnp.ones((own_tokens, META), jnp.bool_), visible], axis=1)
    query_groups = query_rot.reshape(own_tokens, KVH, repeats, HD).transpose(1, 2, 0, 3)
    key_groups = keys_all.reshape(key_count, KVH, HD).transpose(1, 0, 2)
    value_groups = values_all.reshape(key_count, KVH, HD).transpose(1, 0, 2)

    def group_scores(query_grp, key_grp):
        raw_scores = (
            jnp.einsum("rqd,kd->rqk", query_grp, key_grp, preferred_element_type=jnp.float32)
            * score_scale
        )
        return jnp.where(visible[None], raw_scores, NEG)

    def group_forward(operands):
        query_grp, key_grp, value_grp = operands
        scores = group_scores(query_grp, key_grp)
        highest = jnp.max(scores, axis=-1, keepdims=True)
        exponent = jnp.exp(scores - highest)
        totals = jnp.sum(exponent, axis=-1, keepdims=True)
        softmax_out = exponent / totals
        output = jnp.einsum(
            "rqk,kd->rqd", low(softmax_out), value_grp, preferred_element_type=jnp.float32
        )
        return (output, (highest + jnp.log(totals))[..., 0])

    attn_groups, log_totals = lax.map(group_forward, (query_groups, key_groups, value_groups))
    attn_flat = attn_groups.transpose(2, 0, 1, 3).reshape(own_tokens, D)
    attn_factor, attn_normed = local_norm(attn_flat, attn_gain)
    attn_low = low(attn_normed)
    attn_part = lax.all_to_all(attn_low, GROUP, split_axis=1, concat_axis=0, tiled=True)
    attn_rows = col_joined(attn_part)

    scan_out, kept = run_outputs(
        step_pad, mixed_pad, keep_wide, in_gate, out_gate, rates, scan_part, scan_span, state_in
    )
    mixed_out = scan_out[:, :quarter] + skip_g[None, :] * mixed_in
    z_silu = jax.nn.silu(gate_z)
    mixer_value = mixed_out * z_silu
    mixer_mean = lax.psum(jnp.sum(mixer_value * mixer_value, axis=1), GROUP) / DI
    mixer_factor = lax.rsqrt(mixer_mean + EPS)
    mixer_low = low(mixer_value * mixer_factor[:, None] * mixer_g[None, :])
    mixer_rows = col_joined(mixer_low)

    def row_summed(part):
        part = low(part)
        return wide(part) + wide(swapped(part, "row"))

    mix_m = row_summed(
        0.5 * (dot_plain(attn_rows, attn_out_weight) + dot_plain(mixer_rows, mixer_out_weight))
    )
    mix_o = swapped(mix_m, "col")
    resid_m, resid_o = hm + mix_m, ho + mix_o
    post_factor = lax.rsqrt(
        (jnp.sum(resid_m * resid_m, axis=1) + jnp.sum(resid_o * resid_o, axis=1)) / D + EPS
    )
    second_m = low(resid_m * post_factor[:, None] * gains_m[1][None, :])
    second_o = low(resid_o * post_factor[:, None] * gains_o[1][None, :])
    gate_act = dot_plain(second_m, gate_w) + dot_plain(second_o, gate_got)
    up_act = dot_plain(second_m, up_w) + dot_plain(second_o, up_got)
    dact = dot_right(grad_m, down_w) + dot_right(grad_o, down_got)
    sig_gate = jax.nn.sigmoid(gate_act)
    act_low = low(gate_act * sig_gate * up_act)
    dgate_low = low(dact * up_act * sig_gate * (1.0 + gate_act * (1.0 - sig_gate)))
    dup_low = low(dact * gate_act * sig_gate)
    dgate_rows = col_joined(dgate_low)
    dup_rows = col_joined(dup_low)
    act_rows = col_joined(act_low)
    dsecond_m = row_summed(dot_right(dgate_rows, gate_weight) + dot_right(dup_rows, up_weight))
    dsecond_o = swapped(dsecond_m, "col")
    weighted_m = dsecond_m * gains_m[1][None, :]
    weighted_o = dsecond_o * gains_o[1][None, :]
    inner_sum = (jnp.sum(weighted_m * resid_m, axis=1) + jnp.sum(weighted_o * resid_o, axis=1)) / D
    pull_back = (post_factor**3 * inner_sum)[:, None]
    dmid_m = wide(grad_m) + post_factor[:, None] * weighted_m - resid_m * pull_back
    dmid_o = wide(grad_o) + post_factor[:, None] * weighted_o - resid_o * pull_back
    post_part = jnp.sum(dsecond_m * resid_m * post_factor[:, None], axis=0)
    low_m, low_o = low(dmid_m), low(dmid_o)

    dmixer_low = low(0.5 * (dot_right(low_m, mixer_out_w) + dot_right(low_o, mixer_out_got)))
    dattn_part = low(0.5 * (dot_right(low_m, attn_out_w) + dot_right(low_o, attn_out_got)))
    dattn_core = lax.all_to_all(dattn_part, GROUP, split_axis=0, concat_axis=1, tiled=True)

    grad_down = seq_reduce(low(dot_left(grad_m, act_rows)))
    grad_gate = seq_reduce(low(dot_left(dgate_rows, second_m)))
    grad_up = seq_reduce(low(dot_left(dup_rows, second_m)))
    grad_attn_out = seq_reduce(low(0.5 * dot_left(low_m, attn_rows)))
    grad_mixer_out = seq_reduce(low(0.5 * dot_left(low_m, mixer_rows)))

    dmixer_wide = wide(dmixer_low)
    mixer_weighted = dmixer_wide * mixer_g[None, :]
    mixer_sum = lax.psum(jnp.sum(mixer_weighted * mixer_value, axis=1), GROUP) / DI
    dmixer_value = (
        mixer_factor[:, None] * mixer_weighted
        - mixer_value * (mixer_factor**3 * mixer_sum)[:, None]
    )
    mixer_gain_part = jnp.sum(dmixer_wide * mixer_value * mixer_factor[:, None], axis=0)
    sig_z = jax.nn.sigmoid(gate_z)
    dmixed_out = dmixer_value * z_silu
    dgate_z = dmixer_value * mixed_out * sig_z * (1.0 + gate_z * (1.0 - sig_z))
    skip_part = jnp.sum(dmixed_out * mixed_in, axis=0)
    dout_pad = padded(dmixed_out, lanes)
    back_end, back_part = run_adjoint_totals(
        step_pad, dout_pad, keep_wide, out_gate, rates, scan_span
    )
    adjoint_in = entering_state(shared_ends(back_end), spans, rates, True)

    dattn_flat, attn_gain_part = local_norm_back(attn_flat, attn_factor, attn_gain, wide(dattn_core))
    dattn_groups = low(dattn_flat).reshape(own_tokens, KVH, repeats, HD).transpose(1, 2, 0, 3)

    def group_backward(operands):
        query_grp, key_grp, value_grp, dout_grp, lse_grp = operands
        scores = group_scores(query_grp, key_grp)
        softmax_out = jnp.exp(scores - lse_grp[..., None])
        dprobs = jnp.einsum("rqd,kd->rqk", dout_grp, value_grp, preferred_element_type=jnp.float32)
        delta_row = jnp.sum(softmax_out * dprobs, axis=-1, keepdims=True)
        dscores = low(softmax_out * (dprobs - delta_row))
        dquery = (
            jnp.einsum("rqk,kd->rqd", dscores, key_grp, preferred_element_type=jnp.float32)
            * score_scale
        )
        dkey = (
            jnp.einsum("rqk,rqd->kd", dscores, query_grp, preferred_element_type=jnp.float32)
            * score_scale
        )
        dvalue = jnp.einsum(
            "rqk,rqd->kd", low(softmax_out), dout_grp, preferred_element_type=jnp.float32
        )
        return (dquery, dkey, dvalue)

    dquery_groups, dkey_groups, dvalue_groups = lax.map(
        group_backward, (query_groups, key_groups, value_groups, dattn_groups, log_totals)
    )
    dquery_flat = dquery_groups.transpose(2, 0, 1, 3).reshape(own_tokens, H, HD)
    dkey_all = dkey_groups.transpose(1, 0, 2).reshape(key_count, kv_width)
    dvalue_all = dvalue_groups.transpose(1, 0, 2).reshape(key_count, kv_width)
    dpair_all = jnp.concatenate([dkey_all, dvalue_all], axis=1)
    dpair_own = dpair_all[META + halo_rows :]
    for offset in range(1, devices_back + 1):
        low_row = META + (devices_back - offset) * own_tokens
        piece = low(dpair_all[low_row : low_row + own_tokens])
        dpair_own = dpair_own + wide(moved(piece, ALL, -offset))
    dquery_rot = rope_back(dquery_flat, cosine, sine_tab).reshape(own_tokens, D)
    dkey_rot = rope_back(
        dpair_own[:, :kv_width].reshape(own_tokens, KVH, HD), cosine, sine_tab
    ).reshape(own_tokens, kv_width)
    dqkv_core = low(jnp.concatenate([dquery_rot, dkey_rot, dpair_own[:, kv_width:]], axis=1))
    dqkv_part = lax.all_to_all(dqkv_core, GROUP, split_axis=1, concat_axis=0, tiled=True)
    dqkv_rows = col_joined(dqkv_part)
    grad_qkv = seq_reduce(low(dot_left(dqkv_rows, first_m)))

    dproduct, dstep_decay, drates, dgate_wide, dread_wide = run_adjoint_grads(
        step_pad, mixed_pad, keep_wide, dout_pad, in_gate, out_gate, rates, back_part, scan_span,
        adjoint_in, kept,
    )

    def by_token(values):
        summed = jnp.sum(values, axis=-1).reshape(tokens // SUB, STATE, SUB)
        return summed.transpose(2, 0, 1).reshape(tokens, STATE)

    dproduct = dproduct[:, :quarter]
    dsteps = dstep_decay[:, :quarter] + dproduct * mixed_in
    dstep_pre = dsteps * jax.nn.sigmoid(step_pre)
    step_bias_part = jnp.sum(dstep_pre, axis=0)
    step_weight_part = exact_left(step_low, dstep_pre)
    dselected = group_total(
        jnp.concatenate(
            [exact_right(dstep_pre, step_w), by_token(dgate_wide), by_token(dread_wide)], axis=1
        )
    )
    select_part = exact_left(dselected, mixed_in)
    dmixed_in = (
        dmixed_out * skip_g[None, :]
        + dproduct * step_sizes
        + exact_right(dselected, select_w)
    )
    sig_conv = jax.nn.sigmoid(conv_sum)
    dconv_sum = dmixed_in * sig_conv * (1.0 + conv_sum * (1.0 - sig_conv))
    conv_bias_part = jnp.sum(dconv_sum, axis=0)
    conv_rows = []
    dconv_input = jnp.zeros((tokens + tail_rows, quarter), jnp.float32)
    for tap in range(CONV):
        masked_grad = dconv_sum * tap_masks[tap]
        conv_rows.append(jnp.sum(masked_grad * conv_input[tap : tap + tokens], axis=0))
        dconv_input = dconv_input + jnp.pad(
            masked_grad * conv_w[tap][None, :], ((tap, tail_rows - tap), (0, 0))
        )
    dtail_back = moved(dconv_input[:tail_rows], "seq", -1)
    dinner_own = low(
        dconv_input[tail_rows:] + jnp.pad(dtail_back, ((tokens - tail_rows, 0), (0, 0)))
    )
    dz_own = low(dgate_z)
    got_back = swapped(by_row(dz_own, dinner_own), "row")
    near_m = by_row(dinner_own, got_back)
    far_m = by_row(got_back, dz_own)
    near_o, far_o = swapped(near_m, "col"), swapped(far_m, "col")
    near = [jnp.where(col == 0, near_m, near_o), jnp.where(col == 0, near_o, near_m)]
    far = [jnp.where(col == 0, far_m, far_o), jnp.where(col == 0, far_o, far_m)]
    dinner_rows = jnp.concatenate(near + far, axis=1)
    grad_mixer_in = seq_reduce(low(dot_left(dinner_rows, first_m)))

    params = jnp.concatenate(
        [
            select_part,
            step_weight_part,
            drates[:, :quarter] * decay_rates,
            jnp.stack(conv_rows, axis=0),
            conv_bias_part[None],
            step_bias_part[None],
            skip_part[None],
            mixer_gain_part[None],
        ],
        axis=0,
    )
    params = seq_reduce(low(params))
    params = wide(lax.all_gather(low(params), ALL))
    count = lax.axis_size("seq")
    params = params.reshape((count, 4) + params.shape[1:]).transpose(0, 2, 1, 3).reshape(-1, DI)

    dfirst_part = dot_right(dqkv_rows, qkv_weight) + dot_right(dinner_rows, mixer_in_weight)
    first_sum = lax.psum(jnp.sum(dfirst_part * gains_m[0][None, :] * hm, axis=1), GROUP) / D

    def block(values):
        parts = pieces_of(values, 2, 1)
        return by_row(*parts)

    def row_scattered(part):
        parts = pieces_of(part, 2, 1)
        away = low(by_row(parts[1], parts[0]))
        return by_row(*parts) + wide(swapped(away, "row"))

    dfirst = row_scattered(dfirst_part)
    own_hidden = wide(hidden_in)
    grad_in = (
        block(dmid_m)
        + pre_factor[:, None] * dfirst * pre_gain[None, :]
        - own_hidden * (pre_factor**3 * first_sum)[:, None]
    )
    pre_part = jnp.sum(dfirst * own_hidden * pre_factor[:, None], axis=0)
    hidden_out = low(block(resid_m) + row_scattered(dot_plain(act_rows, down_weight)))

    gain_block = pre_gain.shape[0]
    block_pos = (2 * col + row) * gain_block

    def spread(part):
        return lax.dynamic_update_slice(jnp.zeros((D,), jnp.float32), part, (block_pos,))

    meta_part = jnp.stack([dkey_all[:META], dvalue_all[:META]], axis=0)
    post_own = block(post_part[None])[0]
    meta_grad, attn_gain_grad, post_grad = lax.psum(
        (meta_part, attn_gain_part, spread(post_own)), ALL
    )
    pre_grad = lax.psum(spread(pre_part), ALL)
    ranks = DT_RANK + 2 * STATE
    at_rates = ranks + DT_RANK
    at_conv = at_rates + STATE
    return (
        hidden_out,
        grad_in,
        pre_grad,
        grad_qkv.T,
        grad_mixer_in.T,
        meta_grad,
        params[at_conv : at_conv + CONV],
        params[at_conv + CONV],
        params[:ranks].T,
        params[ranks:at_rates],
        params[at_conv + CONV + 1],
        params[at_rates:at_conv].T,
        params[at_conv + CONV + 2],
        attn_gain_grad,
        params[at_conv + CONV + 3],
        grad_attn_out.T,
        grad_mixer_out.T,
        post_grad,
        grad_gate.T,
        grad_up.T,
        grad_down.T,
    )


def solution(mesh):
    in_specs = (
        P("seq", ("col", "row")),
        P("seq", ("col", "row")),
        P(),
        P(("col", "row")),
        P("col", "row"),
        P("col", "row"),
        P(),
        P(),
        P(),
        P(),
        P(),
        P(),
        P(),
        P(),
        P(),
        P(),
        P("row", "col"),
        P("row", "col"),
        P(("col", "row")),
        P("col", "row"),
        P("col", "row"),
        P("row", "col"),
    )
    out_specs = (
        P("seq", ("col", "row")),
        P("seq", ("col", "row")),
        P(),
        P("col", ("row", "seq")),
        P("col", ("row", "seq")),
        P(),
        P(),
        P(),
        P(),
        P(),
        P(),
        P(),
        P(),
        P(),
        P(),
        P("row", ("col", "seq")),
        P("row", ("col", "seq")),
        P(),
        P("col", ("row", "seq")),
        P("col", ("row", "seq")),
        P("row", ("col", "seq")),
    )
    return jax.shard_map(shards, mesh=mesh, in_specs=in_specs, out_specs=out_specs, check_vma=False)
```

time: 6350 us -> 1290 us (0.20)
  local copies, waits for them, and re-layouts: 2650 us -> 255 us
  other arithmetic: 1610 us -> 184 us
  waiting for transfers between devices: 1030 us -> 237 us
  blocking collectives: 652 us -> 97.4 us
  Pallas kernels: 0 us -> 131 us
    pad x416 -> x4, local copies, waits for them, and re-layouts: 1780 us -> 4.87 us  [padded(): return jnp.pad(values, ((0, 0), (0, width - values.shape[1])))]
    add x420 -> x5, other arithmetic: 829 us -> 0.93 us  [the longest x1 0.58 us: shards(): dconv_input + jnp.pad(masked_grad * conv_w[tap][None, :], ((tap, tail_row...]
    unnamed x1 -> x0, blocking collectives: 542 us -> none
    while x1090 -> x0, local copies, waits for them, and re-layouts: 408 us -> none
    reduce_scatter x12 -> x0, waiting for transfers between devices: 299 us -> none  [the longest x1 200 us: reduce_grads(): lax.psum_scatter(values[6], 'seq', scatter_dimension=1, tiled=True)]
    concatenate x202 -> x6, other arithmetic: 282 us -> 2.21 us  [the longest x2 1.33 us: joined(): return jnp.concatenate([first, second], axis=axis)]
    psum x2 -> x1, waiting for transfers between devices: 277 us -> 0.01 us  [shards(): lax.psum((meta_part, attn_gain_part, spread(post_own)), ALL)]
    unnamed x29 -> x2, waiting for transfers between devices: 230 us -> 0.03 us
  transfers between devices with their start and end apart: 68 -> 92, of which waited for: 35 -> 20; matrix products, arithmetic and copies ran while one was open for 47% -> 42% of each run, Pallas kernels for 0% -> 4%
where the time goes in v1:
time: 1290 us; the launch traced here: 1280 us
  local copies, waits for them, and re-layouts  255 us (20%)
  waiting for transfers between devices  237 us (18%)
  matrix products  192 us (15%)
  other arithmetic  184 us (14%)
  starting transfers between devices  165 us (13%)
  Pallas kernels  131 us (10%)
  blocking collectives  97.4 us (8%)
  between operations  17.4 us (1%)
    pallas_call x4, Pallas kernels, scan_call(): pl.pallas_call(functools.partial(body, length), grid=(width // LANE,), in...  131 us
    ppermute x24, waiting for transfers between devices, seq_reduce(): total = total + wide(lax.ppermute(away, 'seq', route))  112 us
    ppermute x8, waiting for transfers between devices, seq_reduce(): got = lax.ppermute(other, 'seq', [(i, i ^ 1) for i in range(count)])  80.4 us
    psum x1, blocking collectives, shards(): pre_grad = lax.psum(spread(pre_part), ALL)  71.9 us
    ppermute x24, starting transfers between devices, seq_reduce(): total = total + wide(lax.ppermute(away, 'seq', route))  56.4 us
    another operation x6, local copies, waits for them, and re-layouts, seq_reduce(): pairs = parts.reshape((lines, 2) + parts.shape[1:])  48.8 us
    dot_general x13, matrix products, dot_plain(): return jnp.dot(left_op, right_op, preferred_element_type=jnp.float32)  45 us
    ppermute x18, starting transfers between devices, moved(): return lax.ppermute(values, axis, route)  44.7 us
  transfers between devices with their start and end apart: 92, of which 20 were waited for; matrix products, arithmetic and copies ran while one was open for 42% of the time, Pallas kernels for 4%

profile of v1, /device:TPU:0, one launch (start us, length us, event | category | flops | bytes accessed | tf_op | source)
XLA Modules:
  0.0 1279.9 jit_solution(8824973892409053959)
XLA Ops:
  7.2 7.3 fusion.268
  117.8 8.2 collective-permute-start.17
  137.7 11.0 collective-permute-done.19
  156.1 18.8 %shard_map.373 = (f32[24,896]{1,0:T(8,128)}, f32[7,16,8,128]{3,2,1,0:T(8,128)}, f32[8,896]{1,0:T(8,128)}) custom-call(f32[512,896]{1,0:T(8,128)} %pad.36.step_ref, f32[512,896]{1,0:T(8,128)} %pad.37.input_ref, f32[512,128]{1,0:T(8,128)} %broadcast_in_dim.61.keep_ref, f32[512,16]{1,0:T(8,128)} %get-tuple-element.419.gate_ref, f32[16,896]{1,0:T(8,128)} %pad.38.rate_ref), custom_call_target="tpu_custom_call" | custom-call | flops 44040192 | bytes 7340032 | tf_op jit(solution)/shard_map/pallas_call | solution.py:215
  176.7 6.9 all-to-all-start.2
  184.6 26.9 %while.26 = (s32[]{:T(128)}, f32[5,5,128,64]{2,3,1,0:T(8,128)}, f32[5,5,128]{2,1,0:T(8,128)}, pred[128,1280]{1,0:T(8,128)(4,1)S(1)}, bf16[5,5,128,64]{2,3,1,0:T(...) while((s32[]{:T(128)}, f32[5,5,128,64]{2,3,1,0:T(8,128)}, ...), condition=%wide.region_6.7_spmd, body=%wide.region_3.6_spmd.sunk | while | flops 216268160 | bytes 10591841 | solution.py:645
  222.2 30.7 %shard_map.374 = (f32[512,896]{1,0:T(8,128)}, f32[7,1040,8,128]{3,2,1,0:T(8,128)}) custom-call(f32[512,896]{1,0:T(8,128)} %pad.36.step_ref, f32[512,896]{1,0:T(8,128)} %pad.37.input_ref, f32[512,128]{1,0:T(8,128)} %broadcast_in_dim.61.keep_ref, f32[512,16]{1,0:T(8,128)} %get-tuple-element.419.gate_ref, f32[512,16]{1,0:T(8,128)} %get-tuple-element.418.read_ref, ...), custom_call_target="tpu_custom_call" | custom-call | flops 66060288 | bytes 7340032 | tf_op jit(solution)/shard_map/pallas_call | solution.py:215
  257.0 7.8 psum.49
  299.1 8.7 collective-permute-done.21
  321.7 4.8 broadcast_select_fusion.2
  341.2 5.2 fusion.52
  352.6 6.5 multiply_convert_fusion.4
  365.6 6.5 fusion.89
  382.0 5.1 convolution_convert_fusion.3
  394.4 17.3 %reshape_reshape.26 = bf16[4,2,344,800]{2,1,0,3:T(2,128)(2,1)} reshape(bf16[2752,800]{0,1:T(8,128)(2,1)} %convolution_convert_fusion.3) | data formatting | bytes 8806400 | tf_op jit(solution)/shard_map/reshape;reshape | solution.py:398
  411.7 10.4 fusion.270
  428.6 17.2 %reshape_reshape.27 = bf16[4,2,344,800]{2,1,0,3:T(2,128)(2,1)} reshape(bf16[2752,800]{0,1:T(8,128)(2,1)} %convolution_convert_fusion.2) | data formatting | bytes 8806400 | tf_op jit(solution)/shard_map/reshape;reshape | solution.py:398
  445.8 10.7 fusion.269
  461.8 5.0 convolution_convert_fusion.1
  466.7 5.3 reshape_reshape.28
  495.6 5.6 fusion.45
  503.2 32.5 %collective-permute-done.76 = bf16[4,344,800]{1,2,0:T(8,128)(2,1)} collective-permute-done((bf16[4,344,800]{1,2,0:T(8,128)(2,1)}, bf16[4,344,800]{1,2,0:T(8,128)(2,1)}, u32[]{:S(2)}, u32[]{:S(2)}) %collective-permute-start.76) | collective-permute-done | bytes 2201632 | tf_op jit(solution)/shard_map/ppermute | solution.py:401
  543.7 39.5 %collective-permute-done.80 = bf16[4,100,2752]{2,0,1:T(4,128)(2,1)} collective-permute-done((bf16[4,100,2752]{2,0,1:T(4,128)(2,1)}, bf16[4,100,2752]{2,0,1:T(4,128)(2,1)}, u32[]{:S(2)}, u32[]{:S(2)}) %collective-permute-start.80) | collective-permute-done | bytes 2201632 | tf_op jit(solution)/shard_map/ppermute | solution.py:401
  612.5 6.0 psum.50
  651.7 19.6 %shard_map.375 = (f32[16,896]{1,0:T(8,128)}, f32[7,16,8,128]{3,2,1,0:T(8,128)}) custom-call(f32[512,896]{1,0:T(8,128)} %pad.36.step_ref, f32[512,896]{1,0:T(8,128)} %pad.39.dout_ref, f32[512,128]{1,0:T(8,128)} %broadcast_in_dim.61.keep_ref, f32[512,16]{1,0:T(8,128)} %get-tuple-element.418.read_ref, f32[16,896]{1,0:T(8,128)} %pad.38.rate_ref, ...), custom_call_target="tpu_custom_call" | custom-call | flops 44040192 | bytes 7340032 | tf_op jit(solution)/shard_map/pallas_call | solution.py:215
  675.2 5.0 all-to-all-start.5
  686.4 7.3 all-to-all-done.5
  694.4 62.0 %shard_map.376 = (f32[512,896]{1,0:T(8,128)}, f32[512,896]{1,0:T(8,128)}, f32[16,896]{1,0:T(8,128)}, f32[1024,8,128]{2,1,0:T(8,128)}, f32[1024,8,128]{2,1,0:T(8,128)}) custom-call(f32[512,896]{1,0:T(8,128)} %pad.36.step_ref, f32[512,896]{1,0:T(8,128)} %pad.37.input_ref, f32[512,128]{1,0:T(8,128)} %broadcast_in_dim.61.keep_ref, f32[512,896]{1,0:T(8,128)} %pad.39.dout_ref, ...), custom_call_target="tpu_custom_call" | custom-call | flops 132120576 | bytes 7340032 | tf_op jit(solution)/shard_map/pallas_call | solution.py:215
  774.7 5.6 collective-permute-done.46
  780.4 6.4 multiply_reduce_fusion.3
  803.8 52.5 %while.27 = (s32[]{:T(128)}, f32[5,5,128,64]{2,3,1,0:T(8,128)S(1)}, f32[5,1280,64]{1,2,0:T(8,128)}, f32[5,1280,64]{1,2,0:T(8,128)}, pred[128,1280]{1,0:T(8,128)(...) while((s32[]{:T(128)}, f32[5,5,128,64]{2,3,1,0:T(8,128)S(1)}, ...), condition=%wide.region_17.18_spmd, body=%wide.region_15.17_spmd.sunk | while | flops 531783040 | bytes 26396280 | solution.py:749
  877.2 8.0 collective-permute-start.79
  889.2 10.8 all-to-all-start.4
  900.1 4.8 collective-permute-done.64
  906.3 6.9 collective-permute-start.67
  913.2 17.9 %collective-permute-start.66 = (bf16[100,800]{1,0:T(8,128)(2,1)S(1)}, bf16[100,800]{1,0:T(8,128)(2,1)S(1)}, u32[]{:S(2)}, u32[]{:S(2)}) collective-permute-start(bf16[100,800]{1,0:T(8,128)(2,1)S(1)} %get-tuple-element.415), channel_id=1, source_target_pairs={{0,16},{4,20},{8,24},{12,28},{16,0},{20,4},{24,8},{28,12},{1,17},{... | collective-permute-start | bytes 480008 | tf_op jit(solution)/shard_map/ppermute | solution.py:407
  931.1 27.7 %collective-permute-done.78 = bf16[344,800]{0,1:T(8,128)(2,1)} collective-permute-done((bf16[344,800]{0,1:T(8,128)(2,1)}, bf16[344,800]{0,1:T(8,128)(2,1)}, u32[]{:S(2)}, u32[]{:S(2)}) %collective-permute-start.78) | collective-permute-done | bytes 550432 | tf_op jit(solution)/shard_map/ppermute | solution.py:407
  964.5 4.9 collective-permute-done.66
  1013.8 20.3 %collective-permute-done.70 = bf16[100,1600]{1,0:T(8,128)(2,1)S(1)} collective-permute-done((bf16[100,1600]{1,0:T(8,128)(2,1)}, bf16[100,1600]{1,0:T(8,128)(2,1)S(1)}, u32[]{:S(2)}, u32[]{:S(2)}) %collective-permute-start.70) | collective-permute-done | bytes 320032 | tf_op jit(solution)/shard_map/ppermute | solution.py:407
  1051.6 7.2 concatenate.179
  1058.8 8.6 fusion.288
  1067.4 5.5 convolution_convert_fusion
  1072.9 8.6 copy.384
  1095.3 11.7 psum.51
  1111.8 71.9 %all-reduce.11 = (f32[1600]{0:T(1024)}, f32[1600]{0:T(1024)}, f32[1600]{0:T(1024)}) all-reduce(f32[1600]{0:T(1024)S(1)} %dynamic_update_slice.24, f32[1600]{0:T(1024)S(1)} %reduce_sum.269, f32[1600]{0:T(1024)S(1)} %copy-done.151), channel_id=1, replica_groups=mesh['seq'=8,'row'=2,'col'=2] {'seq','row','col'}, use_global_device_ids=true, to_apply=%region_25.26 | all-reduce | flops 4800 | bytes 38400 | tf_op jit(solution)/shard_map/psum | solution.py:871
  1188.0 5.4 reshape.402
  1211.1 14.1 %collective-permute-done.59 = bf16[400,800]{1,0:T(8,128)(2,1)S(1)} collective-permute-done((bf16[400,800]{1,0:T(8,128)(2,1)S(1)}, bf16[400,800]{1,0:T(8,128)(2,1)S(1)}, u32[]{:S(2)}, u32[]{:S(2)}) %collective-permute-start.59) | collective-permute-done | bytes 640032 | tf_op jit(solution)/shard_map/ppermute | solution.py:407
  1225.2 44.5 %collective-permute-done.58 = bf16[400,800]{1,0:T(8,128)(2,1)S(1)} collective-permute-done((bf16[400,800]{1,0:T(8,128)(2,1)S(1)}, bf16[400,800]{1,0:T(8,128)(2,1)S(1)}, u32[]{:S(2)}, u32[]{:S(2)}) %collective-permute-start.58) | collective-permute-done | bytes 640032 | tf_op jit(solution)/shard_map/ppermute | solution.py:407
  (915 shorter events, 600.4 us)
Async XLA Ops:
  29.8 36.9 %collective-permute-start.15 = (bf16[800,800]{0,1:T(8,128)(2,1)}, bf16[800,800]{0,1:T(8,128)(2,1)}, u32[]{:S(2)}, u32[]{:S(2)}) collective-permute-start(bf16[800,800]{0,1:T(8,128)(2,1)} %get-tuple-element.338), channel_id=1, source_target_pairs={{0,1},{1,0},{2,3},{3,2},{4,5},{5,4},{6,7},{7,6},{8,9},{9,8},{10,11... | collective-permute-start | bytes 3840008 | tf_op jit(solution)/shard_map/ppermute | solution.py:359
  34.2 39.7 %collective-permute-start.14 = (bf16[800,800]{0,1:T(8,128)(2,1)}, bf16[800,800]{0,1:T(8,128)(2,1)}, u32[]{:S(2)}, u32[]{:S(2)}) collective-permute-start(bf16[800,800]{0,1:T(8,128)(2,1)} %get-tuple-element.339), channel_id=1, source_target_pairs={{0,1},{1,0},{2,3},{3,2},{4,5},{5,4},{6,7},{7,6},{8,9},{9,8},{10,11... | collective-permute-start | bytes 3840008 | tf_op jit(solution)/shard_map/ppermute | solution.py:359
  72.0 38.8 %collective-permute-start.16 = (bf16[512,800]{0,1:T(8,128)(2,1)}, bf16[512,800]{0,1:T(8,128)(2,1)}, u32[]{:S(2)}, u32[]{:S(2)}) collective-permute-start(bf16[512,800]{0,1:T(8,128)(2,1)} %add_convert_fusion.2), channel_id=1, source_target_pairs={{0,2},{2,0},{1,3},{3,1},{4,6},{6,4},{5,7},{7,5},{8,10},{10,8},{9,1... | collective-permute-start | bytes 2457608 | tf_op jit(solution)/shard_map/ppermute | solution.py:359
  176.7 38.6 %all-to-all-start.2 = ((f32[8,24,896]{2,1,0:T(8,128)}), f32[8,24,896]{2,1,0:T(8,128)}, u32[]{:S(2)}, u32[]{:S(2)}) async-start(f32[8,24,896]{2,1,0:T(8,128)} %broadcast_in_dim.62), calls=%async_computation.2 | async-start | bytes 1376256 | tf_op jit(solution)/shard_map/all_to_all | solution.py:451
  215.3 54.2 %all-to-all-start.1 = ((bf16[128,4,400]{0,2,1:T(8,128)(2,1)}), bf16[128,4,400]{0,2,1:T(8,128)(2,1)}, u32[]{:S(2)}, u32[]{:S(2)}) async-start(bf16[128,4,400]{0,2,1:T(8,128)(2,1)} %multiply_convert_fusion.12), calls=%async_computation.1 | async-start | bytes 819200 | tf_op jit(solution)/shard_map/all_to_all | solution.py:649
  286.9 20.8 %collective-permute-start.21 = (bf16[512,800]{0,1:T(8,128)(2,1)}, bf16[512,800]{0,1:T(8,128)(2,1)}, u32[]{:S(2)}, u32[]{:S(2)}) collective-permute-start(bf16[512,800]{0,1:T(8,128)(2,1)} %copy.343), channel_id=1, source_target_pairs={{0,2},{2,0},{1,3},{3,1},{4,6},{6,4},{5,7},{7,5},{8,10},{10,8},{9,1... | collective-permute-start | bytes 2457608 | tf_op jit(solution)/shard_map/ppermute | solution.py:359
  293.1 33.5 %collective-permute-start.29 = (bf16[1376,800]{0,1:T(8,128)(2,1)}, bf16[1376,800]{0,1:T(8,128)(2,1)}, u32[]{:S(2)}, u32[]{:S(2)}) collective-permute-start(bf16[1376,800]{0,1:T(8,128)(2,1)} %broadcast_select_fusion), channel_id=1, source_target_pairs={{0,1},{1,0},{2,3},{3,2},{4,5},{5,4},{6,7},{7,6},{8,9},{9,8},{10,11... | collective-permute-start | bytes 6604808 | tf_op jit(solution)/shard_map/ppermute | solution.py:359
  298.6 27.9 %collective-permute-start.28 = (bf16[512,800]{0,1:T(8,128)(2,1)}, bf16[512,800]{0,1:T(8,128)(2,1)}, u32[]{:S(2)}, u32[]{:S(2)}) collective-permute-start(bf16[512,800]{0,1:T(8,128)(2,1)} %copy.352), channel_id=1, source_target_pairs={{0,1},{1,0},{2,3},{3,2},{4,5},{5,4},{6,7},{7,6},{8,9},{9,8},{10,11... | collective-permute-start | bytes 2457608 | tf_op jit(solution)/shard_map/ppermute | solution.py:359
  321.2 27.8 %collective-permute-start.24 = (bf16[800,1376]{1,0:T(8,128)(2,1)}, bf16[800,1376]{1,0:T(8,128)(2,1)}, u32[]{:S(2)}, u32[]{:S(2)}) collective-permute-start(bf16[800,1376]{1,0:T(8,128)(2,1)} %broadcast_select_fusion.1), channel_id=1, source_target_pairs={{0,1},{1,0},{2,3},{3,2},{4,5},{5,4},{6,7},{7,6},{8,9},{9,8},{10,11... | collective-permute-start | bytes 6604808 | tf_op jit(solution)/shard_map/ppermute | solution.py:359
  326.5 26.0 %collective-permute-start.23 = (bf16[800,1376]{1,0:T(8,128)(2,1)}, bf16[800,1376]{1,0:T(8,128)(2,1)}, u32[]{:S(2)}, u32[]{:S(2)}) collective-permute-start(bf16[800,1376]{1,0:T(8,128)(2,1)} %broadcast_select_fusion.2), channel_id=1, source_target_pairs={{0,1},{1,0},{2,3},{3,2},{4,5},{5,4},{6,7},{7,6},{8,9},{9,8},{10,11... | collective-permute-start | bytes 6604808 | tf_op jit(solution)/shard_map/ppermute | solution.py:359
  372.3 109.8 %collective-permute-start.26 = (bf16[512,400]{1,0:T(8,128)(2,1)S(1)}, bf16[512,400]{1,0:T(8,128)(2,1)}, u32[]{:S(2)}, u32[]{:S(2)}) collective-permute-start(bf16[512,400]{1,0:T(8,128)(2,1)S(1)} %select_convert_fusion.1), channel_id=1, source_target_pairs={{0,2},{2,0},{1,3},{3,1},{4,6},{6,4},{5,7},{7,5},{8,10},{10,8},{9,1... | collective-permute-start | bytes 1228808 | tf_op jit(solution)/shard_map/ppermute | solution.py:359
  393.5 92.6 %collective-permute-start.32 = (bf16[512,800]{0,1:T(8,128)(2,1)}, bf16[512,800]{0,1:T(8,128)(2,1)}, u32[]{:S(2)}, u32[]{:S(2)}) collective-permute-start(bf16[512,800]{0,1:T(8,128)(2,1)} %copy.355), channel_id=1, source_target_pairs={{0,2},{2,0},{1,3},{3,1},{4,6},{6,4},{5,7},{7,5},{8,10},{10,8},{9,1... | collective-permute-start | bytes 2457608 | tf_op jit(solution)/shard_map/ppermute | solution.py:359
  426.6 68.9 %collective-permute-start.72 = (bf16[4,344,800]{1,2,0:T(8,128)(2,1)}, bf16[4,344,800]{1,2,0:T(8,128)(2,1)}, u32[]{:S(2)}, u32[]{:S(2)}) collective-permute-start(bf16[4,344,800]{1,2,0:T(8,128)(2,1)} %select_bitcast_fusion.1), channel_id=1, source_target_pairs={{0,4},{4,0},{8,12},{12,8},{16,20},{20,16},{24,28},{28,24},{1,5},{5... | collective-permute-start | bytes 6604808 | tf_op jit(solution)/shard_map/ppermute | solution.py:401
  461.7 74.0 %collective-permute-start.76 = (bf16[4,344,800]{1,2,0:T(8,128)(2,1)}, bf16[4,344,800]{1,2,0:T(8,128)(2,1)}, u32[]{:S(2)}, u32[]{:S(2)}) collective-permute-start(bf16[4,344,800]{1,2,0:T(8,128)(2,1)} %select_bitcast_fusion), channel_id=1, source_target_pairs={{0,4},{4,0},{8,12},{12,8},{16,20},{20,16},{24,28},{28,24},{1,5},{5... | collective-permute-start | bytes 6604808 | tf_op jit(solution)/shard_map/ppermute | solution.py:401
  476.9 106.3 %collective-permute-start.80 = (bf16[4,100,2752]{2,0,1:T(4,128)(2,1)}, bf16[4,100,2752]{2,0,1:T(4,128)(2,1)}, u32[]{:S(2)}, u32[]{:S(2)}) collective-permute-start(bf16[4,100,2752]{2,0,1:T(4,128)(2,1)} %copy.402), channel_id=1, source_target_pairs={{0,4},{4,0},{8,12},{12,8},{16,20},{20,16},{24,28},{28,24},{1,5},{5... | collective-permute-start | bytes 6604808 | tf_op jit(solution)/shard_map/ppermute | solution.py:401
  482.2 122.5 %collective-permute-start.44 = (bf16[800,800]{0,1:T(8,128)(2,1)}, bf16[800,800]{0,1:T(8,128)(2,1)}, u32[]{:S(2)}, u32[]{:S(2)}) collective-permute-start(bf16[800,800]{0,1:T(8,128)(2,1)} %broadcast_select_fusion.3), channel_id=1, source_target_pairs={{0,1},{1,0},{2,3},{3,2},{4,5},{5,4},{6,7},{7,6},{8,9},{9,8},{10,11... | collective-permute-start | bytes 3840008 | tf_op jit(solution)/shard_map/ppermute | solution.py:359
  486.1 137.2 %collective-permute-start.34 = (bf16[400,800]{1,0:T(8,128)(2,1)}, bf16[400,800]{1,0:T(8,128)(2,1)}, u32[]{:S(2)}, u32[]{:S(2)}) collective-permute-start(bf16[400,800]{1,0:T(8,128)(2,1)} %broadcast_select_fusion.28), channel_id=1, source_target_pairs={{0,1},{1,0},{2,3},{3,2},{4,5},{5,4},{6,7},{7,6},{8,9},{9,8},{10,11... | collective-permute-start | bytes 1920008 | tf_op jit(solution)/shard_map/ppermute | solution.py:359
  495.5 95.4 %collective-permute-start.33 = (f32[512,800]{0,1:T(8,128)}, f32[512,800]{0,1:T(8,128)S(1)}, u32[]{:S(2)}, u32[]{:S(2)}) collective-permute-start(f32[512,800]{0,1:T(8,128)} %copy.357), channel_id=1, source_target_pairs={{0,1},{1,0},{2,3},{3,2},{4,5},{5,4},{6,7},{7,6},{8,9},{9,8},{10,11... | collective-permute-start | bytes 4915208 | tf_op jit(solution)/shard_map/ppermute | solution.py:359
  535.7 109.6 %collective-permute-start.75 = (bf16[344,800]{0,1:T(8,128)(2,1)}, bf16[344,800]{0,1:T(8,128)(2,1)}, u32[]{:S(2)}, u32[]{:S(2)}) collective-permute-start(bf16[344,800]{0,1:T(8,128)(2,1)} %get-tuple-element.366), channel_id=1, source_target_pairs={{0,24},{4,28},{8,0},{12,4},{16,8},{20,12},{24,16},{28,20},{1,25},{... | collective-permute-start | bytes 1651208 | tf_op jit(solution)/shard_map/ppermute | solution.py:407
  583.2 88.2 %collective-permute-start.74 = (bf16[344,800]{0,1:T(8,128)(2,1)}, bf16[344,800]{0,1:T(8,128)(2,1)}, u32[]{:S(2)}, u32[]{:S(2)}) collective-permute-start(bf16[344,800]{0,1:T(8,128)(2,1)} %get-tuple-element.367), channel_id=1, source_target_pairs={{0,16},{4,20},{8,24},{12,28},{16,0},{20,4},{24,8},{28,12},{1,17},{... | collective-permute-start | bytes 1651208 | tf_op jit(solution)/shard_map/ppermute | solution.py:407
  592.0 79.4 %collective-permute-start.73 = (bf16[344,800]{0,1:T(8,128)(2,1)}, bf16[344,800]{0,1:T(8,128)(2,1)}, u32[]{:S(2)}, u32[]{:S(2)}) collective-permute-start(bf16[344,800]{0,1:T(8,128)(2,1)} %get-tuple-element.365), channel_id=1, source_target_pairs={{0,8},{4,12},{8,16},{12,20},{16,24},{20,28},{24,0},{28,4},{1,9},{5... | collective-permute-start | bytes 1651208 | tf_op jit(solution)/shard_map/ppermute | solution.py:407
  604.7 75.6 %collective-permute-start.83 = (bf16[100,2752]{1,0:T(8,128)(2,1)}, bf16[100,2752]{1,0:T(8,128)(2,1)}, u32[]{:S(2)}, u32[]{:S(2)}) collective-permute-start(bf16[100,2752]{1,0:T(8,128)(2,1)} %get-tuple-element.369), channel_id=1, source_target_pairs={{0,24},{4,28},{8,0},{12,4},{16,8},{20,12},{24,16},{28,20},{1,25},{... | collective-permute-start | bytes 1651208 | tf_op jit(solution)/shard_map/ppermute | solution.py:407
  623.3 57.0 %collective-permute-start.82 = (bf16[100,2752]{1,0:T(8,128)(2,1)}, bf16[100,2752]{1,0:T(8,128)(2,1)}, u32[]{:S(2)}, u32[]{:S(2)}) collective-permute-start(bf16[100,2752]{1,0:T(8,128)(2,1)} %get-tuple-element.370), channel_id=1, source_target_pairs={{0,16},{4,20},{8,24},{12,28},{16,0},{20,4},{24,8},{28,12},{1,17},{... | collective-permute-start | bytes 1651208 | tf_op jit(solution)/shard_map/ppermute | solution.py:407
  626.7 47.6 %all-to-all-start.3 = ((bf16[4,128,400]{1,2,0:T(8,128)(2,1)}), bf16[4,128,400]{1,2,0:T(8,128)(2,1)}, u32[]{:S(2)}, u32[]{:S(2)}) async-start(bf16[4,128,400]{1,2,0:T(8,128)(2,1)} %bitcast.558), calls=%async_computation.3 | async-start | bytes 819200 | tf_op jit(solution)/shard_map/all_to_all | solution.py:700
  645.3 35.0 %collective-permute-start.81 = (bf16[100,2752]{1,0:T(8,128)(2,1)}, bf16[100,2752]{1,0:T(8,128)(2,1)}, u32[]{:S(2)}, u32[]{:S(2)}) collective-permute-start(bf16[100,2752]{1,0:T(8,128)(2,1)} %get-tuple-element.368), channel_id=1, source_target_pairs={{0,8},{4,12},{8,16},{12,20},{16,24},{20,28},{24,0},{28,4},{1,9},{5... | collective-permute-start | bytes 1651208 | tf_op jit(solution)/shard_map/ppermute | solution.py:407
  680.2 503.5 %all-gather.3.cloned.1.call-start = ((), (), s32[]{:S(2)}) async-start(), calls=%async_computation.7 | async-start | bytes 1892352 | tf_op jit(solution)/shard_map/all_gather | solution.py:834
  801.3 55.0 %collective-permute-start.63 = (bf16[32,800]{1,0:T(8,128)(2,1)S(1)}, bf16[32,800]{1,0:T(8,128)(2,1)S(1)}, u32[]{:S(2)}, u32[]{:S(2)}) collective-permute-start(bf16[32,800]{1,0:T(8,128)(2,1)S(1)} %get-tuple-element.421), channel_id=1, source_target_pairs={{0,24},{4,28},{8,0},{12,4},{16,8},{20,12},{24,16},{28,20},{1,25},{... | collective-permute-start | bytes 153608 | tf_op jit(solution)/shard_map/ppermute | solution.py:407
  802.5 53.8 %collective-permute-start.62 = (bf16[32,800]{1,0:T(8,128)(2,1)S(1)}, bf16[32,800]{1,0:T(8,128)(2,1)S(1)}, u32[]{:S(2)}, u32[]{:S(2)}) collective-permute-start(bf16[32,800]{1,0:T(8,128)(2,1)S(1)} %get-tuple-element.422), channel_id=1, source_target_pairs={{0,16},{4,20},{8,24},{12,28},{16,0},{20,4},{24,8},{28,12},{1,17},{... | collective-permute-start | bytes 153608 | tf_op jit(solution)/shard_map/ppermute | solution.py:407
  803.6 52.6 %collective-permute-start.61 = (bf16[32,800]{1,0:T(8,128)(2,1)S(1)}, bf16[32,800]{1,0:T(8,128)(2,1)S(1)}, u32[]{:S(2)}, u32[]{:S(2)}) collective-permute-start(bf16[32,800]{1,0:T(8,128)(2,1)S(1)} %get-tuple-element.420), channel_id=1, source_target_pairs={{0,8},{4,12},{8,16},{12,20},{16,24},{20,28},{24,0},{28,4},{1,9},{5... | collective-permute-start | bytes 153608 | tf_op jit(solution)/shard_map/ppermute | solution.py:407
  877.2 36.0 %collective-permute-start.79 = (bf16[344,800]{0,1:T(8,128)(2,1)}, bf16[344,800]{0,1:T(8,128)(2,1)}, u32[]{:S(2)}, u32[]{:S(2)}) collective-permute-start(bf16[344,800]{0,1:T(8,128)(2,1)} %get-tuple-element.363), channel_id=1, source_target_pairs={{0,24},{4,28},{8,0},{12,4},{16,8},{20,12},{24,16},{28,20},{1,25},{... | collective-permute-start | bytes 1651208 | tf_op jit(solution)/shard_map/ppermute | solution.py:407
  885.1 73.7 %collective-permute-start.78 = (bf16[344,800]{0,1:T(8,128)(2,1)}, bf16[344,800]{0,1:T(8,128)(2,1)}, u32[]{:S(2)}, u32[]{:S(2)}) collective-permute-start(bf16[344,800]{0,1:T(8,128)(2,1)} %get-tuple-element.364), channel_id=1, source_target_pairs={{0,16},{4,20},{8,24},{12,28},{16,0},{20,4},{24,8},{28,12},{1,17},{... | collective-permute-start | bytes 1651208 | tf_op jit(solution)/shard_map/ppermute | solution.py:407
  885.2 73.7 %collective-permute-start.77 = (bf16[344,800]{0,1:T(8,128)(2,1)}, bf16[344,800]{0,1:T(8,128)(2,1)}, u32[]{:S(2)}, u32[]{:S(2)}) collective-permute-start(bf16[344,800]{0,1:T(8,128)(2,1)} %get-tuple-element.362), channel_id=1, source_target_pairs={{0,8},{4,12},{8,16},{12,20},{16,24},{20,28},{24,0},{28,4},{1,9},{5... | collective-permute-start | bytes 1651208 | tf_op jit(solution)/shard_map/ppermute | solution.py:407
  887.6 85.6 %collective-permute-start.68 = (bf16[4,100,1600]{2,0,1:T(4,128)(2,1)}, bf16[4,100,1600]{2,0,1:T(4,128)(2,1)}, u32[]{:S(2)}, u32[]{:S(2)}) collective-permute-start(bf16[4,100,1600]{2,0,1:T(4,128)(2,1)} %copy.396), channel_id=1, source_target_pairs={{0,4},{4,0},{8,12},{12,8},{16,20},{20,16},{24,28},{28,24},{1,5},{5... | collective-permute-start | bytes 3840008 | tf_op jit(solution)/shard_map/ppermute | solution.py:401
  889.2 81.9 %all-to-all-start.4 = ((bf16[128,4,560]{0,2,1:T(8,128)(2,1)}), bf16[128,4,560]{0,2,1:T(8,128)(2,1)}, u32[]{:S(2)}, u32[]{:S(2)}) async-start(bf16[128,4,560]{0,2,1:T(8,128)(2,1)} %bitcast.626), calls=%async_computation.4 | async-start | bytes 1146880 | tf_op jit(solution)/shard_map/all_to_all | solution.py:766
  900.1 371.1 %all-reduce.14.cloned.1.call-start = ((), (), s32[]{:S(2)}) async-start(), calls=%async_computation.6 | async-start | bytes 655360 | tf_op jit(solution)/shard_map/psum | solution.py:868
  906.3 58.2 %collective-permute-start.67 = (bf16[100,800]{1,0:T(8,128)(2,1)S(1)}, bf16[100,800]{1,0:T(8,128)(2,1)S(1)}, u32[]{:S(2)}, u32[]{:S(2)}) collective-permute-start(bf16[100,800]{1,0:T(8,128)(2,1)S(1)} %get-tuple-element.414), channel_id=1, source_target_pairs={{0,24},{4,28},{8,0},{12,4},{16,8},{20,12},{24,16},{28,20},{1,25},{... | collective-permute-start | bytes 480008 | tf_op jit(solution)/shard_map/ppermute | solution.py:407
  913.2 56.2 %collective-permute-start.66 = (bf16[100,800]{1,0:T(8,128)(2,1)S(1)}, bf16[100,800]{1,0:T(8,128)(2,1)S(1)}, u32[]{:S(2)}, u32[]{:S(2)}) collective-permute-start(bf16[100,800]{1,0:T(8,128)(2,1)S(1)} %get-tuple-element.415), channel_id=1, source_target_pairs={{0,16},{4,20},{8,24},{12,28},{16,0},{20,4},{24,8},{28,12},{1,17},{... | collective-permute-start | bytes 480008 | tf_op jit(solution)/shard_map/ppermute | solution.py:407
  1002.0 34.2 %collective-permute-start.52 = (bf16[4,140,800]{2,0,1:T(4,128)(2,1)}, bf16[4,140,800]{2,0,1:T(4,128)(2,1)}, u32[]{:S(2)}, u32[]{:S(2)}) collective-permute-start(bf16[4,140,800]{2,0,1:T(4,128)(2,1)} %copy.382), channel_id=1, source_target_pairs={{0,4},{4,0},{8,12},{12,8},{16,20},{20,16},{24,28},{28,24},{1,5},{5... | collective-permute-start | bytes 2688008 | tf_op jit(solution)/shard_map/ppermute | solution.py:401
  1003.2 30.9 %collective-permute-start.70 = (bf16[100,1600]{1,0:T(8,128)(2,1)}, bf16[100,1600]{1,0:T(8,128)(2,1)S(1)}, u32[]{:S(2)}, u32[]{:S(2)}) collective-permute-start(bf16[100,1600]{1,0:T(8,128)(2,1)} %get-tuple-element.395), channel_id=1, source_target_pairs={{0,16},{4,20},{8,24},{12,28},{16,0},{20,4},{24,8},{28,12},{1,17},{... | collective-permute-start | bytes 960008 | tf_op jit(solution)/shard_map/ppermute | solution.py:407
  1004.3 29.8 %collective-permute-start.69 = (bf16[100,1600]{1,0:T(8,128)(2,1)}, bf16[100,1600]{1,0:T(8,128)(2,1)}, u32[]{:S(2)}, u32[]{:S(2)}) collective-permute-start(bf16[100,1600]{1,0:T(8,128)(2,1)} %get-tuple-element.393), channel_id=1, source_target_pairs={{0,8},{4,12},{8,16},{12,20},{16,24},{20,28},{24,0},{28,4},{1,9},{5... | collective-permute-start | bytes 960008 | tf_op jit(solution)/shard_map/ppermute | solution.py:407
  1012.0 31.8 %collective-permute-start.49 = (bf16[512,800]{0,1:T(8,128)(2,1)}, bf16[512,800]{0,1:T(8,128)(2,1)}, u32[]{:S(2)}, u32[]{:S(2)}) collective-permute-start(bf16[512,800]{0,1:T(8,128)(2,1)} %copy.371), channel_id=1, source_target_pairs={{0,1},{1,0},{2,3},{3,2},{4,5},{5,4},{6,7},{7,6},{8,9},{9,8},{10,11... | collective-permute-start | bytes 2457608 | tf_op jit(solution)/shard_map/ppermute | solution.py:359
  1013.6 35.0 %collective-permute-start.50 = (bf16[512,800]{0,1:T(8,128)(2,1)}, bf16[512,800]{0,1:T(8,128)(2,1)}, u32[]{:S(2)}, u32[]{:S(2)}) collective-permute-start(bf16[512,800]{0,1:T(8,128)(2,1)} %copy.375), channel_id=1, source_target_pairs={{0,1},{1,0},{2,3},{3,2},{4,5},{5,4},{6,7},{7,6},{8,9},{9,8},{10,11... | collective-permute-start | bytes 2457608 | tf_op jit(solution)/shard_map/ppermute | solution.py:359
  1039.6 53.4 %collective-permute-start.55 = (bf16[140,800]{1,0:T(8,128)(2,1)}, bf16[140,800]{1,0:T(8,128)(2,1)}, u32[]{:S(2)}, u32[]{:S(2)}) collective-permute-start(bf16[140,800]{1,0:T(8,128)(2,1)} %get-tuple-element.403), channel_id=1, source_target_pairs={{0,24},{4,28},{8,0},{12,4},{16,8},{20,12},{24,16},{28,20},{1,25},{... | collective-permute-start | bytes 672008 | tf_op jit(solution)/shard_map/ppermute | solution.py:407
  1039.6 53.4 %collective-permute-start.54 = (bf16[140,800]{1,0:T(8,128)(2,1)}, bf16[140,800]{1,0:T(8,128)(2,1)}, u32[]{:S(2)}, u32[]{:S(2)}) collective-permute-start(bf16[140,800]{1,0:T(8,128)(2,1)} %get-tuple-element.404), channel_id=1, source_target_pairs={{0,16},{4,20},{8,24},{12,28},{16,0},{20,4},{24,8},{28,12},{1,17},{... | collective-permute-start | bytes 672008 | tf_op jit(solution)/shard_map/ppermute | solution.py:407
  1041.8 51.3 %collective-permute-start.53 = (bf16[140,800]{1,0:T(8,128)(2,1)}, bf16[140,800]{1,0:T(8,128)(2,1)}, u32[]{:S(2)}, u32[]{:S(2)}) collective-permute-start(bf16[140,800]{1,0:T(8,128)(2,1)} %get-tuple-element.402), channel_id=1, source_target_pairs={{0,8},{4,12},{8,16},{12,20},{16,24},{20,28},{24,0},{28,4},{1,9},{5... | collective-permute-start | bytes 672008 | tf_op jit(solution)/shard_map/ppermute | solution.py:407
  1086.3 115.8 %collective-permute-start.56 = (bf16[4,400,800]{2,1,0:T(8,128)(2,1)}, bf16[4,400,800]{2,1,0:T(8,128)(2,1)}, u32[]{:S(2)}, u32[]{:S(2)}) collective-permute-start(bf16[4,400,800]{2,1,0:T(8,128)(2,1)} %fusion.48), channel_id=1, source_target_pairs={{0,4},{4,0},{8,12},{12,8},{16,20},{20,16},{24,28},{28,24},{1,5},{5... | collective-permute-start | bytes 7680008 | tf_op jit(solution)/shard_map/ppermute | solution.py:401
  1208.6 61.0 %collective-permute-start.58 = (bf16[400,800]{1,0:T(8,128)(2,1)S(1)}, bf16[400,800]{1,0:T(8,128)(2,1)S(1)}, u32[]{:S(2)}, u32[]{:S(2)}) collective-permute-start(bf16[400,800]{1,0:T(8,128)(2,1)S(1)} %get-tuple-element.355), channel_id=1, source_target_pairs={{0,16},{4,20},{8,24},{12,28},{16,0},{20,4},{24,8},{28,12},{1,17},{... | collective-permute-start | bytes 1920008 | tf_op jit(solution)/shard_map/ppermute | solution.py:407
  1208.6 61.0 %collective-permute-start.57 = (bf16[400,800]{1,0:T(8,128)(2,1)S(1)}, bf16[400,800]{1,0:T(8,128)(2,1)S(1)}, u32[]{:S(2)}, u32[]{:S(2)}) collective-permute-start(bf16[400,800]{1,0:T(8,128)(2,1)S(1)} %get-tuple-element.353), channel_id=1, source_target_pairs={{0,8},{4,12},{8,16},{12,20},{16,24},{20,28},{24,0},{28,4},{1,9},{5... | collective-permute-start | bytes 1920008 | tf_op jit(solution)/shard_map/ppermute | solution.py:407
  (244 other events, 2801.7 us)
Sparse Core Ops, SparseCore 0:
  857.1 88.3 all-gather.2
  964.6 137.2 all-reduce.13

commit v2 on v1

v2 whole, which is shorter than its diff:
```python
import functools
import math

import jax
import jax.numpy as jnp
from jax import lax
from jax.experimental import pallas as pl
from jax.experimental.layout import Layout, with_layout_constraint
from jax.experimental.pallas import tpu as pltpu
from jax.sharding import PartitionSpec as P

D = 1600
H = 25
KVH = 5
HD = 64
DI = 3200
STATE = 16
DT_RANK = 100
CONV = 4
META = 128
WIN = 1024


EPS = 1e-05
NEG = -1e30
THETA = 10000.0
HIGH = lax.Precision.HIGHEST
ALL = ("seq", "row", "col")
GROUP = ("row", "col")
LOG2E = 1.4426950408889634
LN2 = 0.6931471805599453
FAR = 1e30
SUB = 8
LANE = 128
TAIL = CONV - 1
GATES = 2 * STATE
SELECTED = DT_RANK + GATES
VMEM_ASK = 58 * 2**20
SMALL = pl.CostEstimate(flops=1024, transcendentals=0, bytes_accessed=1024)


def nothing(*after, since=None):
    total = 0.0
    for values in after:
        start = (0,) * values.ndim
        if since is not None:
            start = (since,) + start[1:]
        corner = lax.dynamic_slice(values, start, (1,) * values.ndim)
        total = total + jnp.abs(corner.astype(jnp.float32).reshape(()))
    return jnp.minimum(jnp.float32(total), 0.0).astype(jnp.int32)


def exact(left_op, right_op, left_dim, right_dim):
    return lax.dot_general(
        left_op,
        right_op,
        (((left_dim,), (right_dim,)), ((), ())),
        precision=HIGH,
        preferred_element_type=jnp.float32,
    )


def gate_places():
    shape = (GATES, SELECTED)
    found = lax.broadcasted_iota(jnp.int32, shape, 1) - lax.broadcasted_iota(jnp.int32, shape, 0)
    return (found == DT_RANK).astype(jnp.float32)


def token_row(values):
    return exact(jnp.ones((SUB, LANE), jnp.float32), values, 1, 1)


def upright(ref):
    return ref[...].astype(jnp.float32).T


def spread_gates(source, length, *targets):

    def one(t, carry):
        rows = source[pl.ds(t, SUB, stride=length), :]
        for low, target in targets:
            for n in range(STATE):
                column = rows[:, low + n : low + n + 1]
                target[t * STATE + n] = jnp.broadcast_to(column, (SUB, LANE))
        return carry

    lax.fori_loop(0, length, one, 0)


def chunk_decay(rate_ref, total_row):
    return jnp.exp2(rate_ref[...] * total_row)


def convolved(inner_ref, tail_ref, age_ref, weight_ref, bias_ref, padded):
    total = inner_ref.shape[1]
    padded[0:SUB, :] = tail_ref[...]
    padded[SUB : SUB + total, :] = upright(inner_ref)
    result = jnp.broadcast_to(bias_ref[...], (total, LANE))
    for tap in range(CONV):
        found = padded[SUB - TAIL + tap : SUB - TAIL + tap + total, :]
        if tap < TAIL:
            found = jnp.where(age_ref[...] >= TAIL - tap, found, 0.0)
        result = result + weight_ref[tap : tap + 1, :] * found
    return result


def first_mixer(inner_ref, tail_ref, age_ref, weight_ref, bias_ref, select_ref, mixed_ref, picked_ref, padded):
    conv = convolved(inner_ref, tail_ref, age_ref, weight_ref, bias_ref, padded)
    mixed = conv * jax.nn.sigmoid(conv)
    mixed_ref[...] = mixed
    part = exact(mixed, select_ref[...], 1, 1)

    @pl.when(pl.program_id(0) == 0)
    def _():
        picked_ref[...] = part

    @pl.when(pl.program_id(0) > 0)
    def _():
        picked_ref[...] += part


def lapse_of(age_ref, rows, step):
    return jnp.where(age_ref[rows, :] > 0.0, step, FAR)


def scan_totals(
    picked_ref, mixed_ref, age_ref, weight_ref, bias_ref, rate_ref,
    step_ref, pre_ref, end_ref, part_ref, span_ref, gates, wide,
):
    length = mixed_ref.shape[0] // SUB

    @pl.when(pl.program_id(0) == 0)
    def _():
        gates[...] = exact(picked_ref[...], gate_places(), 1, 1)
        spread_gates(gates, length, (0, wide))

    pre = exact(picked_ref[...], weight_ref[...], 1, 0) + bias_ref[...]
    pre_ref[...] = pre
    step_ref[...] = jnp.maximum(pre, 0.0) + jnp.log1p(jnp.exp(-jnp.abs(pre)))
    rates = [jnp.broadcast_to(rate_ref[n : n + 1, :], (SUB, LANE)) for n in range(STATE)]

    def one(t, carry):
        states, span = carry
        rows = pl.ds(t, SUB, stride=length)
        step = step_ref[rows, :]
        lapse = lapse_of(age_ref, rows, step)
        push = step * mixed_ref[rows, :]
        states = tuple(
            jnp.exp2(lapse * rates[n]) * states[n] + push * wide[t * STATE + n] for n in range(STATE)
        )
        return (states, span + lapse)

    zero = jnp.zeros((SUB, LANE), jnp.float32)
    states, span = lax.fori_loop(0, length, one, ((zero,) * STATE, zero), unroll=2)
    for n in range(STATE):
        part_ref[0, n] = states[n]
    span_ref[...] = span
    total = jnp.zeros((STATE, LANE), jnp.float32)
    lapsed = jnp.zeros((1, LANE), jnp.float32)
    for k in range(SUB):
        here = span_ref[k : k + 1, :]
        total = chunk_decay(rate_ref, here) * total + part_ref[0, :, k, :]
        lapsed = lapsed + here
    end_ref[0:STATE, :] = total
    end_ref[STATE:, :] = jnp.broadcast_to(lapsed, (SUB, LANE))


def scan_outputs(
    step_ref, mixed_ref, age_ref, picked_ref, rate_ref, part_ref, span_ref, start_ref, skip_ref, z_ref,
    mixed_out_ref, value_ref, square_ref, kept_ref, gates, wide, wide_read, squares,
):
    length = mixed_ref.shape[0] // SUB

    @pl.when(pl.program_id(0) == 0)
    def _():
        gates[...] = exact(picked_ref[...], gate_places(), 1, 1)
        spread_gates(gates, length, (0, wide), (STATE, wide_read))
        squares[...] = jnp.zeros_like(squares)

    state = start_ref[...]
    for k in range(SUB):
        kept_ref[0, 0:STATE, k, :] = state
        state = chunk_decay(rate_ref, span_ref[k : k + 1, :]) * state + part_ref[0, :, k, :]
    rates = [jnp.broadcast_to(rate_ref[n : n + 1, :], (SUB, LANE)) for n in range(STATE)]

    def one(t, states):
        rows = pl.ds(t, SUB, stride=length)
        step = step_ref[rows, :]
        lapse = lapse_of(age_ref, rows, step)
        push = step * mixed_ref[rows, :]
        new = []
        seen = [None, None]
        for n in range(STATE):
            value = jnp.exp2(lapse * rates[n]) * states[n] + push * wide[t * STATE + n]
            kept_ref[0, (t + 1) * STATE + n] = value
            part = value * wide_read[t * STATE + n]
            seen[n % 2] = part if seen[n % 2] is None else seen[n % 2] + part
            new.append(value)
        mixed_out_ref[rows, :] = seen[0] + seen[1]
        return tuple(new)

    lax.fori_loop(0, length, one, tuple(kept_ref[0, n] for n in range(STATE)), unroll=2)
    mixed_out = mixed_out_ref[...] + skip_ref[...] * mixed_ref[...]
    mixed_out_ref[...] = mixed_out
    z = upright(z_ref)
    value = mixed_out * z * jax.nn.sigmoid(z)
    value_ref[...] = value
    squares[...] += value * value

    @pl.when(pl.program_id(0) == pl.num_programs(0) - 1)
    def _():
        square_ref[...] = token_row(squares[...])


def normed(value_ref, factor_ref, gain_ref, out_ref):
    out_ref[...] = (value_ref[...].T * factor_ref[0:1, :] * gain_ref[...]).astype(out_ref.dtype)


def norm_pull(value_ref, grad_ref, gain_ref, sum_ref, sums):
    part = upright(grad_ref) * gain_ref[...] * value_ref[...]

    @pl.when(pl.program_id(0) == 0)
    def _():
        sums[...] = part

    @pl.when(pl.program_id(0) > 0)
    def _():
        sums[...] += part

    @pl.when(pl.program_id(0) == pl.num_programs(0) - 1)
    def _():
        sum_ref[...] = token_row(sums[...])


def adjoint_totals(
    value_ref, grad_ref, gain_ref, stats_ref, z_ref, mixed_out_ref, mixed_ref,
    step_ref, age_ref, picked_ref, rate_ref, span_ref,
    dmixed_ref, dz_ref, side_ref, end_ref, part_ref, gates, wide, factors, pulls,
):
    total = mixed_ref.shape[0]
    length = total // SUB

    @pl.when(pl.program_id(0) == 0)
    def _():
        gates[...] = exact(picked_ref[...], gate_places(), 1, 1)
        spread_gates(gates, length, (STATE, wide))
        columns = stats_ref[...].T
        factors[...] = jnp.broadcast_to(columns[:, 0:1], (total, LANE))
        pulls[...] = jnp.broadcast_to(columns[:, 1:2], (total, LANE))

    grad, z, value = upright(grad_ref), upright(z_ref), value_ref[...]
    dvalue = factors[...] * gain_ref[...] * grad - value * pulls[...]
    sig = jax.nn.sigmoid(z)
    dmixed = dvalue * z * sig
    dmixed_ref[...] = dmixed
    dz = dvalue * mixed_out_ref[...] * sig * (1.0 + z * (1.0 - sig))
    dz_ref[...] = dz.T.astype(dz_ref.dtype)
    side_ref[...] = jnp.zeros_like(side_ref)
    side_ref[0:1, :] = jnp.sum(dmixed * mixed_ref[...], axis=0, keepdims=True)
    side_ref[1:2, :] = jnp.sum(grad * value * factors[...], axis=0, keepdims=True)
    rates = [jnp.broadcast_to(rate_ref[n : n + 1, :], (SUB, LANE)) for n in range(STATE)]

    def one(k, carry):
        t = length - 1 - k
        rows = pl.ds(t, SUB, stride=length)
        lapse = lapse_of(age_ref, rows, step_ref[rows, :])
        dout = dmixed_ref[rows, :]
        return tuple(
            jnp.exp2(lapse * rates[n]) * (carry[n] + dout * wide[t * STATE + n]) for n in range(STATE)
        )

    zero = jnp.zeros((SUB, LANE), jnp.float32)
    carry = lax.fori_loop(0, length, one, (zero,) * STATE, unroll=2)
    for n in range(STATE):
        part_ref[0, n] = carry[n]
    ends = jnp.zeros((STATE, LANE), jnp.float32)
    for k in reversed(range(SUB)):
        ends = chunk_decay(rate_ref, span_ref[k : k + 1, :]) * ends + part_ref[0, :, k, :]
    end_ref[...] = ends


def adjoint_grads(
    step_ref, mixed_ref, age_ref, dout_ref, picked_ref, rate_ref, part_ref, span_ref, start_ref, kept_ref,
    pre_ref, weight_ref, skip_ref,
    direct_ref, side_ref, drate_ref, dweight_ref, dpicked_ref,
    gates, wide, wide_read, entry, dgate_ref, dread_ref, dprod_ref, dstep_ref,
):
    length = mixed_ref.shape[0] // SUB

    @pl.when(pl.program_id(0) == 0)
    def _():
        gates[...] = exact(picked_ref[...], gate_places(), 1, 1)
        spread_gates(gates, length, (0, wide), (STATE, wide_read))
        dgate_ref[...] = jnp.zeros_like(dgate_ref)
        dread_ref[...] = jnp.zeros_like(dread_ref)

    state = start_ref[...]
    for k in reversed(range(SUB)):
        entry[:, k, :] = state
        state = chunk_decay(rate_ref, span_ref[k : k + 1, :]) * state + part_ref[0, :, k, :]
    half = STATE // 2
    zero = jnp.zeros((SUB, LANE), jnp.float32)
    for low in (0, half):
        rates = [jnp.broadcast_to(rate_ref[n : n + 1, :], (SUB, LANE)) for n in range(low, low + half)]

        def one(j, carry, low=low, rates=rates):
            incoming, rate_sum = carry
            t = length - 1 - j
            rows = pl.ds(t, SUB, stride=length)
            step = step_ref[rows, :]
            lapse = lapse_of(age_ref, rows, step)
            push = step * mixed_ref[rows, :]
            dout = dout_ref[rows, :]
            outgoing, sums = [], []
            dprod, dstep = zero, zero
            for i in range(half):
                at = t * STATE + low + i
                adjoint = incoming[i] + dout * wide_read[at]
                dread_ref[at] = dread_ref[at] + kept_ref[0, at + STATE] * dout
                dgate_ref[at] = dgate_ref[at] + adjoint * push
                dprod = dprod + adjoint * wide[at]
                passed = jnp.exp2(lapse * rates[i]) * adjoint
                pull = passed * kept_ref[0, at]
                dstep = dstep + pull * rates[i]
                sums.append(rate_sum[i] + pull * step)
                outgoing.append(passed)
            if low == 0:
                dprod_ref[rows, :] = dprod
                dstep_ref[rows, :] = dstep
            else:
                dprod_ref[rows, :] = dprod_ref[rows, :] + dprod
                dstep_ref[rows, :] = (dstep_ref[rows, :] + dstep) * LN2
            return (tuple(outgoing), tuple(sums))

        start = (tuple(entry[low + i] for i in range(half)), (zero,) * half)
        _, rate_sum = lax.fori_loop(0, length, one, start)
        for i in range(half):
            found = jnp.sum(rate_sum[i], axis=0, keepdims=True)
            drate_ref[low + i : low + i + 1, :] = found * rate_ref[low + i : low + i + 1, :] * LN2

    dprod = dprod_ref[...]
    direct_ref[...] = dout_ref[...] * skip_ref[...] + dprod * step_ref[...]
    dpre = (dstep_ref[...] + dprod * mixed_ref[...]) * jax.nn.sigmoid(pre_ref[...])
    side_ref[...] = jnp.broadcast_to(jnp.sum(dpre, axis=0, keepdims=True), (SUB, LANE))
    dweight_ref[...] = exact(picked_ref[...], dpre, 0, 0)
    part = exact(dpre, weight_ref[...], 1, 1)

    @pl.when(pl.program_id(0) == 0)
    def _():
        dpicked_ref[...] = part

    @pl.when(pl.program_id(0) > 0)
    def _():
        dpicked_ref[...] += part

    @pl.when(pl.program_id(0) == pl.num_programs(0) - 1)
    def _():
        place = lax.broadcasted_iota(jnp.int32, (SUB, GATES), 1)

        def gather(t, carry):
            found = jnp.zeros((SUB, GATES), jnp.float32)
            for base, source in ((0, dgate_ref), (STATE, dread_ref)):
                for n in range(STATE):
                    summed = jnp.sum(source[t * STATE + n], axis=1, keepdims=True)
                    found = jnp.where(place == base + n, summed, found)
            gates[pl.ds(t, SUB, stride=length), :] = found
            return carry

        lax.fori_loop(0, length, gather, 0)
        dpicked_ref[...] += exact(gates[...], gate_places(), 1, 0)


def last_mixer(
    inner_ref, tail_ref, age_ref, weight_ref, bias_ref, select_ref, dpicked_ref, direct_ref, mixed_ref,
    dinner_ref, edge_ref, side_ref, dselect_ref, padded, spilled,
):
    total = mixed_ref.shape[0]
    conv = convolved(inner_ref, tail_ref, age_ref, weight_ref, bias_ref, padded)
    sig = jax.nn.sigmoid(conv)
    dmixed = direct_ref[...] + exact(dpicked_ref[...], select_ref[...], 1, 0)
    dconv = dmixed * sig * (1.0 + conv * (1.0 - sig))
    dselect_ref[...] = exact(dpicked_ref[...], mixed_ref[...], 0, 0)
    side_ref[...] = jnp.zeros_like(side_ref)
    side_ref[CONV : CONV + 1, :] = jnp.sum(dconv, axis=0, keepdims=True)
    spilled[...] = jnp.zeros_like(spilled)
    for tap in range(CONV):
        at = slice(SUB - TAIL + tap, SUB - TAIL + tap + total)
        masked = dconv
        if tap < TAIL:
            masked = jnp.where(age_ref[...] >= TAIL - tap, dconv, 0.0)
        side_ref[tap : tap + 1, :] = jnp.sum(masked * padded[at, :], axis=0, keepdims=True)
        spilled[at, :] += masked * weight_ref[tap : tap + 1, :]
    edge_ref[0:SUB, :] = spilled[0:SUB, :]
    edge_ref[SUB:, :] = spilled[total : total + SUB, :]
    dinner_ref[...] = spilled[SUB:, :].T.astype(dinner_ref.dtype)


def column(rows):
    return pl.BlockSpec((rows, LANE), lambda i: (0, i))


def banded(rows, width):
    return pl.BlockSpec((rows, width), lambda i: (i, 0))


def shared(shape):
    return pl.BlockSpec(shape, lambda i: (0,) * len(shape))


def tile_of(shape):
    return pl.BlockSpec((1,) + shape, lambda i: (i,) + (0,) * len(shape))


def run_tiles(body, steps, ins, outs, scratch=(), after=()):
    args = [value for value, _ in ins]
    specs = [spec for _, spec in ins]
    args = args + list(after)
    specs = specs + [pl.BlockSpec(memory_space=pl.ANY)] * len(after)

    def kernel(*refs):
        body(*refs[: len(ins)], *refs[len(args) :])

    return pl.pallas_call(
        kernel,
        grid=(steps,),
        in_specs=specs,
        out_specs=[spec for _, _, spec in outs],
        out_shape=[jax.ShapeDtypeStruct(shape, dtype) for shape, dtype, _ in outs],
        scratch_shapes=[pltpu.VMEM(shape, jnp.float32) for shape in scratch],
        compiler_params=pltpu.CompilerParams(
            dimension_semantics=("arbitrary",), vmem_limit_bytes=VMEM_ASK
        ),
        cost_estimate=SMALL,
    )(*args)


def handed_on(source_ref, target_ref):
    target_ref[...] = source_ref[...]


def held_until(values, after):
    whole = shared(values.shape)
    return run_tiles(handed_on, 1, [(values, whole)], [(values.shape, values.dtype, whole)], (), after)[0]


class Mixer:

    def __init__(self, tokens, width, age, inner, tail, z, conv_w, conv_b, select_w, step_w, step_b, rates, skip, gain):
        self.tokens, self.width, self.tiles = tokens, width, width // LANE
        self.long = column(tokens)
        self.tall = banded(LANE, tokens)
        self.row = column(1)
        picked = shared((tokens, SELECTED))
        self.picked_spec = picked
        self.age = (age, shared((tokens, LANE)))
        self.conv = [
            (inner, self.tall), (tail, column(SUB)), self.age, (conv_w, column(CONV)), (conv_b, self.row),
            (select_w, column(SELECTED)),
        ]
        self.z = (z, self.tall)
        self.step_w = (step_w, column(SELECTED))
        self.step_b = (step_b, self.row)
        self.rates = (rates, column(STATE))
        self.skip, self.gain = (skip, self.row), (gain, self.row)
        self.wide = (tokens // SUB * STATE, SUB, LANE)
        self.states = (STATE, SUB, LANE)
        self.buffer = (tokens + SUB, LANE)

    def f32(self, rows, spec=None):
        return ((rows, self.width), jnp.float32, spec or column(rows))

    def low_out(self):
        return ((self.width, self.tokens), jnp.bfloat16, self.tall)

    def row_out(self):
        return ((SUB, self.tokens), jnp.float32, shared((SUB, self.tokens)))

    def picked_out(self):
        return ((self.tokens, SELECTED), jnp.float32, self.picked_spec)

    def states_out(self):
        return ((self.tiles,) + self.states, jnp.float32, tile_of(self.states))

    def run(self, body, ins, outs, scratch=(), after=()):
        return run_tiles(body, self.tiles, ins, outs, scratch, after)

    def first(self):
        mixed, picked = self.run(first_mixer, self.conv, [self.f32(self.tokens), self.picked_out()], [self.buffer])
        self.mixed = (mixed, self.long)
        return mixed, picked

    def totals(self, picked, after):
        self.picked = (picked, self.picked_spec)
        step, pre, end, part, span = self.run(
            scan_totals,
            [self.picked, self.mixed, self.age, self.step_w, self.step_b, self.rates],
            [self.f32(self.tokens)] * 2 + [self.f32(STATE + SUB), self.states_out(), self.f32(SUB)],
            [(self.tokens, GATES), self.wide],
            after,
        )
        self.step, self.pre = (step, self.long), (pre, self.long)
        self.part, self.span = (part, tile_of(self.states)), (span, column(SUB))
        return end

    def outputs(self, state_in, after):
        kept_shape = (self.wide[0] + STATE, SUB, LANE)
        mixed_out, value, squares, kept = self.run(
            scan_outputs,
            [self.step, self.mixed, self.age, self.picked, self.rates, self.part, self.span,
             (state_in, column(STATE)), self.skip, self.z],
            [self.f32(self.tokens)] * 2 + [self.row_out(),
             ((self.tiles,) + kept_shape, jnp.float32, tile_of(kept_shape))],
            [(self.tokens, GATES), self.wide, self.wide, (self.tokens, LANE)],
            after,
        )
        self.mixed_out, self.value = (mixed_out, self.long), (value, self.long)
        self.kept = (kept, tile_of(kept_shape))
        return squares[0]

    def normed(self, factor, gain):
        factor = jnp.broadcast_to(factor[None, :], (SUB, self.tokens))
        return self.run(
            normed,
            [self.value, (factor, shared((SUB, self.tokens))), (gain[:, None], banded(LANE, 1))],
            [self.low_out()],
        )[0]

    def norm_pull(self, grad):
        self.grad = (grad, self.tall)
        return self.run(
            norm_pull, [self.value, self.grad, self.gain], [self.row_out()], [(self.tokens, LANE)]
        )[0][0]

    def back_totals(self, factor, pull, after):
        stats = jnp.concatenate(
            [factor[None], pull[None], jnp.zeros((SUB - 2, self.tokens), jnp.float32)], axis=0
        )
        dmixed, dz, side, end, part = self.run(
            adjoint_totals,
            [self.value, self.grad, self.gain, (stats, shared((SUB, self.tokens))), self.z,
             self.mixed_out, self.mixed, self.step, self.age, self.picked, self.rates, self.span],
            [self.f32(self.tokens), self.low_out(), self.f32(SUB), self.f32(STATE), self.states_out()],
            [(self.tokens, GATES), self.wide, (self.tokens, LANE), (self.tokens, LANE)],
            after,
        )
        self.dmixed, self.back_part = (dmixed, self.long), (part, tile_of(self.states))
        return end, dz, side

    def back_grads(self, adjoint_in, after):
        direct, side, drates, dweight, dpicked = self.run(
            adjoint_grads,
            [self.step, self.mixed, self.age, self.dmixed, self.picked, self.rates, self.back_part, self.span,
             (adjoint_in, column(STATE)), self.kept, self.pre, self.step_w, self.skip],
            [self.f32(self.tokens), self.f32(SUB), self.f32(STATE), self.f32(SELECTED), self.picked_out()],
            [(self.tokens, GATES), self.wide, self.wide, self.states, self.wide, self.wide,
             (self.tokens, LANE), (self.tokens, LANE)],
            after,
        )
        self.direct = (direct, self.long)
        return side, drates, dweight, dpicked

    def last(self, dpicked, after):
        return self.run(
            last_mixer,
            self.conv + [(dpicked, self.picked_spec), self.direct, self.mixed],
            [self.low_out(), self.f32(2 * SUB), self.f32(SUB), self.f32(SELECTED)],
            [self.buffer, self.buffer],
            after,
        )


def over_rows(left_op, right_op):
    return lax.dot_general(
        left_op, right_op, (((0,), (0,)), ((), ())), preferred_element_type=jnp.float32
    )


def over_lanes(left_op, right_op):
    return lax.dot_general(
        left_op, right_op, (((1,), (1,)), ((), ())), preferred_element_type=jnp.float32
    )


def attend(repeats, query_ref, key_ref, value_ref, mask_ref, out_ref, total_ref):
    keys, values = key_ref[...], value_ref[...]
    for h in range(repeats):
        rows = slice(h * HD, (h + 1) * HD)
        scores = over_rows(keys, query_ref[rows, :]) + mask_ref[...]
        highest = jnp.max(scores, axis=0, keepdims=True)
        weights = jnp.exp(scores - highest)
        total = jnp.sum(weights, axis=0, keepdims=True)
        mixed = jnp.dot(values, weights.astype(jnp.bfloat16), preferred_element_type=jnp.float32)
        out_ref[rows, :] = mixed / total
        total_ref[0, h : h + 1, :] = highest + jnp.log(total)


def attend_back(
    repeats, query_ref, key_ref, value_ref, mask_ref, dout_ref, total_ref, delta_ref, place_ref,
    dquery_ref, dkey_ref, dvalue_ref,
):
    keys, values = key_ref[...], value_ref[...]
    reach = keys.shape[1] - META
    moved_to = pl.ds(pl.multiple_of(META + place_ref[0], LANE), reach)
    dkey_sum, dvalue_sum = 0.0, 0.0
    for h in range(repeats):
        rows = slice(h * HD, (h + 1) * HD)
        query, dout = query_ref[rows, :], dout_ref[rows, :]
        scores = over_rows(keys, query) + mask_ref[...]
        probs = jnp.exp(scores - total_ref[0, h : h + 1, :])
        dprobs = over_rows(values, dout)
        dscores = (probs * (dprobs - delta_ref[0, h : h + 1, :])).astype(jnp.bfloat16)
        probs = probs.astype(jnp.bfloat16)
        dquery_ref[rows, :] = jnp.dot(keys, dscores, preferred_element_type=jnp.float32)
        dkey_sum = dkey_sum + over_lanes(query, dscores)
        dvalue_sum = dvalue_sum + over_lanes(dout, probs)
    for target, found in ((dkey_ref, dkey_sum), (dvalue_ref, dvalue_sum)):
        target[...] = jnp.zeros_like(target)
        target[:, 0:META] = found[:, 0:META]
        target[:, moved_to] = found[:, META:]


def run_attention(query, keys, values, mask, after):
    count, reach = query.shape[1], keys.shape[1]
    tall = banded(HD * (H // KVH), count)
    stats = tile_of((SUB, count))
    keyed = banded(HD, reach)
    return run_tiles(
        functools.partial(attend, H // KVH),
        KVH,
        [(query, tall), (keys, keyed), (values, keyed), (mask, shared((reach, count)))],
        [(query.shape, jnp.float32, tall), ((KVH, SUB, count), jnp.float32, stats)],
        (),
        after,
    )


def run_attention_back(query, keys, values, mask, dout, totals, delta, place, spread, after):
    count, reach = query.shape[1], keys.shape[1]
    tall = banded(HD * (H // KVH), count)
    stats = tile_of((SUB, count))
    keyed = banded(HD, reach)
    found = ((keys.shape[0], spread), jnp.float32, banded(HD, spread))
    return run_tiles(
        functools.partial(attend_back, H // KVH),
        KVH,
        [
            (query, tall), (keys, keyed), (values, keyed), (mask, shared((reach, count))), (dout, tall),
            (totals, stats), (delta, stats), (place, pl.BlockSpec(memory_space=pltpu.SMEM)),
        ],
        [(query.shape, jnp.float32, tall), found, found],
        (),
        after,
    )


def dot_plain(left_op, right_op):
    return jnp.dot(left_op, right_op, preferred_element_type=jnp.float32)


def dot_left(left_op, right_op):
    return lax.dot_general(
        left_op, right_op, (((0,), (0,)), ((), ())), preferred_element_type=jnp.float32
    )


def dot_right(left_op, right_op):
    return lax.dot_general(
        left_op, right_op, (((1,), (1,)), ((), ())), preferred_element_type=jnp.float32
    )


def exact_dot(left_op, right_op):
    return jnp.dot(left_op, right_op, precision=HIGH, preferred_element_type=jnp.float32)


def exact_left(left_op, right_op):
    return lax.dot_general(
        left_op,
        right_op,
        (((0,), (0,)), ((), ())),
        precision=HIGH,
        preferred_element_type=jnp.float32,
    )


def exact_right(left_op, right_op):
    return lax.dot_general(
        left_op,
        right_op,
        (((1,), (1,)), ((), ())),
        precision=HIGH,
        preferred_element_type=jnp.float32,
    )


def low(values):
    return values.astype(jnp.bfloat16)


def wide(values):
    return values.astype(jnp.float32)


def swapped(values, axis):
    return straight(lax.ppermute(straight(values), axis, [(0, 1), (1, 0)]))


def moved(values, axis, distance):
    count = lax.axis_size(axis)
    route = [(i, i + distance) for i in range(count) if 0 <= i + distance < count]
    return lax.ppermute(values, axis, route)


def joined(mine, other, place):
    which = lax.broadcasted_iota(jnp.int32, (2,) + (1,) * mine.ndim, 0)
    both = jnp.where(which == place, mine[None], other[None])
    return both.reshape((2 * mine.shape[0],) + mine.shape[1:])


def chosen(pieces, place):
    result = pieces[0]
    for index, piece in enumerate(pieces[1:], 1):
        result = jnp.where(place == index, piece, result)
    return result


def pieces_of(values, count, axis):
    size = values.shape[axis] // count
    return [lax.slice_in_dim(values, i * size, (i + 1) * size, axis=axis) for i in range(count)]


def group_total(values):
    over_cols = values + swapped(values, "col")
    return over_cols + swapped(over_cols, "row")


def straight(values):
    return with_layout_constraint(values, Layout(tuple(range(values.ndim))))


def kept_apart(values, place, size, axis=0):
    mine = lax.dynamic_slice_in_dim(values, place * size, size, axis=axis)
    away = lax.dynamic_slice_in_dim(values, (1 - place) * size, size, axis=axis)
    return mine, away


class SeqSum:

    def __init__(self, left, right, scale=1.0, flip=False, after=()):
        self.count, self.place = lax.axis_size("seq"), lax.axis_index("seq")
        self.bits = self.count.bit_length() - 1
        self.right, self.scale, self.flip = right, scale, flip
        self.rows = left.shape[0] // self.count
        left = left.reshape((self.count, self.rows) + left.shape[1:])
        left = jnp.pad(left, ((0, 0), (0, -self.rows % 8), (0, 0)))
        self.left = left.reshape((2,) * self.bits + left.shape[1:])
        self.stage = 0
        self.send(low(self.product(self.half(self.left, True, after))))

    def half(self, values, away, after=()):
        bit = (self.place // 2**self.stage) % 2
        which = (1 - bit if away else bit) + nothing(*after)
        return lax.dynamic_index_in_dim(
            values, which, self.bits - 1 - self.stage, keepdims=False
        )

    def product(self, left):
        operands = (self.right, left) if self.flip else (left, self.right)
        dims = ((operands[0].ndim - 1,), (operands[1].ndim - 1,))
        found = lax.dot_general(
            *operands, (dims, ((), ())), preferred_element_type=jnp.float32
        )
        return self.scale * (jnp.moveaxis(found, 0, -2) if self.flip else found)

    def send(self, values):
        self.sent = straight(values)
        route = [(i, i ^ 2**self.stage) for i in range(self.count)]
        self.got = straight(lax.ppermute(self.sent, "seq", route))

    def step(self, *after):
        if self.stage == 0:
            mine = self.product(self.half(self.left, False, after))
        else:
            mine = wide(self.half(self.now, False, after))
        total = mine + wide(self.got)
        self.stage += 1
        if self.stage == self.bits:
            self.total = total
        else:
            self.now = straight(low(total))
            self.send(self.half(self.now, True))
        return self

    def finish(self, *after):
        while self.stage < self.bits:
            self.step(*after)
        rows = self.rows
        return self.total[:, :rows] if self.flip else self.total[:rows]


def seq_reduce(values):
    count, place = lax.axis_size("seq"), lax.axis_index("seq")
    bits = count.bit_length() - 1
    parts = values.reshape((2,) * bits + (values.shape[0] // count,) + values.shape[1:])
    for stage in range(bits):
        bit = (place // 2**stage) % 2
        axis = bits - 1 - stage
        mine = lax.dynamic_index_in_dim(parts, bit, axis, keepdims=False)
        away = lax.dynamic_index_in_dim(parts, 1 - bit, axis, keepdims=False)
        route = [(i, i ^ 2**stage) for i in range(count)]
        parts = mine + wide(lax.ppermute(low(away), "seq", route))
    return parts


def told(values, axes):
    count = lax.axis_size(axes)
    return lax.all_to_all(
        jnp.broadcast_to(values[None], (count,) + values.shape), axes, split_axis=0, concat_axis=0
    )


def all_total(values):
    count = lax.axis_size(ALL)
    shares = lax.all_to_all(values.reshape(count, -1), ALL, split_axis=0, concat_axis=0, tiled=True)
    return told(jnp.sum(shares, axis=0), ALL).reshape(-1)


def turned(values, cosine, sine, back):
    heads = values.reshape((values.shape[0] // HD, 2, HD // 2) + values.shape[1:])
    first, second = heads[:, :1], heads[:, 1:]
    sine = -sine if back else sine
    turned_pair = [first * cosine - second * sine, second * cosine + first * sine]
    return jnp.concatenate(turned_pair, axis=1).reshape(values.shape)


def entering_state(ends, spans, rates, reverse):
    count, place = lax.axis_size("seq"), lax.axis_index("seq")
    state = jnp.zeros_like(ends[0])
    for k in range(count):
        at = count - 1 - k if reverse else k
        reached = at > place if reverse else at < place
        decay = jnp.exp2(rates * spans[at][None, :])
        state = jnp.where(reached, decay * state + ends[at], state)
    return state


def shards(
    hidden_in,
    grad_out,
    segment_ids,
    pre_gain,
    qkv_weight,
    mixer_in_weight,
    meta_cache,
    conv_weight,
    conv_bias,
    select_weight,
    step_weight,
    step_bias,
    log_rates,
    skip_gain,
    attn_gain,
    mixer_gain,
    attn_out_weight,
    mixer_out_weight,
    post_gain,
    gate_weight,
    up_weight,
    down_weight,
):
    row, col, seq = lax.axis_index("row"), lax.axis_index("col"), lax.axis_index("seq")
    tokens = hidden_in.shape[0]
    quarter = DI // 4
    half = D // 2
    lanes = -(-quarter // LANE) * LANE
    member = 2 * row + col

    def by_row(first, second):
        return jnp.where(row == 0, first, second)

    def row_joined(values):
        return joined(values, swapped(values, "row"), row)

    def col_joined(values):
        return joined(values, swapped(values, "col"), col)

    def col_summed(part):
        mine, away = kept_apart(part, col, part.shape[0] // 2)
        return mine + wide(swapped(low(away), "col"))

    def row_summed(part):
        part = low(part)
        return wide(part) + wide(swapped(part, "row"))

    def row_scattered(part):
        mine, away = kept_apart(part, row, part.shape[0] // 2)
        return mine + wide(swapped(low(away), "row"))

    def over_cols(values):
        return values + swapped(values, "col")

    hidden_m = row_joined(hidden_in.T)
    gains_m = row_joined(jnp.stack([pre_gain, post_gain], axis=1))
    pre_g, post_g = gains_m[:, :1], gains_m[:, 1:]
    hm = wide(hidden_m)
    pre_factor = lax.rsqrt(over_cols(jnp.sum(hm * hm, axis=0)) / D + EPS)[None, :]
    first_m = low(hm * pre_factor * pre_g)

    inner_part = straight(over_rows(mixer_in_weight, first_m))
    near, far = inner_part[: 2 * quarter], inner_part[2 * quarter :]
    near_m, near_away = kept_apart(near, col, quarter)
    far_m, far_away = kept_apart(far, col, quarter)
    give_m, keep_m = by_row(far_m, near_m), by_row(near_m, far_m)
    give_got = swapped(low(by_row(far_away, near_away)), "col")
    keep_got = swapped(low(by_row(near_away, far_away)), "col")
    given = low(give_m + wide(give_got))
    taken = swapped(given, "row")
    kept_in = low(keep_m + wide(keep_got))
    qkv_part = low(col_summed(over_rows(qkv_weight, first_m)))
    qkv_core = lax.all_to_all(qkv_part, GROUP, split_axis=1, concat_axis=0, tiled=True)
    def filled(values):
        return jnp.pad(values, ((0, lanes - quarter), (0, 0)))

    def channels(values, axis):
        part = chosen(pieces_of(values, 4, axis), member)
        sides = [(0, lanes - quarter) if i == axis else (0, 0) for i in range(values.ndim)]
        return jnp.pad(part, sides)

    inner_own = filled(by_row(kept_in, taken))
    gate_z = filled(by_row(taken, kept_in))

    own_tokens = tokens // 4
    devices_back = (WIN + own_tokens - 2) // own_tokens
    halo_rows = devices_back * own_tokens
    tail_rows = CONV - 1
    kv_width = KVH * HD
    start_row = seq * tokens + member * own_tokens
    seg_padded = jnp.concatenate([jnp.full((halo_rows,), -1, jnp.int32), segment_ids])
    key_segs = lax.dynamic_slice(seg_padded, (start_row,), (halo_rows + own_tokens,))
    query_segs = key_segs[halo_rows:]
    query_glob = start_row + jnp.arange(own_tokens, dtype=jnp.int32)
    key_glob = start_row - halo_rows + jnp.arange(halo_rows + own_tokens, dtype=jnp.int32)
    doc_start = jnp.sum((segment_ids[:, None] < query_segs[None, :]).astype(jnp.int32), axis=0)
    frequency = THETA ** (-2.0 * jnp.arange(HD // 2, dtype=jnp.float32) / HD)
    angles = frequency[:, None] * wide(query_glob - doc_start)[None, :]
    cosine, sine = jnp.cos(angles), jnp.sin(angles)
    score_scale = HD ** (-0.5)
    query = low(turned(wide(qkv_core[:D]), cosine, sine, False) * score_scale)
    key_own = low(turned(wide(qkv_core[D : D + kv_width]), cosine, sine, False))
    pair_own = jnp.concatenate([key_own, qkv_core[D + kv_width :]], axis=0)
    groups_back = (WIN + tokens - 2) // tokens
    distance = query_glob[None, :] - key_glob[:, None]
    visible = (key_segs[:, None] == query_segs[None, :]) & (distance >= 0) & (distance < WIN)
    mask = jnp.where(
        jnp.concatenate([jnp.ones((META, own_tokens), jnp.bool_), visible], axis=0), 0.0, NEG
    )

    conv_w, conv_b = channels(conv_weight, 1), channels(conv_bias, 0)
    select_w, step_w = channels(select_weight.T, 1), channels(step_weight, 1)
    step_b, skip_g = channels(step_bias, 0), channels(skip_gain, 0)
    mixer_g = channels(mixer_gain, 0)
    decay_rates = jnp.exp(channels(log_rates, 0).T)
    valid = lax.broadcasted_iota(jnp.int32, (1, lanes), 1) < quarter
    rates = jnp.where(valid, -LOG2E * decay_rates, 0.0)

    edge = wide(inner_own[:, tokens - LANE :])[:, LANE - tail_rows :].T
    tail = jnp.pad(moved(edge, "seq", 1), ((SUB - tail_rows, 0), (0, 0)))
    conv_segs = lax.dynamic_slice(
        seg_padded, (seq * tokens + halo_rows - tail_rows,), (tokens + tail_rows,)
    )
    own_segs = conv_segs[tail_rows:]
    age = sum(wide(conv_segs[tap : tap + tokens] == own_segs) for tap in range(tail_rows))
    age = jnp.broadcast_to(age[:, None], (tokens, LANE))
    step_w = jnp.pad(step_w, ((0, SELECTED - DT_RANK), (0, 0)))
    mixer = Mixer(
        tokens, lanes, age, inner_own, tail, gate_z, conv_w, conv_b[None], select_w, step_w, step_b[None],
        rates, skip_g[None], mixer_g[None],
    )
    mixed_in, picked = mixer.first()
    pairs = told(pair_own, GROUP)
    pair_group = jnp.concatenate(
        [
            lax.dynamic_index_in_dim(pairs, i + nothing(mixed_in), 0, keepdims=False)
            for i in range(pairs.shape[0])
        ],
        axis=1,
    )
    halo = [moved(pair_group, "seq", offset) for offset in range(groups_back, 0, -1)]
    skipped = (groups_back * tokens - halo_rows) + member * own_tokens
    window = lax.dynamic_slice_in_dim(
        jnp.concatenate(halo + [pair_group], axis=1), skipped, halo_rows + own_tokens, axis=1
    )
    meta_pair = meta_cache.transpose(0, 2, 1).reshape(2 * kv_width, META)
    pair_all = jnp.concatenate([meta_pair, window], axis=1)
    selected = group_total(picked)
    attn, log_totals = run_attention(query, pair_all[:kv_width], pair_all[kv_width:], mask, ())
    end = mixer.totals(selected, (attn,))
    ends = told(end, "seq")
    spans = ends[:, STATE, :]
    state_in = entering_state(ends[:, :STATE], spans, rates, False)

    attn_factor = lax.rsqrt(jnp.mean(attn * attn, axis=0, keepdims=True) + EPS)
    attn_low = low(attn * attn_factor * attn_gain[:, None])
    attn_part = lax.all_to_all(attn_low, GROUP, split_axis=0, concat_axis=1, tiled=True)
    attn_rows = col_joined(attn_part)
    grad_m = row_joined(grad_out.T)
    down_t, mixer_out_t = down_weight.T, mixer_out_weight.T
    dact = col_summed(over_rows(down_t, grad_m))

    squares = mixer.outputs(state_in, (attn_rows, dact))
    mixer_factor = lax.rsqrt(group_total(squares) / DI + EPS)
    mixer_rows = col_joined(mixer.normed(mixer_factor, mixer_g)[:quarter])

    mix_m = row_summed(
        0.5 * (over_rows(attn_out_weight, attn_rows) + dot_plain(mixer_out_t, mixer_rows))
    )
    resid_m = hm + mix_m
    post_factor = lax.rsqrt(over_cols(jnp.sum(resid_m * resid_m, axis=0)) / D + EPS)[None, :]
    second_m = low(resid_m * post_factor * post_g)
    gate_act = col_summed(over_rows(gate_weight, second_m))
    up_act = col_summed(over_rows(up_weight, second_m))
    sig_gate = jax.nn.sigmoid(gate_act)
    dgate_low = low(dact * up_act * sig_gate * (1.0 + gate_act * (1.0 - sig_gate)))
    dup_low = low(dact * gate_act * sig_gate)
    act_low = low(gate_act * sig_gate * up_act)
    dgate_rows = col_joined(dgate_low)
    dup_rows = col_joined(dup_low)
    act_rows = col_joined(act_low)
    dsecond_m = row_summed(dot_plain(gate_weight, dgate_rows) + dot_plain(up_weight, dup_rows))
    sum_gate = SeqSum(dgate_rows, second_m, 1.0, True)
    sum_up = SeqSum(dup_rows, second_m, 1.0, True)
    weighted_m = dsecond_m * post_g
    inner_sum = over_cols(jnp.sum(weighted_m * resid_m, axis=0)) / D
    pull_back = post_factor**3 * inner_sum[None, :]
    dmid_m = wide(grad_m) + post_factor * weighted_m - resid_m * pull_back
    post_part = jnp.sum(dsecond_m * resid_m * post_factor, axis=1)
    low_m = low(dmid_m)

    dmixer_low = filled(low(0.5 * col_summed(over_rows(mixer_out_t, low_m))))
    dattn_part = low(0.5 * col_summed(dot_plain(attn_out_weight, low_m)))
    dattn_core = lax.all_to_all(dattn_part, GROUP, split_axis=1, concat_axis=0, tiled=True)

    mixer_sum = group_total(mixer.norm_pull(dmixer_low)) / DI
    back_end, dz_own, side_norm = mixer.back_totals(
        mixer_factor,
        mixer_factor**3 * mixer_sum,
        [sum_gate.sent, sum_up.sent],
    )
    adjoint_in = entering_state(told(back_end, "seq"), spans, rates, True)

    incoming = wide(dattn_core)
    attn_weighted = incoming * attn_gain[:, None]
    attn_sum = jnp.mean(attn_weighted * attn, axis=0, keepdims=True)
    dattn = low(attn_factor * attn_weighted - attn * (attn_factor**3 * attn_sum))
    attn_gain_part = jnp.sum(incoming * attn * attn_factor, axis=1)
    delta = jnp.sum((wide(dattn) * attn).reshape(H, HD, own_tokens), axis=1)
    delta = jnp.pad(
        delta.reshape(KVH, H // KVH, own_tokens), ((0, 0), (0, SUB - H // KVH), (0, 0))
    )
    reach = groups_back * tokens
    dquery, dkey, dvalue = run_attention_back(
        query, pair_all[:kv_width], pair_all[kv_width:], mask, dattn, log_totals, delta,
        skipped.reshape((1,)), META + reach + tokens,
        [back_end, sum_gate.got],
    )
    sum_gate.step(dquery)
    sum_up.step(sum_gate.now)

    sum_down = SeqSum(grad_m, act_rows, 1.0, False, [adjoint_in])
    both_rows = jnp.concatenate([attn_rows, mixer_rows], axis=0)
    sum_out = SeqSum(low_m, both_rows, 0.5, False, [adjoint_in])
    side_step, drates, step_weight_part, dpicked = mixer.back_grads(
        adjoint_in,
        [sum_gate.now, sum_up.now, sum_down.sent, sum_out.sent],
    )
    dpicked = held_until(dpicked, [sum_gate.got, sum_up.got, sum_down.got, sum_out.got])
    sums = [sum_gate, sum_up, sum_out, sum_down]
    for part in sums:
        part.step(drates)
    dinner_own, edges, side_conv, select_part = mixer.last(
        group_total(dpicked),
        [sum_gate.got, sum_up.got],
    )
    held = wide(nothing(drates))
    dgroup = jnp.concatenate([dkey[:, META + reach :], dvalue[:, META + reach :]], axis=0)
    dgroup = dgroup + wide(nothing(select_part))
    for offset in range(1, groups_back + 1):
        at = slice(META + reach - offset * tokens, META + reach - (offset - 1) * tokens)
        piece = low(jnp.concatenate([dkey[:, at], dvalue[:, at]], axis=0) + held)
        dgroup = dgroup + wide(moved(piece, "seq", -offset))
    shares = lax.all_to_all(
        low(dgroup).reshape(2 * kv_width, 4, own_tokens), GROUP, split_axis=1, concat_axis=1
    )
    dpair_own = jnp.sum(wide(shares), axis=1)
    dquery = turned(dquery * score_scale, cosine, sine, True)
    dkey_own = turned(dpair_own[:kv_width], cosine, sine, True)
    dqkv_core = low(
        jnp.concatenate([dquery, dkey_own, dpair_own[kv_width:]], axis=0)
    )
    dqkv_part = lax.all_to_all(dqkv_core, GROUP, split_axis=0, concat_axis=1, tiled=True)
    dqkv_rows = col_joined(dqkv_part)
    sum_qkv = SeqSum(dqkv_rows, first_m)

    lost = moved(edges[SUB - tail_rows : SUB], "seq", -1)
    ending = low(edges[2 * SUB - tail_rows :] + lost).T
    dinner_own = lax.dynamic_update_slice(dinner_own, ending, (0, tokens - tail_rows))[:quarter]
    dz_t = dz_own[:quarter]
    got_back = swapped(by_row(dz_t, dinner_own), "row")
    dnear = col_joined(by_row(dinner_own, got_back))
    dfar = col_joined(by_row(got_back, dz_t))
    dinner_rows = jnp.concatenate([dnear, dfar], axis=0)
    dchunks = dinner_rows.reshape(lax.axis_size("seq"), -1, tokens)
    cut = dchunks.shape[1] // 16 * 8
    sum_out.step(select_part)
    sum_down.step(select_part)
    sums_in = [
        SeqSum(dchunks[:, :cut].reshape(-1, tokens), first_m, 1.0, False, [sum_out.got]),
        SeqSum(dchunks[:, cut:].reshape(-1, tokens), first_m),
    ]
    begun = [part.sent for part in sums_in]
    params = jnp.concatenate(
        [
            select_part,
            step_weight_part[:DT_RANK],
            drates,
            side_conv[: CONV + 1],
            side_step[:1] + wide(nothing(*begun)),
            side_norm[:2],
        ],
        axis=0,
    )
    params = seq_reduce(low(params))
    params = wide(told(low(params), ALL))
    count = lax.axis_size("seq")
    params = params.reshape((count, 4) + params.shape[1:])
    params = jnp.concatenate(
        [params[:, q].reshape(-1, lanes)[:, :quarter] for q in range(4)], axis=1
    )

    dqkv_late = lax.dynamic_slice_in_dim(dqkv_rows, nothing(*begun), dqkv_rows.shape[0], axis=0)
    dfirst_part = dot_plain(qkv_weight, dqkv_late) + dot_plain(mixer_in_weight, dinner_rows)
    first_sum = group_total(jnp.sum(dfirst_part * pre_g * hm, axis=0)) / D

    def block(values):
        return lax.dynamic_slice_in_dim(values, row * (half // 2), half // 2, axis=0)

    dfirst = row_scattered(dfirst_part)
    own_hidden = block(hm)
    grad_in = (
        block(dmid_m)
        + pre_factor * dfirst * block(pre_g)
        - own_hidden * (pre_factor**3 * first_sum[None, :])
    )
    pre_part = jnp.sum(dfirst * own_hidden * pre_factor, axis=1)
    act_late = lax.dynamic_slice_in_dim(act_rows, nothing(*begun), act_rows.shape[0], axis=0)
    hidden_out = low(block(resid_m) + row_scattered(dot_plain(down_t, act_late)))

    gain_block = pre_gain.shape[0]
    block_pos = (2 * col + row) * gain_block

    def spread(part):
        return lax.dynamic_update_slice(jnp.zeros((D,), jnp.float32), part, (block_pos,))

    early = all_total(
        jnp.concatenate(
            [
                (dkey[:, :META] + wide(nothing(*begun))).reshape(-1),
                dvalue[:, :META].reshape(-1),
                attn_gain_part,
                spread(block(post_part[:, None])[:, 0]),
            ]
        )
    )
    meta_size = 2 * kv_width * META
    meta_grad = early[:meta_size].reshape(2, kv_width, META).transpose(0, 2, 1)
    attn_gain_grad = early[meta_size : meta_size + D]
    post_grad = early[meta_size + D :]
    pre_parts = told(pre_part, ALL).reshape((count, 2, 2, gain_block))
    pre_grad = jnp.sum(pre_parts, axis=0).transpose(1, 0, 2).reshape(-1)
    out_grads = sum_out.finish(*begun)
    for part in sums_in + sums_in + [sum_qkv]:
        part.step(*begun)
    ranks = DT_RANK + 2 * STATE
    at_rates = ranks + DT_RANK
    at_conv = at_rates + STATE
    return (
        hidden_out.T,
        grad_in.T,
        pre_grad,
        sum_qkv.finish(*begun).T,
        jnp.concatenate([piece.finish(params) for piece in sums_in], axis=0).T,
        meta_grad,
        params[at_conv : at_conv + CONV],
        params[at_conv + CONV],
        params[:ranks].T,
        params[ranks:at_rates],
        params[at_conv + CONV + 1],
        params[at_rates:at_conv].T,
        params[at_conv + CONV + 2],
        attn_gain_grad,
        params[at_conv + CONV + 3],
        out_grads[:, :half].T,
        out_grads[:, half:].T,
        post_grad,
        sum_gate.finish(*begun),
        sum_up.finish(*begun),
        sum_down.finish(*begun).T,
    )


def solution(mesh):
    in_specs = (
        P("seq", ("col", "row")),
        P("seq", ("col", "row")),
        P(),
        P(("col", "row")),
        P("col", "row"),
        P("col", "row"),
        P(),
        P(),
        P(),
        P(),
        P(),
        P(),
        P(),
        P(),
        P(),
        P(),
        P("row", "col"),
        P("row", "col"),
        P(("col", "row")),
        P("col", "row"),
        P("col", "row"),
        P("row", "col"),
    )
    out_specs = (
        P("seq", ("col", "row")),
        P("seq", ("col", "row")),
        P(),
        P("col", ("row", "seq")),
        P("col", ("row", "seq")),
        P(),
        P(),
        P(),
        P(),
        P(),
        P(),
        P(),
        P(),
        P(),
        P(),
        P("row", ("col", "seq")),
        P("row", ("col", "seq")),
        P(),
        P("col", ("row", "seq")),
        P("col", ("row", "seq")),
        P("row", ("col", "seq")),
    )
    return jax.shard_map(shards, mesh=mesh, in_specs=in_specs, out_specs=out_specs, check_vma=False)
```

time: 1290 us -> 1050 us (0.81)
  matrix products: 192 us -> 91.8 us
  blocking collectives: 97.4 us -> 0 us
  local copies, waits for them, and re-layouts: 255 us -> 169 us
  Pallas kernels: 131 us -> 211 us
  waiting for transfers between devices: 237 us -> 282 us
  other arithmetic: 184 us -> 141 us
  starting transfers between devices: 165 us -> 132 us
    psum x4 -> x0, blocking collectives: 97.4 us -> none  [the longest x1 71.9 us: shards(): pre_grad = lax.psum(spread(pre_part), ALL)]
    dot_general x58 -> x21, matrix products: 147 us -> 65.5 us  [the longest x14 40.4 us: product(): lax.dot_general(*operands, (dims, ((), ())), preferred_element_type=jnp.f...]
    pallas_call x4 -> x11, Pallas kernels: 131 us -> 211 us  [run_tiles(): pl.pallas_call(kernel, grid=(steps,), in_specs=specs, out_specs=[spec for...]
    another operation x14 -> x2, local copies, waits for them, and re-layouts: 52.2 us -> 2.46 us  [the longest x1 1.64 us: straight(): return with_layout_constraint(values, Layout(tuple(range(values.ndim))))]
    broadcast_in_dim x8 -> x43, local copies, waits for them, and re-layouts: 5.77 us -> 48.9 us  [the longest x28 35 us: joined(): both = jnp.where(which == place, mine[None], other[None])]
    ppermute x66 -> x62, waiting for transfers between devices: 219 us -> 252 us  [the longest x21 128 us: send(): self.got = straight(lax.ppermute(self.sent, 'seq', route))]
    reduce_sum x20 -> x12, other arithmetic: 40 us -> 9.7 us  [the longest x1 1.85 us: shards(): jnp.sum((segment_ids[:, None] < query_segs[None, :]).astype(jnp.int32), a...]
    unnamed x429 -> x336, local copies, waits for them, and re-layouts: 43.3 us -> 13.8 us
  transfers between devices with their start and end apart: 92 -> 80, of which waited for: 20 -> 30; matrix products, arithmetic and copies ran while one was open for 42% -> 34% of each run, Pallas kernels for 4% -> 17%
where the time goes in v2:
time: 1050 us; the launch traced here: 1040 us
  waiting for transfers between devices  282 us (27%)
  Pallas kernels  211 us (20%)
  local copies, waits for them, and re-layouts  169 us (16%)
  other arithmetic  141 us (13%)
  starting transfers between devices  132 us (13%)
  matrix products  91.8 us (9%)
    pallas_call x11, Pallas kernels, run_tiles(): pl.pallas_call(kernel, grid=(steps,), in_specs=specs, out_specs=[spec for...  211 us
    ppermute x21, waiting for transfers between devices, send(): self.got = straight(lax.ppermute(self.sent, 'seq', route))  128 us
    ppermute x38, waiting for transfers between devices, swapped(): return straight(lax.ppermute(straight(values), axis, [(0, 1), (1, 0)]))  72.4 us
    ppermute x3, waiting for transfers between devices, seq_reduce(): parts = mine + wide(lax.ppermute(low(away), 'seq', route))  51.8 us
    dot_general x14, matrix products, product(): lax.dot_general(*operands, (dims, ((), ())), preferred_element_type=jnp.f...  40.4 us
    all_to_all x6, starting transfers between devices, told(): lax.all_to_all(jnp.broadcast_to(values[None], (count,) + values.shape), a...  36.6 us
    broadcast_in_dim x28, local copies, waits for them, and re-layouts, joined(): both = jnp.where(which == place, mine[None], other[None])  35 us
    convert_element_type x21, other arithmetic, low(): return values.astype(jnp.bfloat16)  33.7 us
  transfers between devices with their start and end apart: 80, of which 30 were waited for; matrix products, arithmetic and copies ran while one was open for 34% of the time, Pallas kernels for 17%

profile of v2, /device:TPU:0, one launch (start us, length us, event | category | flops | bytes accessed | tf_op | source)
XLA Modules:
  0.0 1036.1 jit_solution(12308321985137883584)
XLA Ops:
  38.9 6.1 convolution_bitcast_fusion
  54.3 4.2 all-to-all-start
  71.1 4.6 all-to-all-start.1
  75.7 10.2 collective-permute-done.6
  86.0 3.9 broadcast_select_fusion.8
  90.1 4.3 collective-permute-start.7
  94.4 8.3 fusion.163
  108.4 8.2 shard_map.373
  119.7 4.5 collective-permute-start.8
  141.2 13.4 %shard_map.374 = (f32[1600,128]{1,0:T(8,128)}, f32[5,8,128]{2,1,0:T(8,128)}) custom-call(bf16[1600,128]{1,0:T(8,128)(2,1)} %bitcast.645, bf16[320,1280]{1,0:T(8,128)(2,1)} %get-tuple-element.127.refs_1_, bf16[320,1280]{1,0:T(8,128)(2,1)} %get-tuple-element.126.refs_2_, f32[1280,128]{1,0:T(8,128)} %pad_select_fusion.refs_3_), custom_call_target="tpu_custom_call" | custom-call | flops 1024 | bytes 1024 | tf_op jit(solution)/shard_map/pallas_call | solution.py:423
  158.2 4.1 all-to-all-start.2
  168.1 24.4 %shard_map.375 = (f32[512,896]{1,0:T(8,128)}, f32[512,896]{1,0:T(8,128)}, f32[24,896]{1,0:T(8,128)}, f32[7,16,8,128]{3,2,1,0:T(8,128)}, f32[8,896]{1,0:T(8,128)}) custom-call(f32[512,132]{1,0:T(8,128)} %add.718.refs_0_.refs_3_.refs_9_.refs_4_, f32[512,896]{1,0:T(8,128)} %get-tuple-element.51.refs_1_.refs_6_.refs_8_, ...), custom_call_target="tpu_custom_call" | custom-call | flops 1024 | bytes 1024 | tf_op jit(solution)/shard_map/pallas_call | solution.py:423
  194.3 17.6 %all-to-all-start.3 = ((f32[8,24,896]{2,1,0:T(8,128)}), f32[8,24,896]{2,1,0:T(8,128)}, u32[]{:S(2)}, u32[]{:S(2)}) async-start(f32[8,24,896]{2,1,0:T(8,128)} %broadcast_in_dim.496), calls=%async_computation.3 | async-start | bytes 1376256 | tf_op jit(solution)/shard_map/all_to_all | solution.py:817
  217.8 4.2 bitcast_add_fusion.4.refs_11_
  224.0 6.6 all-to-all-done.3
  234.0 28.3 %shard_map.376 = (f32[512,896]{1,0:T(8,128)}, f32[512,896]{1,0:T(8,128)}, f32[8,512]{1,0:T(8,128)}, f32[7,1040,8,128]{3,2,1,0:T(8,128)}) custom-call(f32[512,896]{1,0:T(8,128)} %get-tuple-element.54.refs_0_.refs_7_, f32[512,896]{1,0:T(8,128)} %get-tuple-element.51.refs_1_.refs_6_.refs_8_, f32[512,128]{1,0:T(8,128)} %broadcast_in_dim.481.refs_2_.refs_8_, ...), custom_call_target="tpu_custom_call" | custom-call | flops 1024 | bytes 1024 | tf_op jit(solution)/shard_map/pallas_call | solution.py:423
  268.9 5.5 shard_map.377
  285.9 18.7 %collective-permute-done.18 = bf16[800,512]{1,0:T(8,128)(2,1)S(1)} collective-permute-done((bf16[800,512]{1,0:T(8,128)(2,1)S(1)}, bf16[800,512]{1,0:T(8,128)(2,1)S(1)}, u32[]{:S(2)}, u32[]{:S(2)}) %collective-permute-start.18) | collective-permute-done | bytes 819232 | tf_op jit(solution)/shard_map/ppermute | solution.py:705
  348.5 7.6 bitcast_select_fusion.1
  356.1 5.8 fusion.168
  364.4 4.9 fusion.169
  372.3 4.2 broadcast_select_fusion.1
  379.6 12.4 %collective-permute-done.26 = bf16[800,512]{1,0:T(8,128)(2,1)S(1)} collective-permute-done((bf16[800,512]{1,0:T(8,128)(2,1)S(1)}, bf16[800,512]{1,0:T(8,128)(2,1)S(1)}, u32[]{:S(2)}, u32[]{:S(2)}) %collective-permute-start.26) | collective-permute-done | bytes 819232 | tf_op jit(solution)/shard_map/ppermute | solution.py:705
  425.2 5.6 shard_map.378
  437.4 23.6 %shard_map.379 = (f32[512,896]{1,0:T(8,128)}, bf16[896,512]{1,0:T(8,128)(2,1)}, f32[8,896]{1,0:T(8,128)}, f32[16,896]{1,0:T(8,128)}, f32[7,16,8,128]{3,2,1,0:T(8,128)}) custom-call(f32[512,896]{1,0:T(8,128)} %get-tuple-element.58.refs_0_, bf16[896,512]{1,0:T(8,128)(2,1)} %pad.77.refs_1_, f32[1,896]{1,0:T(1,128)} %broadcast_in_dim.527.refs_2_, ...), custom_call_target="tpu_custom_call" | custom-call | flops 1024 | bytes 1024 | tf_op jit(solution)/shard_map/pallas_call | solution.py:423
  462.6 4.1 all-to-all-start.5
  468.1 17.3 %shard_map.380 = (f32[1600,128]{1,0:T(8,128)}, f32[320,1664]{1,0:T(8,128)}, f32[320,1664]{1,0:T(8,128)}) custom-call(bf16[1600,128]{1,0:T(8,128)(2,1)} %bitcast.646, bf16[320,1280]{1,0:T(8,128)(2,1)} %get-tuple-element.127.refs_1_, bf16[320,1280]{1,0:T(8,128)(2,1)} %get-tuple-element.126.refs_2_, f32[1280,128]{1,0:T(8,128)} %pad_select_fusion.refs_3_, ...), custom_call_target="tpu_custom_call" | custom-call | flops 1024 | bytes 1024 | tf_op jit(solution)/shard_map/pallas_call | solution.py:423
  497.0 12.1 %collective-permute-done.33 = bf16[2,2,800,344]{3,2,1,0:T(8,128)(2,1)} collective-permute-done((bf16[2,2,800,344]{3,2,1,0:T(8,128)(2,1)}, bf16[2,2,800,344]{3,2,1,0:T(8,128)(2,1)}, u32[]{:S(2)}, u32[]{:S(2)}) %collective-permute-start.33) | collective-permute-done | bytes 2201632 | tf_op jit(solution)/shard_map/ppermute | solution.py:778
  509.1 5.3 fusion.refs_14_
  519.3 4.2 fusion.2.refs_16_
  532.3 71.0 %shard_map.381 = (f32[512,896]{1,0:T(8,128)}, f32[8,896]{1,0:T(8,128)}, f32[16,896]{1,0:T(8,128)}, f32[132,896]{1,0:T(8,128)}, f32[512,132]{1,0:T(8,128)}) custom-call(f32[512,896]{1,0:T(8,128)} %get-tuple-element.54.refs_0_.refs_7_, f32[512,896]{1,0:T(8,128)} %get-tuple-element.51.refs_1_.refs_6_.refs_8_, f32[512,128]{1,0:T(8,128)} %broadcast_in_dim.481.refs_2_.refs_8_, ...), custom_call_target="tpu_custom_call" | custom-call | flops 1024 | bytes 1024 | tf_op jit(solution)/shard_map/pallas_call | solution.py:423
  618.0 5.2 collective-permute-start.40
  639.4 9.2 collective-permute-done.39
  652.6 30.4 %collective-permute-done.40.refs_9_ = bf16[800,344]{1,0:T(8,128)(2,1)S(1)} collective-permute-done((bf16[800,344]{1,0:T(8,128)(2,1)}, bf16[800,344]{1,0:T(8,128)(2,1)S(1)}, u32[]{:S(2)}, u32[]{:S(2)}) %collective-permute-start.40) | collective-permute-done | bytes 550432 | tf_op jit(solution)/shard_map/ppermute | solution.py:778
  682.9 10.6 %collective-permute-done.41.refs_10_ = bf16[800,344]{1,0:T(8,128)(2,1)S(1)} collective-permute-done((bf16[800,344]{1,0:T(8,128)(2,1)}, bf16[800,344]{1,0:T(8,128)(2,1)S(1)}, u32[]{:S(2)}, u32[]{:S(2)}) %collective-permute-start.41) | collective-permute-done | bytes 550432 | tf_op jit(solution)/shard_map/ppermute | solution.py:778
  694.4 10.9 %shard_map.383 = (bf16[896,512]{1,0:T(8,128)(2,1)}, f32[16,896]{1,0:T(8,128)}, f32[8,896]{1,0:T(8,128)}, f32[132,896]{1,0:T(8,128)}) custom-call(bf16[896,512]{1,0:T(8,128)(2,1)} %pad.64.refs_0_, f32[8,896]{1,0:T(8,128)} %pad.65.clone.refs_1_, f32[512,128]{1,0:T(8,128)} %broadcast_in_dim.481.refs_2_.refs_8_, f32[4,896]{1,0:T(4,128)} %pad.66.refs_3_, ...), custom_call_target="tpu_custom_call" | custom-call | flops 1024 | bytes 1024 | tf_op jit(solution)/shard_map/pallas_call | solution.py:423
  728.3 3.9 all-to-all-start.7
  733.3 10.9 %collective-permute-done.46 = bf16[800,512]{1,0:T(8,128)(2,1)} collective-permute-done((bf16[800,512]{1,0:T(8,128)(2,1)}, bf16[800,512]{1,0:T(8,128)(2,1)}, u32[]{:S(2)}, u32[]{:S(2)}) %collective-permute-start.46) | collective-permute-done | bytes 819232 | tf_op jit(solution)/shard_map/ppermute | solution.py:705
  752.9 6.1 collective-permute-done.53
  773.8 6.6 fusion.152
  800.5 4.4 concatenate.88
  820.3 43.6 %collective-permute-done.59 = bf16[2,2,32,896]{3,2,1,0:T(8,128)(2,1)} collective-permute-done((bf16[2,2,32,896]{3,2,1,0:T(8,128)(2,1)}, bf16[2,2,32,896]{3,2,1,0:T(8,128)(2,1)}, u32[]{:S(2)}, u32[]{:S(2)}) %collective-permute-start.59) | collective-permute-done | bytes 229408 | tf_op jit(solution)/shard_map/ppermute | solution.py:811
  875.8 17.3 %all-to-all-done.8 = f32[32,1,400]{2,1,0:T(1,128)S(1)} async-done(((f32[32,1,400]{2,1,0:T(1,128)}), f32[32,1,400]{2,1,0:T(1,128)S(1)}, u32[]{:S(2)}, u32[]{:S(2)}) %all-to-all-start.8) | async-done | bytes 51232 | tf_op jit(solution)/shard_map/all_to_all | solution.py:817
  902.3 8.1 collective-permute-done.61
  923.3 36.6 %collective-permute-done.55 = bf16[2,144,800]{2,1,0:T(8,128)(2,1)S(1)} collective-permute-done((bf16[2,144,800]{2,1,0:T(8,128)(2,1)S(1)}, bf16[2,144,800]{2,1,0:T(8,128)(2,1)S(1)}, u32[]{:S(2)}, u32[]{:S(2)}) %collective-permute-start.55) | collective-permute-done | bytes 460832 | tf_op jit(solution)/shard_map/ppermute | solution.py:778
  977.7 12.6 %collective-permute-done.64 = bf16[2,200,800]{2,1,0:T(8,128)(2,1)} collective-permute-done((bf16[2,200,800]{2,1,0:T(8,128)(2,1)}, bf16[2,200,800]{2,1,0:T(8,128)(2,1)}, u32[]{:S(2)}, u32[]{:S(2)}) %collective-permute-start.64) | collective-permute-done | bytes 640032 | tf_op jit(solution)/shard_map/ppermute | solution.py:778
  992.3 19.9 %collective-permute-done.58 = bf16[2,200,800]{2,1,0:T(8,128)(2,1)} collective-permute-done((bf16[2,200,800]{2,1,0:T(8,128)(2,1)}, bf16[2,200,800]{2,1,0:T(8,128)(2,1)}, u32[]{:S(2)}, u32[]{:S(2)}) %collective-permute-start.58) | collective-permute-done | bytes 640032 | tf_op jit(solution)/shard_map/ppermute | solution.py:778
  1016.2 4.7 concatenate.89
  (756 shorter events, 429.9 us)
Async XLA Ops:
  0.7 34.8 %collective-permute-start = (bf16[400,512]{1,0:T(8,128)(2,1)}, bf16[400,512]{1,0:T(8,128)(2,1)S(1)}, u32[]{:S(2)}, u32[]{:S(2)}) collective-permute-start(bf16[400,512]{1,0:T(8,128)(2,1)} %bitcast.639), channel_id=1, source_target_pairs={{0,2},{2,0},{1,3},{3,1},{4,6},{6,4},{5,7},{7,5},{8,10},{10,8},{9,1... | collective-permute-start | bytes 1228808 | tf_op jit(solution)/shard_map/ppermute | solution.py:705
  3.7 61.1 %collective-permute-start.13 = (bf16[400,512]{1,0:T(8,128)(2,1)}, bf16[400,512]{1,0:T(8,128)(2,1)}, u32[]{:S(2)}, u32[]{:S(2)}) collective-permute-start(bf16[400,512]{1,0:T(8,128)(2,1)} %bitcast.666), channel_id=1, source_target_pairs={{0,2},{2,0},{1,3},{3,1},{4,6},{6,4},{5,7},{7,5},{8,10},{10,8},{9,1... | collective-permute-start | bytes 1228808 | tf_op jit(solution)/shard_map/ppermute | solution.py:705
  5.3 25.1 %collective-permute-start.2 = (f32[400,2]{1,0:T(8,128)}, f32[400,2]{1,0:T(8,128)}, u32[]{:S(2)}, u32[]{:S(2)}) collective-permute-start(f32[400,2]{1,0:T(8,128)} %copy.220), channel_id=1, source_target_pairs={{0,2},{2,0},{1,3},{3,1},{4,6},{6,4},{5,7},{7,5},{8,10},{10,8},{9,1... | collective-permute-start | bytes 9608 | tf_op jit(solution)/shard_map/ppermute | solution.py:705
  53.4 22.3 %collective-permute-start.4 = (bf16[800,512]{1,0:T(8,128)(2,1)}, bf16[800,512]{1,0:T(8,128)(2,1)}, u32[]{:S(2)}, u32[]{:S(2)}) collective-permute-start(bf16[800,512]{1,0:T(8,128)(2,1)} %get-tuple-element.108), channel_id=1, source_target_pairs={{0,1},{1,0},{2,3},{3,2},{4,5},{5,4},{6,7},{7,6},{8,9},{9,8},{10,11... | collective-permute-start | bytes 2457608 | tf_op jit(solution)/shard_map/ppermute | solution.py:705
  62.1 23.8 %collective-permute-start.6 = (bf16[800,512]{1,0:T(8,128)(2,1)}, bf16[800,512]{1,0:T(8,128)(2,1)}, u32[]{:S(2)}, u32[]{:S(2)}) collective-permute-start(bf16[800,512]{1,0:T(8,128)(2,1)} %add_convert_fusion.6), channel_id=1, source_target_pairs={{0,2},{2,0},{1,3},{3,1},{4,6},{6,4},{5,7},{7,5},{8,10},{10,8},{9,1... | collective-permute-start | bytes 2457608 | tf_op jit(solution)/shard_map/ppermute | solution.py:705
  71.1 47.3 %all-to-all-start.1 = ((bf16[4,640,128]{2,1,0:T(8,128)(2,1)}), bf16[4,640,128]{2,1,0:T(8,128)(2,1)}, u32[]{:S(2)}, u32[]{:S(2)}) async-start(bf16[4,640,128]{2,1,0:T(8,128)(2,1)} %broadcast_in_dim.480), calls=%async_computation.1 | async-start | bytes 1310720 | tf_op jit(solution)/shard_map/all_to_all | solution.py:817
  129.9 87.9 %collective-permute-start.14 = (bf16[1376,512]{1,0:T(8,128)(2,1)}, bf16[1376,512]{1,0:T(8,128)(2,1)}, u32[]{:S(2)}, u32[]{:S(2)}) collective-permute-start(bf16[1376,512]{1,0:T(8,128)(2,1)} %fusion.16), channel_id=1, source_target_pairs={{0,1},{1,0},{2,3},{3,2},{4,5},{5,4},{6,7},{7,6},{8,9},{9,8},{10,11... | collective-permute-start | bytes 4227080 | tf_op jit(solution)/shard_map/ppermute | solution.py:705
  134.6 31.4 %collective-permute-start.12 = (f32[512,132]{1,0:T(8,128)}, f32[512,132]{1,0:T(8,128)}, u32[]{:S(2)}, u32[]{:S(2)}) collective-permute-start(f32[512,132]{1,0:T(8,128)} %add.717), channel_id=1, source_target_pairs={{0,2},{2,0},{1,3},{3,1},{4,6},{6,4},{5,7},{7,5},{8,10},{10,8},{9,1... | collective-permute-start | bytes 811016 | tf_op jit(solution)/shard_map/ppermute | solution.py:705
  158.2 34.3 %all-to-all-start.2 = ((bf16[4,400,128]{2,1,0:T(8,128)(2,1)}), bf16[4,400,128]{2,1,0:T(8,128)(2,1)}, u32[]{:S(2)}, u32[]{:S(2)}) async-start(bf16[4,400,128]{2,1,0:T(8,128)(2,1)} %bitcast.664), calls=%async_computation.2 | async-start | bytes 819200 | tf_op jit(solution)/shard_map/all_to_all | solution.py:1004
  194.3 36.4 %all-to-all-start.3 = ((f32[8,24,896]{2,1,0:T(8,128)}), f32[8,24,896]{2,1,0:T(8,128)}, u32[]{:S(2)}, u32[]{:S(2)}) async-start(f32[8,24,896]{2,1,0:T(8,128)} %broadcast_in_dim.496), calls=%async_computation.3 | async-start | bytes 1376256 | tf_op jit(solution)/shard_map/all_to_all | solution.py:817
  284.3 20.4 %collective-permute-start.18 = (bf16[800,512]{1,0:T(8,128)(2,1)S(1)}, bf16[800,512]{1,0:T(8,128)(2,1)S(1)}, u32[]{:S(2)}, u32[]{:S(2)}) collective-permute-start(bf16[800,512]{1,0:T(8,128)(2,1)S(1)} %fusion.32), channel_id=1, source_target_pairs={{0,2},{2,0},{1,3},{3,1},{4,6},{6,4},{5,7},{7,5},{8,10},{10,8},{9,1... | collective-permute-start | bytes 2457608 | tf_op jit(solution)/shard_map/ppermute | solution.py:705
  320.6 27.9 %collective-permute-start.24 = (bf16[1376,512]{1,0:T(8,128)(2,1)}, bf16[1376,512]{1,0:T(8,128)(2,1)}, u32[]{:S(2)}, u32[]{:S(2)}) collective-permute-start(bf16[1376,512]{1,0:T(8,128)(2,1)} %get-tuple-element.105), channel_id=1, source_target_pairs={{0,1},{1,0},{2,3},{3,2},{4,5},{5,4},{6,7},{7,6},{8,9},{9,8},{10,11... | collective-permute-start | bytes 4227080 | tf_op jit(solution)/shard_map/ppermute | solution.py:705
  321.0 27.6 %collective-permute-start.25 = (bf16[1376,512]{1,0:T(8,128)(2,1)}, bf16[1376,512]{1,0:T(8,128)(2,1)}, u32[]{:S(2)}, u32[]{:S(2)}) collective-permute-start(bf16[1376,512]{1,0:T(8,128)(2,1)} %get-tuple-element.107), channel_id=1, source_target_pairs={{0,1},{1,0},{2,3},{3,2},{4,5},{5,4},{6,7},{7,6},{8,9},{9,8},{10,11... | collective-permute-start | bytes 4227080 | tf_op jit(solution)/shard_map/ppermute | solution.py:705
  321.1 27.4 %collective-permute-start.22 = (bf16[1376,512]{1,0:T(8,128)(2,1)}, bf16[1376,512]{1,0:T(8,128)(2,1)}, u32[]{:S(2)}, u32[]{:S(2)}) collective-permute-start(bf16[1376,512]{1,0:T(8,128)(2,1)} %get-tuple-element.106), channel_id=1, source_target_pairs={{0,1},{1,0},{2,3},{3,2},{4,5},{5,4},{6,7},{7,6},{8,9},{9,8},{10,11... | collective-permute-start | bytes 4227080 | tf_op jit(solution)/shard_map/ppermute | solution.py:705
  362.8 50.6 %collective-permute-start.23 = (bf16[400,512]{1,0:T(8,128)(2,1)}, bf16[400,512]{1,0:T(8,128)(2,1)}, u32[]{:S(2)}, u32[]{:S(2)}) collective-permute-start(bf16[400,512]{1,0:T(8,128)(2,1)} %fusion.91), channel_id=1, source_target_pairs={{0,2},{2,0},{1,3},{3,1},{4,6},{6,4},{5,7},{7,5},{8,10},{10,8},{9,1... | collective-permute-start | bytes 1228808 | tf_op jit(solution)/shard_map/ppermute | solution.py:705
  396.3 71.8 %collective-permute-start.32 = (bf16[2,2,800,344]{3,2,1,0:T(8,128)(2,1)}, bf16[2,2,800,344]{3,2,1,0:T(8,128)(2,1)}, u32[]{:S(2)}, u32[]{:S(2)}) collective-permute-start(bf16[2,2,800,344]{3,2,1,0:T(8,128)(2,1)} %convert_bitcast_fusion.1.refs_12_), channel_id=1, source_target_pairs={{0,4},{4,0},{8,12},{12,8},{16,20},{20,16},{24,28},{28,24},{1,5},{5... | collective-permute-start | bytes 6604808 | tf_op jit(solution)/shard_map/ppermute | solution.py:778
  397.7 111.4 %collective-permute-start.33 = (bf16[2,2,800,344]{3,2,1,0:T(8,128)(2,1)}, bf16[2,2,800,344]{3,2,1,0:T(8,128)(2,1)}, u32[]{:S(2)}, u32[]{:S(2)}) collective-permute-start(bf16[2,2,800,344]{3,2,1,0:T(8,128)(2,1)} %convert_bitcast_fusion.refs_13_), channel_id=1, source_target_pairs={{0,4},{4,0},{8,12},{12,8},{16,20},{20,16},{24,28},{28,24},{1,5},{5... | collective-permute-start | bytes 6604808 | tf_op jit(solution)/shard_map/ppermute | solution.py:778
  462.6 54.2 %all-to-all-start.5 = ((f32[8,16,896]{2,1,0:T(8,128)}), f32[8,16,896]{2,1,0:T(8,128)}, u32[]{:S(2)}, u32[]{:S(2)}) async-start(f32[8,16,896]{2,1,0:T(8,128)} %broadcast_in_dim.540), calls=%async_computation.5 | async-start | bytes 917504 | tf_op jit(solution)/shard_map/all_to_all | solution.py:817
  493.6 120.2 %collective-permute-start.34 = (bf16[2,800,344]{2,1,0:T(8,128)(2,1)}, bf16[2,800,344]{2,1,0:T(8,128)(2,1)}, u32[]{:S(2)}, u32[]{:S(2)}) collective-permute-start(bf16[2,800,344]{2,1,0:T(8,128)(2,1)} %dynamic-slice_bitcast_fusion.1), channel_id=1, source_target_pairs={{0,8},{4,12},{8,0},{12,4},{16,24},{20,28},{24,16},{28,20},{1,9},{5... | collective-permute-start | bytes 3302408 | tf_op jit(solution)/shard_map/ppermute | solution.py:778
  523.5 102.4 %collective-permute-start.37 = (bf16[2,2,104,2400]{3,2,1,0:T(8,128)(2,1)}, bf16[2,2,104,2400]{3,2,1,0:T(8,128)(2,1)}, u32[]{:S(2)}, u32[]{:S(2)}) collective-permute-start(bf16[2,2,104,2400]{3,2,1,0:T(8,128)(2,1)} %fusion.2.refs_16_), channel_id=1, source_target_pairs={{0,4},{4,0},{8,12},{12,8},{16,20},{20,16},{24,28},{28,24},{1,5},{5... | collective-permute-start | bytes 5990408 | tf_op jit(solution)/shard_map/ppermute | solution.py:778
  527.9 101.2 %collective-permute-start.36 = (bf16[2,2,104,2752]{3,2,1,0:T(8,128)(2,1)}, bf16[2,2,104,2752]{3,2,1,0:T(8,128)(2,1)}, u32[]{:S(2)}, u32[]{:S(2)}) collective-permute-start(bf16[2,2,104,2752]{3,2,1,0:T(8,128)(2,1)} %convolution_convert_fusion.refs_15_), channel_id=1, source_target_pairs={{0,4},{4,0},{8,12},{12,8},{16,20},{20,16},{24,28},{28,24},{1,5},{5... | collective-permute-start | bytes 6869000 | tf_op jit(solution)/shard_map/ppermute | solution.py:778
  529.6 88.4 %collective-permute-start.35 = (bf16[2,800,344]{2,1,0:T(8,128)(2,1)}, bf16[2,800,344]{2,1,0:T(8,128)(2,1)}, u32[]{:S(2)}, u32[]{:S(2)}) collective-permute-start(bf16[2,800,344]{2,1,0:T(8,128)(2,1)} %dynamic-slice_bitcast_fusion), channel_id=1, source_target_pairs={{0,8},{4,12},{8,0},{12,4},{16,24},{20,28},{24,16},{28,20},{1,9},{5... | collective-permute-start | bytes 3302408 | tf_op jit(solution)/shard_map/ppermute | solution.py:778
  608.5 100.8 %collective-permute-start.43 = (bf16[640,512]{1,0:T(8,128)(2,1)}, bf16[640,512]{1,0:T(8,128)(2,1)}, u32[]{:S(2)}, u32[]{:S(2)}) collective-permute-start(bf16[640,512]{1,0:T(8,128)(2,1)} %fusion.31), channel_id=1, source_target_pairs={{8,0},{12,4},{16,8},{20,12},{24,16},{28,20},{9,1},{13,5},{17,9},{2... | collective-permute-start | bytes 1966088 | tf_op jit(solution)/shard_map/ppermute | solution.py:711
  613.8 95.5 %collective-permute-start.42 = (bf16[640,512]{1,0:T(8,128)(2,1)}, bf16[640,512]{1,0:T(8,128)(2,1)}, u32[]{:S(2)}, u32[]{:S(2)}) collective-permute-start(bf16[640,512]{1,0:T(8,128)(2,1)} %fusion.30), channel_id=1, source_target_pairs={{4,0},{8,4},{12,8},{16,12},{20,16},{24,20},{28,24},{5,1},{9,5},{13... | collective-permute-start | bytes 1966088 | tf_op jit(solution)/shard_map/ppermute | solution.py:711
  618.0 64.9 %collective-permute-start.40 = (bf16[800,344]{1,0:T(8,128)(2,1)}, bf16[800,344]{1,0:T(8,128)(2,1)S(1)}, u32[]{:S(2)}, u32[]{:S(2)}) collective-permute-start(bf16[800,344]{1,0:T(8,128)(2,1)} %dynamic-slice_bitcast_fusion.7), channel_id=1, source_target_pairs={{0,16},{4,20},{8,24},{12,28},{16,0},{20,4},{24,8},{28,12},{1,17},{... | collective-permute-start | bytes 1651208 | tf_op jit(solution)/shard_map/ppermute | solution.py:778
  625.9 67.6 %collective-permute-start.41 = (bf16[800,344]{1,0:T(8,128)(2,1)}, bf16[800,344]{1,0:T(8,128)(2,1)S(1)}, u32[]{:S(2)}, u32[]{:S(2)}) collective-permute-start(bf16[800,344]{1,0:T(8,128)(2,1)} %dynamic-slice_bitcast_fusion.6), channel_id=1, source_target_pairs={{0,16},{4,20},{8,24},{12,28},{16,0},{20,4},{24,8},{28,12},{1,17},{... | collective-permute-start | bytes 1651208 | tf_op jit(solution)/shard_map/ppermute | solution.py:778
  648.6 76.1 %collective-permute-start.52 = (bf16[2,104,2400]{2,1,0:T(8,128)(2,1)}, bf16[2,104,2400]{2,1,0:T(8,128)(2,1)}, u32[]{:S(2)}, u32[]{:S(2)}) collective-permute-start(bf16[2,104,2400]{2,1,0:T(8,128)(2,1)} %dynamic-slice_bitcast_fusion.3), channel_id=1, source_target_pairs={{0,8},{4,12},{8,0},{12,4},{16,24},{20,28},{24,16},{28,20},{1,9},{5... | collective-permute-start | bytes 2995208 | tf_op jit(solution)/shard_map/ppermute | solution.py:778
  682.9 67.1 %collective-permute-start.66 = (bf16[2,104,2752]{2,1,0:T(8,128)(2,1)}, bf16[2,104,2752]{2,1,0:T(8,128)(2,1)}, u32[]{:S(2)}, u32[]{:S(2)}) collective-permute-start(bf16[2,104,2752]{2,1,0:T(8,128)(2,1)} %dynamic-slice_bitcast_fusion.2), channel_id=1, source_target_pairs={{0,8},{4,12},{8,0},{12,4},{16,24},{20,28},{24,16},{28,20},{1,9},{5... | collective-permute-start | bytes 3434504 | tf_op jit(solution)/shard_map/ppermute | solution.py:778
  722.7 21.4 %collective-permute-start.46 = (bf16[800,512]{1,0:T(8,128)(2,1)}, bf16[800,512]{1,0:T(8,128)(2,1)}, u32[]{:S(2)}, u32[]{:S(2)}) collective-permute-start(bf16[800,512]{1,0:T(8,128)(2,1)} %broadcast_select_fusion.7), channel_id=1, source_target_pairs={{0,2},{2,0},{1,3},{3,1},{4,6},{6,4},{5,7},{7,5},{8,10},{10,8},{9,1... | collective-permute-start | bytes 2457608 | tf_op jit(solution)/shard_map/ppermute | solution.py:705
  728.3 21.6 %all-to-all-start.7 = ((bf16[4,560,128]{2,1,0:T(8,128)(2,1)}), bf16[4,560,128]{2,1,0:T(8,128)(2,1)S(1)}, u32[]{:S(2)}, u32[]{:S(2)}) async-start(bf16[4,560,128]{2,1,0:T(8,128)(2,1)} %bitcast.120), calls=%async_computation.7 | async-start | bytes 1146880 | tf_op jit(solution)/shard_map/all_to_all | solution.py:1100
  733.1 26.0 %collective-permute-start.53 = (bf16[104,2400]{1,0:T(8,128)(2,1)}, bf16[104,2400]{1,0:T(8,128)(2,1)}, u32[]{:S(2)}, u32[]{:S(2)}) collective-permute-start(bf16[104,2400]{1,0:T(8,128)(2,1)} %dynamic-slice_bitcast_fusion.11), channel_id=1, source_target_pairs={{0,16},{4,20},{8,24},{12,28},{16,0},{20,4},{24,8},{28,12},{1,17},{... | collective-permute-start | bytes 1497608 | tf_op jit(solution)/shard_map/ppermute | solution.py:778
  746.8 24.9 %collective-permute-start.47 = (bf16[800,512]{1,0:T(8,128)(2,1)S(1)}, bf16[800,512]{1,0:T(8,128)(2,1)}, u32[]{:S(2)}, u32[]{:S(2)}) collective-permute-start(bf16[800,512]{1,0:T(8,128)(2,1)S(1)} %get-tuple-element.137), channel_id=1, source_target_pairs={{0,1},{1,0},{2,3},{3,2},{4,5},{5,4},{6,7},{7,6},{8,9},{9,8},{10,11... | collective-permute-start | bytes 2457608 | tf_op jit(solution)/shard_map/ppermute | solution.py:705
  746.8 24.9 %collective-permute-start.48 = (bf16[800,512]{1,0:T(8,128)(2,1)}, bf16[800,512]{1,0:T(8,128)(2,1)}, u32[]{:S(2)}, u32[]{:S(2)}) collective-permute-start(bf16[800,512]{1,0:T(8,128)(2,1)} %get-tuple-element.138), channel_id=1, source_target_pairs={{0,1},{1,0},{2,3},{3,2},{4,5},{5,4},{6,7},{7,6},{8,9},{9,8},{10,11... | collective-permute-start | bytes 2457608 | tf_op jit(solution)/shard_map/ppermute | solution.py:705
  769.4 147.2 %collective-permute-start.54 = (bf16[2,2,144,800]{3,2,1,0:T(8,128)(2,1)}, bf16[2,2,144,800]{3,2,1,0:T(8,128)(2,1)}, u32[]{:S(2)}, u32[]{:S(2)}) collective-permute-start(bf16[2,2,144,800]{3,2,1,0:T(8,128)(2,1)} %convolution_convert_fusion.3), channel_id=1, source_target_pairs={{0,4},{4,0},{8,12},{12,8},{16,20},{20,16},{24,28},{28,24},{1,5},{5... | collective-permute-start | bytes 2764808 | tf_op jit(solution)/shard_map/ppermute | solution.py:778
  787.3 176.2 %collective-permute-start.63 = (bf16[2,2,200,800]{3,2,1,0:T(8,128)(2,1)}, bf16[2,2,200,800]{3,2,1,0:T(8,128)(2,1)}, u32[]{:S(2)}, u32[]{:S(2)}) collective-permute-start(bf16[2,2,200,800]{3,2,1,0:T(8,128)(2,1)} %convolution_convert_fusion.1), channel_id=1, source_target_pairs={{0,4},{4,0},{8,12},{12,8},{16,20},{20,16},{24,28},{28,24},{1,5},{5... | collective-permute-start | bytes 3840008 | tf_op jit(solution)/shard_map/ppermute | solution.py:778
  789.4 177.8 %collective-permute-start.57 = (bf16[2,2,200,800]{3,2,1,0:T(8,128)(2,1)}, bf16[2,2,200,800]{3,2,1,0:T(8,128)(2,1)}, u32[]{:S(2)}, u32[]{:S(2)}) collective-permute-start(bf16[2,2,200,800]{3,2,1,0:T(8,128)(2,1)} %copy-done.158), channel_id=1, source_target_pairs={{0,4},{4,0},{8,12},{12,8},{16,20},{20,16},{24,28},{28,24},{1,5},{5... | collective-permute-start | bytes 3840008 | tf_op jit(solution)/shard_map/ppermute | solution.py:778
  793.2 21.9 %collective-permute-start.50 = (f32[512]{0:T(512)S(1)}, f32[512]{0:T(512)S(1)}, u32[]{:S(2)}, u32[]{:S(2)}) collective-permute-start(f32[512]{0:T(512)S(1)} %get-tuple-element.165), channel_id=1, source_target_pairs={{0,1},{1,0},{2,3},{3,2},{4,5},{5,4},{6,7},{7,6},{8,9},{9,8},{10,11... | collective-permute-start | bytes 6152 | tf_op jit(solution)/shard_map/ppermute | solution.py:705
  798.6 65.3 %collective-permute-start.59 = (bf16[2,2,32,896]{3,2,1,0:T(8,128)(2,1)}, bf16[2,2,32,896]{3,2,1,0:T(8,128)(2,1)}, u32[]{:S(2)}, u32[]{:S(2)}) collective-permute-start(bf16[2,2,32,896]{3,2,1,0:T(8,128)(2,1)} %dynamic-slice_bitcast_fusion.16), channel_id=1, source_target_pairs={{0,4},{4,0},{8,12},{12,8},{16,20},{20,16},{24,28},{28,24},{1,5},{5... | collective-permute-start | bytes 688136 | tf_op jit(solution)/shard_map/ppermute | solution.py:811
  806.2 63.0 %all-to-all-start.10 = ((f32[32,1,2660]{2,1,0:T(1,128)}), f32[32,1,2660]{2,1,0:T(1,128)}, u32[]{:S(2)}, u32[]{:S(2)}) async-start(f32[32,1,2660]{2,1,0:T(1,128)} %all_to_all.92), calls=%async_computation.10 | async-start | bytes 688128 | tf_op jit(solution)/shard_map/all_to_all | solution.py:824
  818.7 47.0 %collective-permute-start.49 = (bf16[400,512]{1,0:T(8,128)(2,1)S(1)}, bf16[400,512]{1,0:T(8,128)(2,1)S(1)}, u32[]{:S(2)}, u32[]{:S(2)}) collective-permute-start(bf16[400,512]{1,0:T(8,128)(2,1)S(1)} %fusion.93), channel_id=1, source_target_pairs={{0,2},{2,0},{1,3},{3,1},{4,6},{6,4},{5,7},{7,5},{8,10},{10,8},{9,1... | collective-permute-start | bytes 1228808 | tf_op jit(solution)/shard_map/ppermute | solution.py:705
  864.0 57.2 %collective-permute-start.67 = (bf16[104,2752]{1,0:T(8,128)(2,1)}, bf16[104,2752]{1,0:T(8,128)(2,1)}, u32[]{:S(2)}, u32[]{:S(2)}) collective-permute-start(bf16[104,2752]{1,0:T(8,128)(2,1)} %get-tuple-element.129), channel_id=1, source_target_pairs={{0,16},{4,20},{8,24},{12,28},{16,0},{20,4},{24,8},{28,12},{1,17},{... | collective-permute-start | bytes 1717256 | tf_op jit(solution)/shard_map/ppermute | solution.py:778
  865.7 31.1 %collective-permute-start.60 = (bf16[2,32,896]{2,1,0:T(8,128)(2,1)}, bf16[2,32,896]{2,1,0:T(8,128)(2,1)}, u32[]{:S(2)}, u32[]{:S(2)}) collective-permute-start(bf16[2,32,896]{2,1,0:T(8,128)(2,1)} %fusion.96), channel_id=1, source_target_pairs={{0,8},{4,12},{8,0},{12,4},{16,24},{20,28},{24,16},{28,20},{1,9},{5... | collective-permute-start | bytes 344072 | tf_op jit(solution)/shard_map/ppermute | solution.py:811
  869.8 23.3 %all-to-all-start.8 = ((f32[32,1,400]{2,1,0:T(1,128)}), f32[32,1,400]{2,1,0:T(1,128)S(1)}, u32[]{:S(2)}, u32[]{:S(2)}) async-start(f32[32,1,400]{2,1,0:T(1,128)} %broadcast_in_dim.560), calls=%async_computation.8 | async-start | bytes 131072 | tf_op jit(solution)/shard_map/all_to_all | solution.py:817
  912.8 101.6 %all-to-all-start.9 = ((bf16[32,32,896]{2,1,0:T(8,128)(2,1)}), bf16[32,32,896]{2,1,0:T(8,128)(2,1)S(1)}, u32[]{:S(2)}, u32[]{:S(2)}) async-start(bf16[32,32,896]{2,1,0:T(8,128)(2,1)} %broadcast_in_dim.566), calls=%async_computation.9 | async-start | bytes 3670016 | tf_op jit(solution)/shard_map/all_to_all | solution.py:817
  919.2 40.8 %collective-permute-start.55 = (bf16[2,144,800]{2,1,0:T(8,128)(2,1)S(1)}, bf16[2,144,800]{2,1,0:T(8,128)(2,1)S(1)}, u32[]{:S(2)}, u32[]{:S(2)}) collective-permute-start(bf16[2,144,800]{2,1,0:T(8,128)(2,1)S(1)} %dynamic-slice_bitcast_fusion.10), channel_id=1, source_target_pairs={{0,8},{4,12},{8,0},{12,4},{16,24},{20,28},{24,16},{28,20},{1,9},{5... | collective-permute-start | bytes 1382408 | tf_op jit(solution)/shard_map/ppermute | solution.py:778
  966.9 23.4 %collective-permute-start.64 = (bf16[2,200,800]{2,1,0:T(8,128)(2,1)}, bf16[2,200,800]{2,1,0:T(8,128)(2,1)}, u32[]{:S(2)}, u32[]{:S(2)}) collective-permute-start(bf16[2,200,800]{2,1,0:T(8,128)(2,1)} %dynamic-slice_bitcast_fusion.4), channel_id=1, source_target_pairs={{0,8},{4,12},{8,0},{12,4},{16,24},{20,28},{24,16},{28,20},{1,9},{5... | collective-permute-start | bytes 1920008 | tf_op jit(solution)/shard_map/ppermute | solution.py:778
  971.6 40.6 %collective-permute-start.58 = (bf16[2,200,800]{2,1,0:T(8,128)(2,1)}, bf16[2,200,800]{2,1,0:T(8,128)(2,1)}, u32[]{:S(2)}, u32[]{:S(2)}) collective-permute-start(bf16[2,200,800]{2,1,0:T(8,128)(2,1)} %dynamic-slice_bitcast_fusion.5), channel_id=1, source_target_pairs={{0,8},{4,12},{8,0},{12,4},{16,24},{20,28},{24,16},{28,20},{1,9},{5... | collective-permute-start | bytes 1920008 | tf_op jit(solution)/shard_map/ppermute | solution.py:778
  992.3 40.0 %collective-permute-start.65 = (bf16[200,800]{1,0:T(8,128)(2,1)}, bf16[200,800]{1,0:T(8,128)(2,1)}, u32[]{:S(2)}, u32[]{:S(2)}) collective-permute-start(bf16[200,800]{1,0:T(8,128)(2,1)} %dynamic-slice_bitcast_fusion.12), channel_id=1, source_target_pairs={{0,16},{4,20},{8,24},{12,28},{16,0},{20,4},{24,8},{28,12},{1,17},{... | collective-permute-start | bytes 960008 | tf_op jit(solution)/shard_map/ppermute | solution.py:778
  (197 other events, 1770.1 us)

commit v3 on v2

--- a/solution.py
+++ b/solution.py
@@ -443,6 +443,48 @@
     return run_tiles(handed_on, 1, [(values, whole)], [(values.shape, values.dtype, whole)], (), after)[0]
 
 
+def join_halves(place_ref, *refs):
+    pairs = len(refs) // 3
+    first = place_ref[0] == pl.program_id(0)
+    for mine, other, out in zip(refs[:pairs], refs[pairs : 2 * pairs], refs[2 * pairs :]):
+
+        @pl.when(first)
+        def _(source=mine, target=out):
+            target[...] = source[...]
+
+        @pl.when(jnp.logical_not(first))
+        def _(source=other, target=out):
+            target[...] = source[...]
+
+
+def joined_all(mine, other, place):
+    ins = [(place.reshape((1,)), pl.BlockSpec(memory_space=pltpu.SMEM))]
+    ins = ins + [(part, shared(part.shape)) for part in mine + other]
+    outs = [
+        ((2 * part.shape[0],) + part.shape[1:], part.dtype, banded(*part.shape)) for part in mine
+    ]
+    return run_tiles(join_halves, 2, ins, outs)
+
+
+def cut_rows(source_ref, target_ref):
+    rows = source_ref.shape[0] // target_ref.shape[0]
+    pad = target_ref.shape[1] - rows
+    values = source_ref[...].astype(jnp.float32)
+    for k in range(target_ref.shape[0]):
+        part = values[k * rows : (k + 1) * rows]
+        if pad:
+            part = jnp.concatenate([part, jnp.zeros((pad,) + part.shape[1:], jnp.float32)], axis=0)
+        target_ref[k] = part.astype(target_ref.dtype)
+
+
+def chunked(values, count):
+    rows = values.shape[0] // count
+    shape = (count, rows + -rows % 8) + values.shape[1:]
+    return run_tiles(
+        cut_rows, 1, [(values, shared(values.shape))], [(shape, values.dtype, shared(shape))]
+    )[0]
+
+
 class Mixer:
 
     def __init__(self, tokens, width, age, inner, tail, z, conv_w, conv_b, select_w, step_w, step_b, rates, skip, gain):
@@ -746,13 +788,13 @@
 
 class SeqSum:
 
-    def __init__(self, left, right, scale=1.0, flip=False, after=()):
+    def __init__(self, left, right, scale=1.0, flip=False, after=(), rows=None):
         self.count, self.place = lax.axis_size("seq"), lax.axis_index("seq")
         self.bits = self.count.bit_length() - 1
         self.right, self.scale, self.flip = right, scale, flip
-        self.rows = left.shape[0] // self.count
-        left = left.reshape((self.count, self.rows) + left.shape[1:])
-        left = jnp.pad(left, ((0, 0), (0, -self.rows % 8), (0, 0)))
+        if left.ndim == 2:
+            left = left.reshape((self.count, left.shape[0] // self.count) + left.shape[1:])
+        self.rows = rows or left.shape[1]
         self.left = left.reshape((2,) * self.bits + left.shape[1:])
         self.stage = 0
         self.send(low(self.product(self.half(self.left, True, after))))
@@ -977,10 +1019,11 @@
         rates, skip_g[None], mixer_g[None],
     )
     mixed_in, picked = mixer.first()
+    picked = picked + swapped(picked, "col")
     pairs = told(pair_own, GROUP)
     pair_group = jnp.concatenate(
         [
-            lax.dynamic_index_in_dim(pairs, i + nothing(mixed_in), 0, keepdims=False)
+            lax.dynamic_index_in_dim(pairs, i + nothing(picked), 0, keepdims=False)
             for i in range(pairs.shape[0])
         ],
         axis=1,
@@ -992,22 +1035,24 @@
     )
     meta_pair = meta_cache.transpose(0, 2, 1).reshape(2 * kv_width, META)
     pair_all = jnp.concatenate([meta_pair, window], axis=1)
-    selected = group_total(picked)
-    attn, log_totals = run_attention(query, pair_all[:kv_width], pair_all[kv_width:], mask, ())
-    end = mixer.totals(selected, (attn,))
+    selected = picked + swapped(picked, "row")
+    end = mixer.totals(selected, ())
+    attn, log_totals = run_attention(query, pair_all[:kv_width], pair_all[kv_width:], mask, (end,))
     ends = told(end, "seq")
     spans = ends[:, STATE, :]
     state_in = entering_state(ends[:, :STATE], spans, rates, False)
 
     attn_factor = lax.rsqrt(jnp.mean(attn * attn, axis=0, keepdims=True) + EPS)
-    attn_low = low(attn * attn_factor * attn_gain[:, None])
+    attn_low = low(attn * attn_factor * attn_gain[:, None] + wide(nothing(ends)))
     attn_part = lax.all_to_all(attn_low, GROUP, split_axis=0, concat_axis=1, tiled=True)
     attn_rows = col_joined(attn_part)
     grad_m = row_joined(grad_out.T)
+    seq_count = lax.axis_size("seq")
+    grad_chunks = chunked(grad_m, seq_count)
     down_t, mixer_out_t = down_weight.T, mixer_out_weight.T
-    dact = col_summed(over_rows(down_t, grad_m))
-
-    squares = mixer.outputs(state_in, (attn_rows, dact))
+    dact = col_summed(over_rows(down_t, held_until(grad_m, [end])))
+
+    squares = mixer.outputs(state_in, (attn_rows, dact, grad_chunks))
     mixer_factor = lax.rsqrt(group_total(squares) / DI + EPS)
     mixer_rows = col_joined(mixer.normed(mixer_factor, mixer_g)[:quarter])
 
@@ -1023,9 +1068,9 @@
     dgate_low = low(dact * up_act * sig_gate * (1.0 + gate_act * (1.0 - sig_gate)))
     dup_low = low(dact * gate_act * sig_gate)
     act_low = low(gate_act * sig_gate * up_act)
-    dgate_rows = col_joined(dgate_low)
-    dup_rows = col_joined(dup_low)
-    act_rows = col_joined(act_low)
+    ffn_low = [dgate_low, dup_low, act_low]
+    ffn_other = [swapped(part, "col") for part in ffn_low]
+    dgate_rows, dup_rows, act_rows = joined_all(ffn_low, ffn_other, col)
     dsecond_m = row_summed(dot_plain(gate_weight, dgate_rows) + dot_plain(up_weight, dup_rows))
     sum_gate = SeqSum(dgate_rows, second_m, 1.0, True)
     sum_up = SeqSum(dup_rows, second_m, 1.0, True)
@@ -1066,9 +1111,9 @@
     sum_gate.step(dquery)
     sum_up.step(sum_gate.now)
 
-    sum_down = SeqSum(grad_m, act_rows, 1.0, False, [adjoint_in])
+    sum_down = SeqSum(grad_chunks, act_rows, 1.0, False, [adjoint_in], grad_m.shape[0] // seq_count)
     both_rows = jnp.concatenate([attn_rows, mixer_rows], axis=0)
-    sum_out = SeqSum(low_m, both_rows, 0.5, False, [adjoint_in])
+    sum_out = SeqSum(chunked(low_m, seq_count), both_rows, 0.5, False, [adjoint_in], low_m.shape[0] // seq_count)
     side_step, drates, step_weight_part, dpicked = mixer.back_grads(
         adjoint_in,
         [sum_gate.now, sum_up.now, sum_down.sent, sum_out.sent],
@@ -1079,7 +1124,7 @@
         part.step(drates)
     dinner_own, edges, side_conv, select_part = mixer.last(
         group_total(dpicked),
-        [sum_gate.got, sum_up.got],
+        [],
     )
     held = wide(nothing(drates))
     dgroup = jnp.concatenate([dkey[:, META + reach :], dvalue[:, META + reach :]], axis=0)
@@ -1099,11 +1144,13 @@
     )
     dqkv_part = lax.all_to_all(dqkv_core, GROUP, split_axis=0, concat_axis=1, tiled=True)
     dqkv_rows = col_joined(dqkv_part)
-    sum_qkv = SeqSum(dqkv_rows, first_m)
+    sum_qkv = SeqSum(chunked(dqkv_rows, seq_count), first_m, 1.0, False, (), dqkv_rows.shape[0] // seq_count)
 
     lost = moved(edges[SUB - tail_rows : SUB], "seq", -1)
     ending = low(edges[2 * SUB - tail_rows :] + lost).T
-    dinner_own = lax.dynamic_update_slice(dinner_own, ending, (0, tokens - tail_rows))[:quarter]
+    dinner_own = lax.dynamic_update_slice(
+        dinner_own, ending, (nothing(*[part.got for part in sums]), tokens - tail_rows)
+    )[:quarter]
     dz_t = dz_own[:quarter]
     got_back = swapped(by_row(dz_t, dinner_own), "row")
     dnear = col_joined(by_row(dinner_own, got_back))
@@ -1111,38 +1158,49 @@
     dinner_rows = jnp.concatenate([dnear, dfar], axis=0)
     dchunks = dinner_rows.reshape(lax.axis_size("seq"), -1, tokens)
     cut = dchunks.shape[1] // 16 * 8
-    sum_out.step(select_part)
-    sum_down.step(select_part)
-    sums_in = [
-        SeqSum(dchunks[:, :cut].reshape(-1, tokens), first_m, 1.0, False, [sum_out.got]),
-        SeqSum(dchunks[:, cut:].reshape(-1, tokens), first_m),
-    ]
-    begun = [part.sent for part in sums_in]
     params = jnp.concatenate(
         [
             select_part,
             step_weight_part[:DT_RANK],
             drates,
             side_conv[: CONV + 1],
-            side_step[:1] + wide(nothing(*begun)),
+            side_step[:1],
             side_norm[:2],
         ],
         axis=0,
     )
-    params = seq_reduce(low(params))
-    params = wide(told(low(params), ALL))
     count = lax.axis_size("seq")
-    params = params.reshape((count, 4) + params.shape[1:])
+    shares = low(params).reshape((count, -1) + params.shape[1:])
+    shares = lax.all_to_all(shares, "seq", split_axis=0, concat_axis=0, tiled=True)
+    params = jnp.sum(wide(shares), axis=0)
+    spread_out = told(low(params), "seq")
+    spread_out = joined(spread_out, swapped(spread_out, "row"), row)
+    spread_out = joined(spread_out, swapped(spread_out, "col"), col)
+    spread_out = spread_out.reshape((2, 2, -1, lanes))
     params = jnp.concatenate(
-        [params[:, q].reshape(-1, lanes)[:, :quarter] for q in range(4)], axis=1
-    )
-
-    dqkv_late = lax.dynamic_slice_in_dim(dqkv_rows, nothing(*begun), dqkv_rows.shape[0], axis=0)
-    dfirst_part = dot_plain(qkv_weight, dqkv_late) + dot_plain(mixer_in_weight, dinner_rows)
-    first_sum = group_total(jnp.sum(dfirst_part * pre_g * hm, axis=0)) / D
+        [wide(spread_out[q % 2, q // 2][:, :quarter]) for q in range(4)], axis=1
+    )
 
     def block(values):
         return lax.dynamic_slice_in_dim(values, row * (half // 2), half // 2, axis=0)
+
+    gain_block = pre_gain.shape[0]
+    block_pos = (2 * col + row) * gain_block
+
+    def spread(part):
+        return lax.dynamic_update_slice(jnp.zeros((D,), jnp.float32), part, (block_pos,))
+
+    sums_in = [
+        SeqSum(dchunks[:, :cut].reshape(-1, tokens), first_m, 1.0, False, [spread_out]),
+        SeqSum(dchunks[:, cut:].reshape(-1, tokens), first_m),
+    ]
+    begun = [part.sent for part in sums_in]
+    sum_out.step(*begun)
+    sum_down.step(*begun)
+
+    dfirst_part = dot_plain(qkv_weight, dqkv_rows) + dot_plain(mixer_in_weight, dinner_rows)
+    dfirst_part = dfirst_part + wide(nothing(*begun))
+    first_sum = group_total(jnp.sum(dfirst_part * pre_g * hm, axis=0)) / D
 
     dfirst = row_scattered(dfirst_part)
     own_hidden = block(hm)
@@ -1152,19 +1210,19 @@
         - own_hidden * (pre_factor**3 * first_sum[None, :])
     )
     pre_part = jnp.sum(dfirst * own_hidden * pre_factor, axis=1)
-    act_late = lax.dynamic_slice_in_dim(act_rows, nothing(*begun), act_rows.shape[0], axis=0)
-    hidden_out = low(block(resid_m) + row_scattered(dot_plain(down_t, act_late)))
-
-    gain_block = pre_gain.shape[0]
-    block_pos = (2 * col + row) * gain_block
-
-    def spread(part):
-        return lax.dynamic_update_slice(jnp.zeros((D,), jnp.float32), part, (block_pos,))
-
+    out_part = dot_plain(down_t, act_rows) + wide(nothing(*begun))
+    hidden_out = low(block(resid_m) + row_scattered(out_part))
+
+
+    pre_parts = told(pre_part, ALL).reshape((count, 2, 2, gain_block))
+    pre_grad = jnp.sum(pre_parts, axis=0).transpose(1, 0, 2).reshape(-1)
+    out_grads = sum_out.finish(*begun)
+    sums_in[0].step(*begun)
+    sums_in[1].step(sums_in[0].now)
     early = all_total(
         jnp.concatenate(
             [
-                (dkey[:, :META] + wide(nothing(*begun))).reshape(-1),
+                (dkey[:, :META] + wide(nothing(sums_in[1].now))).reshape(-1),
                 dvalue[:, :META].reshape(-1),
                 attn_gain_part,
                 spread(block(post_part[:, None])[:, 0]),
@@ -1175,11 +1233,9 @@
     meta_grad = early[:meta_size].reshape(2, kv_width, META).transpose(0, 2, 1)
     attn_gain_grad = early[meta_size : meta_size + D]
     post_grad = early[meta_size + D :]
-    pre_parts = told(pre_part, ALL).reshape((count, 2, 2, gain_block))
-    pre_grad = jnp.sum(pre_parts, axis=0).transpose(1, 0, 2).reshape(-1)
-    out_grads = sum_out.finish(*begun)
-    for part in sums_in + sums_in + [sum_qkv]:
-        part.step(*begun)
+    sums_in[0].step(sums_in[1].now)
+    sums_in[1].step(sums_in[0].now)
+    sum_qkv.step(sums_in[1].now)
     ranks = DT_RANK + 2 * STATE
     at_rates = ranks + DT_RANK
     at_conv = at_rates + STATE

time: 1050 us -> 984 us (0.937)
  waiting for transfers between devices: 282 us -> 212 us
  Pallas kernels: 211 us -> 235 us
  local copies, waits for them, and re-layouts: 169 us -> 149 us
  other arithmetic: 141 us -> 128 us
  starting transfers between devices: 132 us -> 143 us
    ppermute x3 -> x0, waiting for transfers between devices: 51.8 us -> none  [seq_reduce(): parts = mine + wide(lax.ppermute(low(away), 'seq', route))]
    all_to_all x0 -> x1, starting transfers between devices: none -> 28.2 us  [shards(): lax.all_to_all(shares, 'seq', split_axis=0, concat_axis=0, tiled=True)]
    pallas_call x11 -> x16, Pallas kernels: 211 us -> 235 us  [run_tiles(): pl.pallas_call(kernel, grid=(steps,), in_specs=specs, out_specs=[spec for...]
    all_to_all x6, waiting for transfers between devices: 23.9 us -> 0.02 us  [told(): lax.all_to_all(jnp.broadcast_to(values[None], (count,) + values.shape), a...]
    select_n x10 -> x8, other arithmetic: 26.7 us -> 7.69 us  [joined(): both = jnp.where(which == place, mine[None], other[None])]
    broadcast_in_dim x28 -> x16, local copies, waits for them, and re-layouts: 35 us -> 19.8 us  [joined(): both = jnp.where(which == place, mine[None], other[None])]
    ppermute x21, waiting for transfers between devices: 128 us -> 115 us  [send(): self.got = straight(lax.ppermute(self.sent, 'seq', route))]
    all_to_all x6, starting transfers between devices: 36.6 us -> 25.4 us  [told(): lax.all_to_all(jnp.broadcast_to(values[None], (count,) + values.shape), a...]
  transfers between devices with their start and end apart: 80 -> 80, of which waited for: 30 -> 31; matrix products, arithmetic and copies ran while one was open for 34% -> 33% of each run, Pallas kernels for 17% -> 19%
where the time goes in v3:
time: 984 us; the launch traced here: 970 us
  Pallas kernels  235 us (24%)
  waiting for transfers between devices  212 us (22%)
  local copies, waits for them, and re-layouts  149 us (15%)
  starting transfers between devices  143 us (15%)
  other arithmetic  128 us (13%)
  matrix products  90.4 us (9%)
  between operations  13.5 us (1%)
    pallas_call x16, Pallas kernels, run_tiles(): pl.pallas_call(kernel, grid=(steps,), in_specs=specs, out_specs=[spec for...  235 us
    ppermute x21, waiting for transfers between devices, send(): self.got = straight(lax.ppermute(self.sent, 'seq', route))  115 us
    ppermute x40, waiting for transfers between devices, swapped(): return straight(lax.ppermute(straight(values), axis, [(0, 1), (1, 0)]))  78.5 us
    dot_general x14, matrix products, product(): lax.dot_general(*operands, (dims, ((), ())), preferred_element_type=jnp.f...  44.2 us
    convert_element_type x20, other arithmetic, low(): return values.astype(jnp.bfloat16)  30.3 us
    all_to_all x1, starting transfers between devices, shards(): lax.all_to_all(shares, 'seq', split_axis=0, concat_axis=0, tiled=True)  28.2 us
    ppermute x21, starting transfers between devices, send(): self.got = straight(lax.ppermute(self.sent, 'seq', route))  27.6 us
    all_to_all x6, starting transfers between devices, told(): lax.all_to_all(jnp.broadcast_to(values[None], (count,) + values.shape), a...  25.4 us
  transfers between devices with their start and end apart: 80, of which 31 were waited for; matrix products, arithmetic and copies ran while one was open for 33% of the time, Pallas kernels for 19%

profile of v3, /device:TPU:0, one launch (start us, length us, event | category | flops | bytes accessed | tf_op | source)
XLA Modules:
  0.0 970.5 jit_solution(15623553413574493605)
XLA Ops:
  36.8 6.1 convolution_bitcast_fusion
  52.4 4.4 all-to-all-start
  68.5 15.3 %collective-permute-done.6 = bf16[800,512]{1,0:T(8,128)(2,1)} collective-permute-done((bf16[800,512]{1,0:T(8,128)(2,1)}, bf16[800,512]{1,0:T(8,128)(2,1)}, u32[]{:S(2)}, u32[]{:S(2)}) %collective-permute-start.6) | collective-permute-done | bytes 819232 | tf_op jit(solution)/shard_map/ppermute | solution.py:747
  83.8 3.9 broadcast_select_fusion.5
  89.6 4.2 collective-permute-start.7
  94.7 4.2 all-to-all-start.1
  107.5 8.2 shard_map.373
  140.8 6.2 collective-permute-start.9
  152.5 24.4 %shard_map.374 = (f32[512,896]{1,0:T(8,128)}, f32[512,896]{1,0:T(8,128)}, f32[24,896]{1,0:T(8,128)}, f32[7,16,8,128]{3,2,1,0:T(8,128)}, f32[8,896]{1,0:T(8,128)}) custom-call(f32[512,132]{1,0:T(8,128)} %add.705.refs_0_.refs_3_.refs_9_.refs_4_, f32[512,896]{1,0:T(8,128)} %get-tuple-element.55.refs_1_.refs_6_.refs_8_, ...), custom_call_target="tpu_custom_call" | custom-call | flops 1024 | bytes 1024 | tf_op jit(solution)/shard_map/pallas_call | solution.py:423
  179.9 4.2 all-to-all-start.2
  184.1 5.3 fusion.161
  196.8 13.3 %shard_map.375 = (f32[1600,128]{1,0:T(8,128)}, f32[5,8,128]{2,1,0:T(8,128)}) custom-call(bf16[1600,128]{1,0:T(8,128)(2,1)} %bitcast.623, bf16[320,1280]{1,0:T(8,128)(2,1)} %get-tuple-element.133.refs_1_, bf16[320,1280]{1,0:T(8,128)(2,1)} %get-tuple-element.132.refs_2_, f32[1280,128]{1,0:T(8,128)} %pad_select_fusion.refs_3_, ...), custom_call_target="tpu_custom_call" | custom-call | flops 1024 | bytes 1024 | tf_op jit(solution)/shard_map/pallas_call | solution.py:423
  216.6 4.1 all-to-all-start.3
  224.1 4.3 all-to-all-done.3
  229.5 4.2 bitcast_add_fusion.4.refs_11_
  234.8 28.3 %shard_map.378 = (f32[512,896]{1,0:T(8,128)}, f32[512,896]{1,0:T(8,128)}, f32[8,512]{1,0:T(8,128)}, f32[7,1040,8,128]{3,2,1,0:T(8,128)}) custom-call(f32[512,896]{1,0:T(8,128)} %get-tuple-element.58.refs_0_.refs_7_, f32[512,896]{1,0:T(8,128)} %get-tuple-element.55.refs_1_.refs_6_.refs_8_, f32[512,128]{1,0:T(8,128)} %broadcast_in_dim.440.refs_2_.refs_8_, ...), custom_call_target="tpu_custom_call" | custom-call | flops 1024 | bytes 1024 | tf_op jit(solution)/shard_map/pallas_call | solution.py:423
  269.9 13.7 %shard_map.379 = bf16[896,512]{1,0:T(8,128)(2,1)} custom-call(f32[512,896]{1,0:T(8,128)} %get-tuple-element.61.refs_0_, f32[8,512]{1,0:T(8,128)} %broadcast_in_dim.462.refs_1_, f32[896,1]{1,0:T(8,128)} %broadcast_in_dim.509.refs_2_), custom_call_target="tpu_custom_call" | custom-call | flops 1024 | bytes 1024 | tf_op jit(solution)/shard_map/pallas_call | solution.py:423
  293.9 19.9 %collective-permute-done.18 = bf16[800,512]{1,0:T(8,128)(2,1)S(1)} collective-permute-done((bf16[800,512]{1,0:T(8,128)(2,1)S(1)}, bf16[800,512]{1,0:T(8,128)(2,1)S(1)}, u32[]{:S(2)}, u32[]{:S(2)}) %collective-permute-start.18) | collective-permute-done | bytes 819232 | tf_op jit(solution)/shard_map/ppermute | solution.py:747
  336.8 7.3 shard_map.380
  344.2 5.8 fusion.166
  364.9 9.4 collective-permute-done.25
  376.9 4.4 convert_bitcast_fusion.1.refs_12_
  396.4 4.3 convert_bitcast_fusion.refs_13_
  407.2 5.6 shard_map.381
  419.0 23.6 %shard_map.382 = (f32[512,896]{1,0:T(8,128)}, bf16[896,512]{1,0:T(8,128)(2,1)}, f32[8,896]{1,0:T(8,128)}, f32[16,896]{1,0:T(8,128)}, f32[7,16,8,128]{3,2,1,0:T(8,128)}) custom-call(f32[512,896]{1,0:T(8,128)} %get-tuple-element.61.refs_0_, bf16[896,512]{1,0:T(8,128)(2,1)} %pad.65.refs_1_, f32[1,896]{1,0:T(1,128)} %broadcast_in_dim.468.refs_2_, ...), custom_call_target="tpu_custom_call" | custom-call | flops 1024 | bytes 1024 | tf_op jit(solution)/shard_map/pallas_call | solution.py:423
  444.2 5.8 all-to-all-start.4
  450.7 17.3 %shard_map.383 = (f32[1600,128]{1,0:T(8,128)}, f32[320,1664]{1,0:T(8,128)}, f32[320,1664]{1,0:T(8,128)}) custom-call(bf16[1600,128]{1,0:T(8,128)(2,1)} %bitcast.624, bf16[320,1280]{1,0:T(8,128)(2,1)} %get-tuple-element.133.refs_1_, bf16[320,1280]{1,0:T(8,128)(2,1)} %get-tuple-element.132.refs_2_, f32[1280,128]{1,0:T(8,128)} %pad_select_fusion.refs_3_, ...), custom_call_target="tpu_custom_call" | custom-call | flops 1024 | bytes 1024 | tf_op jit(solution)/shard_map/pallas_call | solution.py:423
  478.2 16.0 %collective-permute-done.32 = bf16[2,2,800,344]{3,2,1,0:T(8,128)(2,1)} collective-permute-done((bf16[2,2,800,344]{3,2,1,0:T(8,128)(2,1)}, bf16[2,2,800,344]{3,2,1,0:T(8,128)(2,1)}, u32[]{:S(2)}, u32[]{:S(2)}) %collective-permute-start.32) | collective-permute-done | bytes 2201632 | tf_op jit(solution)/shard_map/ppermute | solution.py:820
  503.9 4.8 convolution_convert_fusion.refs_15_
  518.2 71.0 %shard_map.385 = (f32[512,896]{1,0:T(8,128)}, f32[8,896]{1,0:T(8,128)}, f32[16,896]{1,0:T(8,128)}, f32[132,896]{1,0:T(8,128)}, f32[512,132]{1,0:T(8,128)}) custom-call(f32[512,896]{1,0:T(8,128)} %get-tuple-element.58.refs_0_.refs_7_, f32[512,896]{1,0:T(8,128)} %get-tuple-element.55.refs_1_.refs_6_.refs_8_, f32[512,128]{1,0:T(8,128)} %broadcast_in_dim.440.refs_2_.refs_8_, ...), custom_call_target="tpu_custom_call" | custom-call | flops 1024 | bytes 1024 | tf_op jit(solution)/shard_map/pallas_call | solution.py:423
  599.6 6.6 collective-permute-done.36.refs_4_
  616.4 11.1 %collective-permute-done.38 = f32[512,132]{1,0:T(8,128)S(1)} collective-permute-done((f32[512,132]{1,0:T(8,128)S(1)}, f32[512,132]{1,0:T(8,128)S(1)}, u32[]{:S(2)}, u32[]{:S(2)}) %collective-permute-start.38) | collective-permute-done | bytes 270368 | tf_op jit(solution)/shard_map/ppermute | solution.py:747
  628.4 10.9 %shard_map.387 = (bf16[896,512]{1,0:T(8,128)(2,1)}, f32[16,896]{1,0:T(8,128)}, f32[8,896]{1,0:T(8,128)}, f32[132,896]{1,0:T(8,128)}) custom-call(bf16[896,512]{1,0:T(8,128)(2,1)} %pad.53.refs_0_, f32[8,896]{1,0:T(8,128)} %pad.54.clone.refs_1_, f32[512,128]{1,0:T(8,128)} %broadcast_in_dim.440.refs_2_.refs_8_, f32[4,896]{1,0:T(4,128)} %pad.55.refs_3_, ...), custom_call_target="tpu_custom_call" | custom-call | flops 1024 | bytes 1024 | tf_op jit(solution)/shard_map/pallas_call | solution.py:423
  649.9 4.5 concatenate.80
  662.7 28.2 %all-to-all-start.6 = ((bf16[8,32,896]{2,1,0:T(8,128)(2,1)}), bf16[8,32,896]{2,1,0:T(8,128)(2,1)}, u32[]{:S(2)}, u32[]{:S(2)}) async-start(bf16[8,32,896]{2,1,0:T(8,128)(2,1)} %bitcast.630), calls=%async_computation.6 | async-start | bytes 917504 | tf_op jit(solution)/shard_map/all_to_all | solution.py:1174
  693.0 8.5 all-to-all-done.6
  744.5 5.7 collective-permute-done.43
  750.5 4.1 fusion.151
  764.2 4.7 concatenate.89
  790.0 4.9 convolution_add_fusion
  823.1 23.7 %collective-permute-done.62 = bf16[104,2400]{1,0:T(8,128)(2,1)} collective-permute-done((bf16[104,2400]{1,0:T(8,128)(2,1)}, bf16[104,2400]{1,0:T(8,128)(2,1)}, u32[]{:S(2)}, u32[]{:S(2)}) %collective-permute-start.62) | collective-permute-done | bytes 499232 | tf_op jit(solution)/shard_map/ppermute | solution.py:820
  850.8 9.1 collective-permute-done.66
  880.2 4.0 all-to-all-start.11
  884.2 26.7 %collective-permute-done.54 = bf16[2,200,800]{2,1,0:T(8,128)(2,1)S(1)} collective-permute-done((bf16[2,200,800]{2,1,0:T(8,128)(2,1)}, bf16[2,200,800]{2,1,0:T(8,128)(2,1)S(1)}, u32[]{:S(2)}, u32[]{:S(2)}) %collective-permute-start.54) | collective-permute-done | bytes 640032 | tf_op jit(solution)/shard_map/ppermute | solution.py:820
  925.2 4.5 all-to-all-start.12
  929.7 11.5 %collective-permute-done.60 = bf16[200,800]{1,0:T(8,128)(2,1)} collective-permute-done((bf16[200,800]{1,0:T(8,128)(2,1)}, bf16[200,800]{1,0:T(8,128)(2,1)}, u32[]{:S(2)}, u32[]{:S(2)}) %collective-permute-start.60) | collective-permute-done | bytes 320032 | tf_op jit(solution)/shard_map/ppermute | solution.py:820
  942.2 10.2 %collective-permute-done.59 = bf16[200,800]{1,0:T(8,128)(2,1)} collective-permute-done((bf16[200,800]{1,0:T(8,128)(2,1)}, bf16[200,800]{1,0:T(8,128)(2,1)}, u32[]{:S(2)}, u32[]{:S(2)}) %collective-permute-start.59) | collective-permute-done | bytes 320032 | tf_op jit(solution)/shard_map/ppermute | solution.py:820
  961.1 7.1 collective-permute-done.58
  (764 shorter events, 421.4 us)
Async XLA Ops:
  2.4 25.9 %collective-permute-start.2 = (f32[400,2]{1,0:T(8,128)}, f32[400,2]{1,0:T(8,128)}, u32[]{:S(2)}, u32[]{:S(2)}) collective-permute-start(f32[400,2]{1,0:T(8,128)} %copy.184), channel_id=1, source_target_pairs={{0,2},{2,0},{1,3},{3,1},{4,6},{6,4},{5,7},{7,5},{8,10},{10,8},{9,1... | collective-permute-start | bytes 9608 | tf_op jit(solution)/shard_map/ppermute | solution.py:747
  5.3 28.0 %collective-permute-start = (bf16[400,512]{1,0:T(8,128)(2,1)}, bf16[400,512]{1,0:T(8,128)(2,1)S(1)}, u32[]{:S(2)}, u32[]{:S(2)}) collective-permute-start(bf16[400,512]{1,0:T(8,128)(2,1)} %bitcast.616), channel_id=1, source_target_pairs={{0,2},{2,0},{1,3},{3,1},{4,6},{6,4},{5,7},{7,5},{8,10},{10,8},{9,1... | collective-permute-start | bytes 1228808 | tf_op jit(solution)/shard_map/ppermute | solution.py:747
  5.4 117.9 %collective-permute-start.13 = (bf16[400,512]{1,0:T(8,128)(2,1)}, bf16[400,512]{1,0:T(8,128)(2,1)}, u32[]{:S(2)}, u32[]{:S(2)}) collective-permute-start(bf16[400,512]{1,0:T(8,128)(2,1)} %bitcast.652), channel_id=1, source_target_pairs={{0,2},{2,0},{1,3},{3,1},{4,6},{6,4},{5,7},{7,5},{8,10},{10,8},{9,1... | collective-permute-start | bytes 1228808 | tf_op jit(solution)/shard_map/ppermute | solution.py:747
  51.5 17.0 %collective-permute-start.4 = (bf16[800,512]{1,0:T(8,128)(2,1)}, bf16[800,512]{1,0:T(8,128)(2,1)}, u32[]{:S(2)}, u32[]{:S(2)}) collective-permute-start(bf16[800,512]{1,0:T(8,128)(2,1)} %get-tuple-element.114), channel_id=1, source_target_pairs={{0,1},{1,0},{2,3},{3,2},{4,5},{5,4},{6,7},{7,6},{8,9},{9,8},{10,11... | collective-permute-start | bytes 2457608 | tf_op jit(solution)/shard_map/ppermute | solution.py:747
  52.4 14.3 %all-to-all-start = ((bf16[560,4,128]{2,0,1:T(8,128)(2,1)}), bf16[560,4,128]{2,0,1:T(8,128)(2,1)}, u32[]{:S(2)}, u32[]{:S(2)}) async-start(bf16[560,4,128]{2,0,1:T(8,128)(2,1)} %copy_bitcast_fusion.2), calls=%async_computation | async-start | bytes 1146880 | tf_op jit(solution)/shard_map/all_to_all | solution.py:962
  60.6 23.2 %collective-permute-start.6 = (bf16[800,512]{1,0:T(8,128)(2,1)}, bf16[800,512]{1,0:T(8,128)(2,1)}, u32[]{:S(2)}, u32[]{:S(2)}) collective-permute-start(bf16[800,512]{1,0:T(8,128)(2,1)} %add_convert_fusion.6), channel_id=1, source_target_pairs={{0,2},{2,0},{1,3},{3,1},{4,6},{6,4},{5,7},{7,5},{8,10},{10,8},{9,1... | collective-permute-start | bytes 2457608 | tf_op jit(solution)/shard_map/ppermute | solution.py:747
  94.7 43.3 %all-to-all-start.1 = ((bf16[4,640,128]{2,1,0:T(8,128)(2,1)}), bf16[4,640,128]{2,1,0:T(8,128)(2,1)}, u32[]{:S(2)}, u32[]{:S(2)}) async-start(bf16[4,640,128]{2,1,0:T(8,128)(2,1)} %broadcast_in_dim.439), calls=%async_computation.1 | async-start | bytes 1310720 | tf_op jit(solution)/shard_map/all_to_all | solution.py:859
  115.7 14.4 %collective-permute-start.8 = (f32[512,132]{1,0:T(8,128)}, f32[512,132]{1,0:T(8,128)}, u32[]{:S(2)}, u32[]{:S(2)}) collective-permute-start(f32[512,132]{1,0:T(8,128)} %get-tuple-element.54), channel_id=1, source_target_pairs={{0,1},{1,0},{2,3},{3,2},{4,5},{5,4},{6,7},{7,6},{8,9},{9,8},{10,11... | collective-permute-start | bytes 811016 | tf_op jit(solution)/shard_map/ppermute | solution.py:747
  132.8 17.6 %collective-permute-start.11 = (f32[512,132]{1,0:T(8,128)}, f32[512,132]{1,0:T(8,128)}, u32[]{:S(2)}, u32[]{:S(2)}) collective-permute-start(f32[512,132]{1,0:T(8,128)} %add.694), channel_id=1, source_target_pairs={{0,2},{2,0},{1,3},{3,1},{4,6},{6,4},{5,7},{7,5},{8,10},{10,8},{9,1... | collective-permute-start | bytes 811016 | tf_op jit(solution)/shard_map/ppermute | solution.py:747
  140.8 50.2 %collective-permute-start.9 = (bf16[640,512]{1,0:T(8,128)(2,1)}, bf16[640,512]{1,0:T(8,128)(2,1)}, u32[]{:S(2)}, u32[]{:S(2)}) collective-permute-start(bf16[640,512]{1,0:T(8,128)(2,1)} %pad_maximum_fusion.2), channel_id=1, source_target_pairs={{0,8},{4,12},{8,16},{12,20},{16,24},{20,28},{1,9},{5,13},{9,17},{1... | collective-permute-start | bytes 1966088 | tf_op jit(solution)/shard_map/ppermute | solution.py:753
  147.0 46.2 %collective-permute-start.10 = (bf16[640,512]{1,0:T(8,128)(2,1)}, bf16[640,512]{1,0:T(8,128)(2,1)}, u32[]{:S(2)}, u32[]{:S(2)}) collective-permute-start(bf16[640,512]{1,0:T(8,128)(2,1)} %pad_maximum_fusion.2), channel_id=1, source_target_pairs={{0,4},{4,8},{8,12},{12,16},{16,20},{20,24},{24,28},{1,5},{5,9},{9,... | collective-permute-start | bytes 1966088 | tf_op jit(solution)/shard_map/ppermute | solution.py:753
  179.9 32.6 %all-to-all-start.2 = ((f32[8,24,896]{2,1,0:T(8,128)}), f32[8,24,896]{2,1,0:T(8,128)}, u32[]{:S(2)}, u32[]{:S(2)}) async-start(f32[8,24,896]{2,1,0:T(8,128)} %broadcast_in_dim.447), calls=%async_computation.2 | async-start | bytes 1376256 | tf_op jit(solution)/shard_map/all_to_all | solution.py:859
  190.9 38.6 %collective-permute-start.14 = (bf16[1376,512]{1,0:T(8,128)(2,1)}, bf16[1376,512]{1,0:T(8,128)(2,1)}, u32[]{:S(2)}, u32[]{:S(2)}) collective-permute-start(bf16[1376,512]{1,0:T(8,128)(2,1)} %fusion.18), channel_id=1, source_target_pairs={{0,1},{1,0},{2,3},{3,2},{4,5},{5,4},{6,7},{7,6},{8,9},{9,8},{10,11... | collective-permute-start | bytes 4227080 | tf_op jit(solution)/shard_map/ppermute | solution.py:747
  293.4 20.3 %collective-permute-start.18 = (bf16[800,512]{1,0:T(8,128)(2,1)S(1)}, bf16[800,512]{1,0:T(8,128)(2,1)S(1)}, u32[]{:S(2)}, u32[]{:S(2)}) collective-permute-start(bf16[800,512]{1,0:T(8,128)(2,1)S(1)} %fusion.34), channel_id=1, source_target_pairs={{0,2},{2,0},{1,3},{3,1},{4,6},{6,4},{5,7},{7,5},{8,10},{10,8},{9,1... | collective-permute-start | bytes 2457608 | tf_op jit(solution)/shard_map/ppermute | solution.py:747
  353.4 20.8 %collective-permute-start.25 = (bf16[800,512]{1,0:T(8,128)(2,1)}, bf16[800,512]{1,0:T(8,128)(2,1)}, u32[]{:S(2)}, u32[]{:S(2)}) collective-permute-start(bf16[800,512]{1,0:T(8,128)(2,1)} %fusion.35), channel_id=1, source_target_pairs={{0,2},{2,0},{1,3},{3,1},{4,6},{6,4},{5,7},{7,5},{8,10},{10,8},{9,1... | collective-permute-start | bytes 2457608 | tf_op jit(solution)/shard_map/ppermute | solution.py:747
  381.3 69.4 %collective-permute-start.31 = (bf16[2,2,800,344]{3,2,1,0:T(8,128)(2,1)}, bf16[2,2,800,344]{3,2,1,0:T(8,128)(2,1)}, u32[]{:S(2)}, u32[]{:S(2)}) collective-permute-start(bf16[2,2,800,344]{3,2,1,0:T(8,128)(2,1)} %convert_bitcast_fusion.1.refs_12_), channel_id=1, source_target_pairs={{0,4},{4,0},{8,12},{12,8},{16,20},{20,16},{24,28},{28,24},{1,5},{5... | collective-permute-start | bytes 6604808 | tf_op jit(solution)/shard_map/ppermute | solution.py:820
  400.6 93.6 %collective-permute-start.32 = (bf16[2,2,800,344]{3,2,1,0:T(8,128)(2,1)}, bf16[2,2,800,344]{3,2,1,0:T(8,128)(2,1)}, u32[]{:S(2)}, u32[]{:S(2)}) collective-permute-start(bf16[2,2,800,344]{3,2,1,0:T(8,128)(2,1)} %convert_bitcast_fusion.refs_13_), channel_id=1, source_target_pairs={{0,4},{4,0},{8,12},{12,8},{16,20},{20,16},{24,28},{28,24},{1,5},{5... | collective-permute-start | bytes 6604808 | tf_op jit(solution)/shard_map/ppermute | solution.py:820
  444.2 57.3 %all-to-all-start.4 = ((f32[8,16,896]{2,1,0:T(8,128)}), f32[8,16,896]{2,1,0:T(8,128)}, u32[]{:S(2)}, u32[]{:S(2)}) async-start(f32[8,16,896]{2,1,0:T(8,128)} %broadcast_in_dim.472), calls=%async_computation.4 | async-start | bytes 917504 | tf_op jit(solution)/shard_map/all_to_all | solution.py:859
  476.2 121.9 %collective-permute-start.33 = (bf16[2,800,344]{2,1,0:T(8,128)(2,1)}, bf16[2,800,344]{2,1,0:T(8,128)(2,1)}, u32[]{:S(2)}, u32[]{:S(2)}) collective-permute-start(bf16[2,800,344]{2,1,0:T(8,128)(2,1)} %dynamic-slice_bitcast_fusion.1), channel_id=1, source_target_pairs={{0,8},{4,12},{8,0},{12,4},{16,24},{20,28},{24,16},{28,20},{1,9},{5... | collective-permute-start | bytes 3302408 | tf_op jit(solution)/shard_map/ppermute | solution.py:820
  499.4 100.2 %collective-permute-start.34 = (bf16[2,800,344]{2,1,0:T(8,128)(2,1)}, bf16[2,800,344]{2,1,0:T(8,128)(2,1)S(1)}, u32[]{:S(2)}, u32[]{:S(2)}) collective-permute-start(bf16[2,800,344]{2,1,0:T(8,128)(2,1)} %dynamic-slice_bitcast_fusion), channel_id=1, source_target_pairs={{0,8},{4,12},{8,0},{12,4},{16,24},{20,28},{24,16},{28,20},{1,9},{5... | collective-permute-start | bytes 3302408 | tf_op jit(solution)/shard_map/ppermute | solution.py:820
  508.7 97.5 %collective-permute-start.35 = (bf16[2,2,104,2752]{3,2,1,0:T(8,128)(2,1)}, bf16[2,2,104,2752]{3,2,1,0:T(8,128)(2,1)}, u32[]{:S(2)}, u32[]{:S(2)}) collective-permute-start(bf16[2,2,104,2752]{3,2,1,0:T(8,128)(2,1)} %convolution_convert_fusion.refs_15_), channel_id=1, source_target_pairs={{0,4},{4,0},{8,12},{12,8},{16,20},{20,16},{24,28},{28,24},{1,5},{5... | collective-permute-start | bytes 6869000 | tf_op jit(solution)/shard_map/ppermute | solution.py:820
  512.8 93.4 %collective-permute-start.36 = (bf16[2,2,104,2400]{3,2,1,0:T(8,128)(2,1)}, bf16[2,2,104,2400]{3,2,1,0:T(8,128)(2,1)}, u32[]{:S(2)}, u32[]{:S(2)}) collective-permute-start(bf16[2,2,104,2400]{3,2,1,0:T(8,128)(2,1)} %fusion.2.refs_16_), channel_id=1, source_target_pairs={{0,4},{4,0},{8,12},{12,8},{16,20},{20,16},{24,28},{28,24},{1,5},{5... | collective-permute-start | bytes 5990408 | tf_op jit(solution)/shard_map/ppermute | solution.py:820
  596.6 46.6 %collective-permute-start.47 = (bf16[640,512]{1,0:T(8,128)(2,1)}, bf16[640,512]{1,0:T(8,128)(2,1)}, u32[]{:S(2)}, u32[]{:S(2)}) collective-permute-start(bf16[640,512]{1,0:T(8,128)(2,1)} %fusion.33), channel_id=1, source_target_pairs={{8,0},{12,4},{16,8},{20,12},{24,16},{28,20},{9,1},{13,5},{17,9},{2... | collective-permute-start | bytes 1966088 | tf_op jit(solution)/shard_map/ppermute | solution.py:753
  598.1 45.1 %collective-permute-start.46 = (bf16[640,512]{1,0:T(8,128)(2,1)S(1)}, bf16[640,512]{1,0:T(8,128)(2,1)S(1)}, u32[]{:S(2)}, u32[]{:S(2)}) collective-permute-start(bf16[640,512]{1,0:T(8,128)(2,1)S(1)} %fusion.32), channel_id=1, source_target_pairs={{4,0},{8,4},{12,8},{16,12},{20,16},{24,20},{28,24},{5,1},{9,5},{13... | collective-permute-start | bytes 1966088 | tf_op jit(solution)/shard_map/ppermute | solution.py:753
  610.9 176.3 %collective-permute-start.63 = (bf16[800,344]{1,0:T(8,128)(2,1)}, bf16[800,344]{1,0:T(8,128)(2,1)}, u32[]{:S(2)}, u32[]{:S(2)}) collective-permute-start(bf16[800,344]{1,0:T(8,128)(2,1)} %dynamic-slice_bitcast_fusion.7), channel_id=1, source_target_pairs={{0,16},{4,20},{8,24},{12,28},{16,0},{20,4},{24,8},{28,12},{1,17},{... | collective-permute-start | bytes 1651208 | tf_op jit(solution)/shard_map/ppermute | solution.py:820
  615.4 179.4 %collective-permute-start.64 = (bf16[800,344]{1,0:T(8,128)(2,1)}, bf16[800,344]{1,0:T(8,128)(2,1)}, u32[]{:S(2)}, u32[]{:S(2)}) collective-permute-start(bf16[800,344]{1,0:T(8,128)(2,1)} %dynamic-slice_bitcast_fusion.6), channel_id=1, source_target_pairs={{0,16},{4,20},{8,24},{12,28},{16,0},{20,4},{24,8},{28,12},{1,17},{... | collective-permute-start | bytes 1651208 | tf_op jit(solution)/shard_map/ppermute | solution.py:820
  640.1 14.4 %collective-permute-start.39 = (f32[3,896]{1,0:T(4,128)S(1)}, f32[3,896]{1,0:T(4,128)S(1)}, u32[]{:S(2)}, u32[]{:S(2)}) collective-permute-start(f32[3,896]{1,0:T(4,128)S(1)} %slice.501), channel_id=1, source_target_pairs={{4,0},{8,4},{12,8},{16,12},{20,16},{24,20},{28,24},{5,1},{9,5},{13... | collective-permute-start | bytes 32264 | tf_op jit(solution)/shard_map/ppermute | solution.py:753
  646.3 16.4 %all-to-all-start.8 = ((bf16[640,4,128]{2,0,1:T(8,128)(2,1)}), bf16[640,4,128]{2,0,1:T(8,128)(2,1)S(1)}, u32[]{:S(2)}, u32[]{:S(2)}) async-start(bf16[640,4,128]{2,0,1:T(8,128)(2,1)} %copy_bitcast_fusion), calls=%async_computation.8 | async-start | bytes 1310720 | tf_op jit(solution)/shard_map/all_to_all | solution.py:1136
  660.7 59.5 %collective-permute-start.40 = (bf16[800,512]{1,0:T(8,128)(2,1)}, bf16[800,512]{1,0:T(8,128)(2,1)}, u32[]{:S(2)}, u32[]{:S(2)}) collective-permute-start(bf16[800,512]{1,0:T(8,128)(2,1)} %broadcast_select_fusion.4), channel_id=1, source_target_pairs={{0,2},{2,0},{1,3},{3,1},{4,6},{6,4},{5,7},{7,5},{8,10},{10,8},{9,1... | collective-permute-start | bytes 2457608 | tf_op jit(solution)/shard_map/ppermute | solution.py:747
  662.7 38.8 %all-to-all-start.6 = ((bf16[8,32,896]{2,1,0:T(8,128)(2,1)}), bf16[8,32,896]{2,1,0:T(8,128)(2,1)}, u32[]{:S(2)}, u32[]{:S(2)}) async-start(bf16[8,32,896]{2,1,0:T(8,128)(2,1)} %bitcast.630), calls=%async_computation.6 | async-start | bytes 917504 | tf_op jit(solution)/shard_map/all_to_all | solution.py:1174
  715.3 22.4 %all-to-all-start.7 = ((bf16[8,32,896]{2,1,0:T(8,128)(2,1)}), bf16[8,32,896]{2,1,0:T(8,128)(2,1)S(1)}, u32[]{:S(2)}, u32[]{:S(2)}) async-start(bf16[8,32,896]{2,1,0:T(8,128)(2,1)} %broadcast_in_dim.483), calls=%async_computation.7 | async-start | bytes 917504 | tf_op jit(solution)/shard_map/all_to_all | solution.py:859
  723.3 14.4 %collective-permute-start.42 = (bf16[800,512]{1,0:T(8,128)(2,1)}, bf16[800,512]{1,0:T(8,128)(2,1)}, u32[]{:S(2)}, u32[]{:S(2)}) collective-permute-start(bf16[800,512]{1,0:T(8,128)(2,1)} %get-tuple-element.144), channel_id=1, source_target_pairs={{0,1},{1,0},{2,3},{3,2},{4,5},{5,4},{6,7},{7,6},{8,9},{9,8},{10,11... | collective-permute-start | bytes 2457608 | tf_op jit(solution)/shard_map/ppermute | solution.py:747
  726.6 44.1 %collective-permute-start.61 = (bf16[2,104,2400]{2,1,0:T(8,128)(2,1)}, bf16[2,104,2400]{2,1,0:T(8,128)(2,1)}, u32[]{:S(2)}, u32[]{:S(2)}) collective-permute-start(bf16[2,104,2400]{2,1,0:T(8,128)(2,1)} %dynamic-slice_bitcast_fusion.3), channel_id=1, source_target_pairs={{0,8},{4,12},{8,0},{12,4},{16,24},{20,28},{24,16},{28,20},{1,9},{5... | collective-permute-start | bytes 2995208 | tf_op jit(solution)/shard_map/ppermute | solution.py:820
  737.3 40.9 %collective-permute-start.65 = (bf16[2,104,2752]{2,1,0:T(8,128)(2,1)}, bf16[2,104,2752]{2,1,0:T(8,128)(2,1)}, u32[]{:S(2)}, u32[]{:S(2)}) collective-permute-start(bf16[2,104,2752]{2,1,0:T(8,128)(2,1)} %dynamic-slice_bitcast_fusion.2), channel_id=1, source_target_pairs={{0,8},{4,12},{8,0},{12,4},{16,24},{20,28},{24,16},{28,20},{1,9},{5... | collective-permute-start | bytes 3434504 | tf_op jit(solution)/shard_map/ppermute | solution.py:820
  754.7 164.7 %collective-permute-start.56 = (bf16[2,2,144,800]{3,2,1,0:T(8,128)(2,1)}, bf16[2,2,144,800]{3,2,1,0:T(8,128)(2,1)}, u32[]{:S(2)}, u32[]{:S(2)}) collective-permute-start(bf16[2,2,144,800]{3,2,1,0:T(8,128)(2,1)} %convolution_convert_fusion.3), channel_id=1, source_target_pairs={{0,4},{4,0},{8,12},{12,8},{16,20},{20,16},{24,28},{28,24},{1,5},{5... | collective-permute-start | bytes 2764808 | tf_op jit(solution)/shard_map/ppermute | solution.py:820
  770.7 98.5 %collective-permute-start.53 = (bf16[2,2,200,800]{3,2,1,0:T(8,128)(2,1)}, bf16[2,2,200,800]{3,2,1,0:T(8,128)(2,1)}, u32[]{:S(2)}, u32[]{:S(2)}) collective-permute-start(bf16[2,2,200,800]{3,2,1,0:T(8,128)(2,1)} %copy-done.163), channel_id=1, source_target_pairs={{0,4},{4,0},{8,12},{12,8},{16,20},{20,16},{24,28},{28,24},{1,5},{5... | collective-permute-start | bytes 3840008 | tf_op jit(solution)/shard_map/ppermute | solution.py:820
  778.2 83.9 %collective-permute-start.52 = (bf16[2,2,200,800]{3,2,1,0:T(8,128)(2,1)}, bf16[2,2,200,800]{3,2,1,0:T(8,128)(2,1)}, u32[]{:S(2)}, u32[]{:S(2)}) collective-permute-start(bf16[2,2,200,800]{3,2,1,0:T(8,128)(2,1)} %copy-done.164), channel_id=1, source_target_pairs={{0,4},{4,0},{8,12},{12,8},{16,20},{20,16},{24,28},{28,24},{1,5},{5... | collective-permute-start | bytes 3840008 | tf_op jit(solution)/shard_map/ppermute | solution.py:820
  787.3 21.1 %collective-permute-start.49 = (bf16[400,512]{1,0:T(8,128)(2,1)}, bf16[400,512]{1,0:T(8,128)(2,1)S(1)}, u32[]{:S(2)}, u32[]{:S(2)}) collective-permute-start(bf16[400,512]{1,0:T(8,128)(2,1)} %fusion.95), channel_id=1, source_target_pairs={{0,2},{2,0},{1,3},{3,1},{4,6},{6,4},{5,7},{7,5},{8,10},{10,8},{9,1... | collective-permute-start | bytes 1228808 | tf_op jit(solution)/shard_map/ppermute | solution.py:747
  808.4 38.5 %collective-permute-start.62 = (bf16[104,2400]{1,0:T(8,128)(2,1)}, bf16[104,2400]{1,0:T(8,128)(2,1)}, u32[]{:S(2)}, u32[]{:S(2)}) collective-permute-start(bf16[104,2400]{1,0:T(8,128)(2,1)} %dynamic-slice_bitcast_fusion.11), channel_id=1, source_target_pairs={{0,16},{4,20},{8,24},{12,28},{16,0},{20,4},{24,8},{28,12},{1,17},{... | collective-permute-start | bytes 1497608 | tf_op jit(solution)/shard_map/ppermute | solution.py:820
  813.5 36.3 %all-to-all-start.10 = ((f32[32,1,400]{2,1,0:T(1,128)}), f32[32,1,400]{2,1,0:T(1,128)S(1)}, u32[]{:S(2)}, u32[]{:S(2)}) async-start(f32[32,1,400]{2,1,0:T(1,128)} %broadcast_in_dim.506), calls=%async_computation.10 | async-start | bytes 131072 | tf_op jit(solution)/shard_map/all_to_all | solution.py:859
  819.3 40.6 %collective-permute-start.66 = (bf16[104,2752]{1,0:T(8,128)(2,1)}, bf16[104,2752]{1,0:T(8,128)(2,1)}, u32[]{:S(2)}, u32[]{:S(2)}) collective-permute-start(bf16[104,2752]{1,0:T(8,128)(2,1)} %get-tuple-element.135), channel_id=1, source_target_pairs={{0,16},{4,20},{8,24},{12,28},{16,0},{20,4},{24,8},{28,12},{1,17},{... | collective-permute-start | bytes 1717256 | tf_op jit(solution)/shard_map/ppermute | solution.py:820
  873.8 38.5 %collective-permute-start.55 = (bf16[2,200,800]{2,1,0:T(8,128)(2,1)}, bf16[2,200,800]{2,1,0:T(8,128)(2,1)}, u32[]{:S(2)}, u32[]{:S(2)}) collective-permute-start(bf16[2,200,800]{2,1,0:T(8,128)(2,1)} %dynamic-slice_bitcast_fusion.4), channel_id=1, source_target_pairs={{0,8},{4,12},{8,0},{12,4},{16,24},{20,28},{24,16},{28,20},{1,9},{5... | collective-permute-start | bytes 1920008 | tf_op jit(solution)/shard_map/ppermute | solution.py:820
  873.8 37.1 %collective-permute-start.54 = (bf16[2,200,800]{2,1,0:T(8,128)(2,1)}, bf16[2,200,800]{2,1,0:T(8,128)(2,1)S(1)}, u32[]{:S(2)}, u32[]{:S(2)}) collective-permute-start(bf16[2,200,800]{2,1,0:T(8,128)(2,1)} %dynamic-slice_bitcast_fusion.5), channel_id=1, source_target_pairs={{0,8},{4,12},{8,0},{12,4},{16,24},{20,28},{24,16},{28,20},{1,9},{5... | collective-permute-start | bytes 1920008 | tf_op jit(solution)/shard_map/ppermute | solution.py:820
  880.2 43.9 %all-to-all-start.11 = ((f32[32,1,2660]{2,1,0:T(1,128)}), f32[32,1,2660]{2,1,0:T(1,128)S(1)}, u32[]{:S(2)}, u32[]{:S(2)}) async-start(f32[32,1,2660]{2,1,0:T(1,128)} %all_to_all.96), calls=%async_computation.11 | async-start | bytes 688128 | tf_op jit(solution)/shard_map/all_to_all | solution.py:866
  915.7 25.4 %collective-permute-start.60 = (bf16[200,800]{1,0:T(8,128)(2,1)}, bf16[200,800]{1,0:T(8,128)(2,1)}, u32[]{:S(2)}, u32[]{:S(2)}) collective-permute-start(bf16[200,800]{1,0:T(8,128)(2,1)} %dynamic-slice_bitcast_fusion.12), channel_id=1, source_target_pairs={{0,16},{4,20},{8,24},{12,28},{16,0},{20,4},{24,8},{28,12},{1,17},{... | collective-permute-start | bytes 960008 | tf_op jit(solution)/shard_map/ppermute | solution.py:820
  918.0 34.5 %collective-permute-start.59 = (bf16[200,800]{1,0:T(8,128)(2,1)}, bf16[200,800]{1,0:T(8,128)(2,1)}, u32[]{:S(2)}, u32[]{:S(2)}) collective-permute-start(bf16[200,800]{1,0:T(8,128)(2,1)} %dynamic-slice_bitcast_fusion.13), channel_id=1, source_target_pairs={{0,16},{4,20},{8,24},{12,28},{16,0},{20,4},{24,8},{28,12},{1,17},{... | collective-permute-start | bytes 960008 | tf_op jit(solution)/shard_map/ppermute | solution.py:820
  922.8 30.7 %collective-permute-start.57 = (bf16[2,144,800]{2,1,0:T(8,128)(2,1)}, bf16[2,144,800]{2,1,0:T(8,128)(2,1)}, u32[]{:S(2)}, u32[]{:S(2)}) collective-permute-start(bf16[2,144,800]{2,1,0:T(8,128)(2,1)} %dynamic-slice_bitcast_fusion.10), channel_id=1, source_target_pairs={{0,8},{4,12},{8,0},{12,4},{16,24},{20,28},{24,16},{28,20},{1,9},{5... | collective-permute-start | bytes 1382408 | tf_op jit(solution)/shard_map/ppermute | solution.py:820
  925.2 32.4 %all-to-all-start.12 = ((f32[32,1,2660]{2,1,0:T(1,128)}), f32[32,1,2660]{2,1,0:T(1,128)}, u32[]{:S(2)}, u32[]{:S(2)}) async-start(f32[32,1,2660]{2,1,0:T(1,128)} %broadcast_in_dim.508), calls=%async_computation.12 | async-start | bytes 688128 | tf_op jit(solution)/shard_map/all_to_all | solution.py:859
  (205 other events, 1563.2 us)
